TPU v7x, 256 devices: a whole 4x4x8 slice. The times are simulated.
256 devices in a mesh: seq: 128 (over y, x, z), chan: 2 (over core).
Axes of the slice: x: 4, y: 4, z: 8, core: 2. Of those that a mesh axis runs over, the one named last changes fastest.
Arguments:
- query_proj: float32 [4096, 32768], P('chan', 'seq'), may hold values from -6 to 6
- key_proj: float32 [4096, 32768], P('chan', 'seq'), may hold values from -6 to 6
- value_proj: float32 [4096, 32768], P('chan', 'seq'), may hold values from -6 to 6
- second_query: float32 [4096, 32768], P('chan', 'seq'), may hold values from -6 to 6
- second_key: float32 [4096, 32768], P('chan', 'seq'), may hold values from -6 to 6
- short_filter: float32 [3, 4096, 3], P(None, 'chan'), may hold values from -3 to 3
- second_short: float32 [3, 4096, 3], P(None, 'chan'), may hold values from -3 to 3
- medium_filter: float32 [4096, 128], P('chan'), may hold values from -0.5 to 0.5
- decay_rate: float32 [4096, 8], P('chan'), may hold values from 6.1035156e-06 to 0.0333333333, as said below
- residue: float32 [4096, 8], P('chan'), may hold values from -1.5 to 1.5
- skip_gain: float32 [4096], P('chan'), may hold values from -1 to 1
- norm_gain: float32 [4096], P('chan'), may hold values from 0.1 to 1.9
Outputs:
- normalized: float32 [4096, 32768], P('chan', 'seq')
Inputs may be any that keep to these rules, and one draw needn't show every extreme that they name: `decay_rate`: positive decay rates, one for each channel and mode.
All inputs are finite; a program needn't handle non-finite values.
Results may differ from a plain program's by a relative error of at most 0.0003.
Values sent between devices are 32-bit elements; how exact they have to be, the bound alone decides.
No kernel may reach another device: no remote copies, remote signals or barrier semaphores. Data moves between devices by JAX's collectives and lax.ppermute only.
A program may use at most 128 MiB of HBM per device.

v0:
```python
import jax
import jax.numpy as jnp
import ml_dtypes
import numpy as np
from jax import lax
from jax.experimental import pallas as pl
from jax.experimental.pallas import tpu as pltpu
from jax.sharding import PartitionSpec as P

norm_eps = 1e-06

T = 256
TAPS = 128
MODES = 8
LANES = 128
SEG = 8
HEAD = 17
MAIN = 15
HEAD_ROWS = HEAD * SEG
MAIN_ROWS = MAIN * SEG
RIMS = 16
LIMIT = 48 * 1024 * 1024

F32 = jnp.float32
BF16 = jnp.bfloat16


def row_times():
    head = [HEAD * i + k for k in range(HEAD) for i in range(SEG)]
    main = [HEAD_ROWS + MAIN * i + k for k in range(MAIN) for i in range(SEG)]
    return np.array(head + main)


def packed_forward(slots):
    k = np.arange(128)[:, None]
    angle = 2.0 * np.pi * k * np.asarray(slots)[None, :] / 256.0
    imag = -np.sin(angle)
    imag[0] = np.cos(np.pi * np.asarray(slots))
    return np.concatenate([np.cos(angle), imag], 0)


def packed_inverse(slots):
    k = np.arange(128)[None, :]
    angle = 2.0 * np.pi * k * np.asarray(slots)[:, None] / 256.0
    real = 2.0 * np.cos(angle)
    real[:, 0] = 1.0
    imag = -2.0 * np.sin(angle)
    imag[:, 0] = np.cos(np.pi * np.asarray(slots))
    return np.concatenate([real, imag], 1) / 256.0


def three_pass(matrix):
    high = matrix.astype(ml_dtypes.bfloat16)
    low = (matrix - high.astype(np.float64)).astype(ml_dtypes.bfloat16)
    return np.concatenate([high, low, high], 1)


def tables():
    times = row_times()
    first = packed_forward(times + 128) * (times < 128)[None, :]
    second = packed_forward(times)
    forward = np.concatenate([first, second], 0)
    taps = packed_forward(np.arange(TAPS))
    real, imag = taps[:128], taps[128:].copy()
    cross = real.copy()
    cross[0] = imag[0]
    imag[0] = 0.0
    spectrum = np.concatenate([real, imag, cross], 0)
    inverse = np.concatenate(
        [
            packed_inverse(times + 128) * (times < 128)[:, None],
            packed_inverse(times) * (times >= 128)[:, None],
        ],
        1,
    )
    halo = packed_forward(np.arange(128))
    halo[:, 0] = 0.0
    head_times = np.concatenate([times[:HEAD_ROWS], np.full(8, 255)])
    halo_back = packed_inverse(head_times + 128) * (head_times < 128)[:, None]
    return [three_pass(m) for m in (forward, spectrum, inverse, halo, halo_back)]


def halves(x):
    high = x.astype(BF16)
    low = (x - high.astype(F32)).astype(BF16)
    return high, low


def matmul3(matrix, x):
    high, low = halves(x)
    stacked = jnp.concatenate([high, high, low], 0)
    return jnp.dot(matrix, stacked, preferred_element_type=F32)


def spectral_product(x, taps):
    real, imag = x[:128], x[128:]
    tap_real, tap_imag, tap_cross = taps[:128], taps[128:256], taps[256:]
    return jnp.concatenate(
        [real * tap_real - imag * tap_imag, real * tap_imag + imag * tap_cross], 0
    )


def sublane(shape):
    return lax.broadcasted_iota(jnp.int32, shape, 0)


def down(x, distance=1):
    return pltpu.roll(x, distance, axis=0)


def fir3(slabs, taps):
    return [
        taps[0] * slabs[k + 2] + taps[1] * slabs[k + 1] + taps[2] * slabs[k]
        for k in range(len(slabs) - 2)
    ]


def with_rims(head, main, rims=None):
    top = sublane(head[0].shape) == 0
    zero = jnp.zeros_like(head[0])
    before = (zero, zero) if rims is None else rims
    ends = [down(head[HEAD - 2]), down(head[HEAD - 1])]
    head_all = [jnp.where(top, before[k], ends[k]) for k in range(2)] + head
    if main is None:
        return head_all, None
    main_all = [jnp.where(top, ends[k], down(main[MAIN - 2 + k])) for k in range(2)] + main
    return head_all, main_all


def rows_of(ref, k, lanes):
    return ref[pl.ds(SEG * k, SEG), lanes]


def spread(row):
    return jnp.broadcast_to(row, (SEG, row.shape[1]))


def recurrence(inputs, decays, gains, skip):
    states = [gains[r] * inputs[0] for r in range(MODES)]
    outs = []
    for k, value in enumerate(inputs):
        if k:
            states = [decays[r] * states[r] + gains[r] * value for r in range(MODES)]
        total = skip * value
        for state in states:
            total = total + state
        outs.append(total)
    return outs, states


def prefix(state, rate, step):
    place = sublane(state.shape)
    total = state
    for distance in (1, 2, 4):
        moved = jnp.where(place >= distance, down(total, distance), 0.0)
        total = total + jnp.exp(-(step * distance) * rate) * moved
    return jnp.where(place >= 1, down(total), 0.0), total[SEG - 1 :]


def tail_kernel(key_ref, value_ref, short_ref, tail_ref, taps_ref):
    taps_ref[...] = jnp.zeros_like(taps_ref)
    taps_ref[0:3, :] = short_ref[1]
    taps_ref[3:6, :] = short_ref[2]
    columns = taps_ref[...].T
    lane = lax.broadcasted_iota(jnp.int32, (key_ref.shape[0], LANES), 1)

    def feature(ref, first):
        here = ref[:, LANES:]
        back_two = jnp.where(lane == LANES - 1, ref[:, :LANES], here)
        return (
            columns[:, first : first + 1] * here
            + columns[:, first + 1 : first + 2] * pltpu.roll(here, 1, axis=1)
            + columns[:, first + 2 : first + 3] * pltpu.roll(back_two, 2, axis=1)
        )

    tail_ref[...] = feature(key_ref, 0) * feature(value_ref, 3)


def local_kernel(
    key_ref,
    value_ref,
    query_ref,
    query2_ref,
    key2_ref,
    short_ref,
    second_ref,
    medium_ref,
    rate_ref,
    amplitude_ref,
    skip_ref,
    forward_ref,
    spectrum_ref,
    inverse_ref,
    taps_out,
    spectrum_out,
    medium_out,
    query_out,
    key2_out,
    query2_out,
    own_out,
    enter_out,
    leave_out,
    first_rows_out,
    rims_out,
    key_t,
    value_t,
    query_t,
    query2_t,
    key2_t,
    taps_t,
    gated_t,
    medium_t,
):
    width = key_ref.shape[0]
    chunks = [pl.ds(LANES * part, LANES) for part in range(width // LANES)]
    first_rows_out[...] = jnp.zeros_like(first_rows_out)
    rims_out[...] = jnp.zeros_like(rims_out)
    for part, lanes in enumerate(chunks):
        for place, (ref, turned) in enumerate(
            (
                (key_ref, key_t),
                (value_ref, value_t),
                (query_ref, query_t),
                (query2_ref, query2_t),
                (key2_ref, key2_t),
            )
        ):
            turned[part] = ref[lanes, :].T
            rims_out[2 * place : 2 * place + 2, lanes] = turned[part, T - 2 : T, :]
            if place < 2:
                first_rows_out[2 * place : 2 * place + 2, lanes] = turned[part, 0:2, :]
        taps_t[part, 0:TAPS, :] = medium_ref[lanes, :].T
        taps_t[part, TAPS:HEAD_ROWS, :] = jnp.zeros((HEAD_ROWS - TAPS, LANES), F32)
        for k in range(HEAD):
            taps_out[pl.ds(SEG * k, SEG), lanes] = taps_t[part, pl.ds(k, SEG, stride=HEAD), :]

    def slabs_of(ref, part):
        head = [ref[part, pl.ds(k, SEG, stride=HEAD), :] for k in range(HEAD)]
        main = [ref[part, pl.ds(HEAD_ROWS + k, SEG, stride=MAIN), :] for k in range(MAIN)]
        return head, main

    def feature(ref, part, taps_of, index, lanes):
        taps = [spread(taps_of[index, j : j + 1, lanes]) for j in range(3)]
        head, main = with_rims(*slabs_of(ref, part))
        return fir3(head, taps) + fir3(main, taps)

    top = sublane((SEG, LANES)) == 0
    for part, lanes in enumerate(chunks):
        keys = feature(key_t, part, short_ref, 1, lanes)
        values = feature(value_t, part, short_ref, 2, lanes)
        for k in range(HEAD + MAIN):
            gated = keys[k] * values[k]
            if k < 2:
                gated = jnp.where(top, 0.0, gated)
            gated_t[pl.ds(SEG * k, SEG), lanes] = gated
        for ref, taps_of, index, out in (
            (query_t, short_ref, 0, query_out),
            (query2_t, second_ref, 0, query2_out),
            (key2_t, second_ref, 1, key2_out),
        ):
            for k, slab in enumerate(feature(ref, part, taps_of, index, lanes)):
                out[pl.ds(SEG * k, SEG), lanes] = slab

    turned = [taps_t[part, 0:TAPS, :] for part in range(len(chunks))]
    spectrum = matmul3(spectrum_ref[...], jnp.concatenate(turned, 1))
    spectrum_out[...] = spectrum
    both = matmul3(forward_ref[...], gated_t[...])
    first = spectral_product(both[:T], spectrum)
    second = spectral_product(both[T:], spectrum)
    medium_t[...] = matmul3(inverse_ref[...], jnp.concatenate([first, second], 0))
    medium_out[...] = medium_t[0:HEAD_ROWS, :]

    for lanes in chunks:
        taps = [spread(second_ref[2, j : j + 1, lanes]) for j in range(3)]
        firsts = [
            rows_of(medium_t, k, lanes) * rows_of(query_out, k, lanes)
            for k in range(HEAD - 2, HEAD + MAIN)
        ]
        ends = [down(firsts[0]), down(firsts[1])]
        main = firsts[2:]
        main_all = [jnp.where(top, ends[k], down(main[MAIN - 2 + k])) for k in range(2)] + main
        rims_out[10:11, lanes] = main[MAIN - 2][SEG - 1 :]
        rims_out[11:12, lanes] = main[MAIN - 1][SEG - 1 :]
        values2 = fir3(main_all, taps)
        inputs = [
            rows_of(key2_out, HEAD + k, lanes) * values2[k] for k in range(MAIN)
        ]
        rates, gains = rate_ref[:, lanes], amplitude_ref[:, lanes]
        decays = jnp.exp(-rates)
        outs, ends = recurrence(
            inputs,
            [spread(decays[r : r + 1]) for r in range(MODES)],
            [spread(gains[r : r + 1]) for r in range(MODES)],
            spread(skip_ref[:, lanes]),
        )
        for k in range(MAIN):
            own_out[pl.ds(SEG * k, SEG), lanes] = outs[k]
        for r in range(MODES):
            enter, leave = prefix(ends[r], spread(rates[r : r + 1]), float(MAIN))
            enter_out[r, :, lanes] = enter
            leave_out[r : r + 1, lanes] = leave


def join_kernel(
    halo_ref,
    rims_ref,
    spectrum_ref,
    medium_ref,
    taps_ref,
    query_ref,
    key2_ref,
    first_rows_ref,
    enter_main_ref,
    leave_main_ref,
    short_ref,
    second_ref,
    rate_ref,
    amplitude_ref,
    skip_ref,
    forward_ref,
    inverse_ref,
    own_out,
    enter_out,
    enter_main_out,
    state_out,
    medium_t,
):
    width = halo_ref.shape[0]
    high, low = halves(halo_ref[...])
    stacked = jnp.concatenate([high, high, low], 1)
    halo = lax.dot_general(
        forward_ref[...], stacked, (((1,), (1,)), ((), ())), preferred_element_type=F32
    )
    product = spectral_product(halo, spectrum_ref[...])
    medium_t[...] = matmul3(inverse_ref[...], product)

    top = sublane((SEG, LANES)) == 0
    for part in range(width // LANES):
        lanes = pl.ds(LANES * part, LANES)

        def rim(k):
            return rims_ref[k : k + 1, lanes]

        def first(k):
            return first_rows_ref[k : k + 1, lanes]

        def taps_of(ref, index):
            return [ref[index, j : j + 1, lanes] for j in range(3)]

        def early(place, index):
            taps = taps_of(short_ref, index)
            zero, one = first(2 * place), first(2 * place + 1)
            older, last = rim(2 * place), rim(2 * place + 1)
            return (
                taps[0] * zero + taps[1] * last + taps[2] * older,
                taps[0] * one + taps[1] * zero + taps[2] * last,
            )

        def mended(ref, place, taps):
            slabs = [rows_of(ref, k, lanes) for k in range(HEAD)]
            older, last = rim(2 * place), rim(2 * place + 1)
            slabs[0] = slabs[0] + jnp.where(top, spread(taps[1] * last + taps[2] * older), 0.0)
            slabs[1] = slabs[1] + jnp.where(top, spread(taps[2] * last), 0.0)
            return slabs

        keys, values = early(0, 1), early(1, 2)
        gated = [spread(keys[k] * values[k]) for k in range(2)]
        taps = [rows_of(taps_ref, k, lanes) for k in range(HEAD)]
        shifted = [jnp.where(top, 0.0, down(taps[HEAD - 1]))] + taps
        query = mended(query_ref, 2, taps_of(short_ref, 0))
        key2 = mended(key2_ref, 4, taps_of(second_ref, 1))
        firsts = [
            query[k]
            * (
                rows_of(medium_ref, k, lanes)
                + rows_of(medium_t, k, lanes)
                + taps[k] * gated[0]
                + shifted[k] * gated[1]
            )
            for k in range(HEAD)
        ]
        firsts_all, _ = with_rims(firsts, None, (spread(rim(10)), spread(rim(11))))
        values2 = fir3(firsts_all, [spread(t) for t in taps_of(second_ref, 2)])
        inputs = [key2[k] * values2[k] for k in range(HEAD)]
        rates, gains = rate_ref[:, lanes], amplitude_ref[:, lanes]
        decays = jnp.exp(-rates)
        outs, ends = recurrence(
            inputs,
            [spread(decays[r : r + 1]) for r in range(MODES)],
            [spread(gains[r : r + 1]) for r in range(MODES)],
            spread(skip_ref[:, lanes]),
        )
        for k in range(HEAD):
            own_out[pl.ds(SEG * k, SEG), lanes] = outs[k]
        segment = sublane((SEG, LANES)).astype(F32)
        for r in range(MODES):
            rate = spread(rates[r : r + 1])
            enter, leave = prefix(ends[r], rate, float(HEAD))
            enter_out[r, :, lanes] = enter
            enter_main_out[r, :, lanes] = enter_main_ref[r, :, lanes] + jnp.exp(
                -(rate * (segment * float(MAIN)))
            ) * spread(leave)
            state_out[part, r : r + 1, :] = leave_main_ref[r : r + 1, lanes] + leave * jnp.exp(
                -float(MAIN_ROWS) * rates[r : r + 1]
            )


def scan_kernel(state_ref, rate_ref, out_ref):
    blocks = state_ref.shape[0]
    place = sublane(state_ref.shape)
    rate = rate_ref[...]
    total = state_ref[...]
    distance = 1
    while distance < blocks:
        moved = jnp.where(place >= distance, down(total, distance), 0.0)
        total = total + jnp.exp(-(float(T) * distance) * rate) * moved
        distance *= 2
    out_ref[...] = jnp.where(place >= 1, down(total), 0.0)


def finish_kernel(
    state_ref,
    own_head_ref,
    own_main_ref,
    enter_head_ref,
    enter_main_ref,
    query2_ref,
    rims_ref,
    second_ref,
    rate_ref,
    gain_ref,
    mixed_out,
    squares_out,
    squares_t,
):
    step = pl.program_id(0)
    width = query2_ref.shape[1]

    @pl.when(step == 0)
    def _():
        squares_t[...] = jnp.zeros_like(squares_t)

    top = sublane((SEG, LANES)) == 0
    segment = sublane((SEG, LANES)).astype(F32)
    for part in range(width // LANES):
        lanes = pl.ds(LANES * part, LANES)
        rates = rate_ref[:, lanes]
        decays = jnp.exp(-rates)
        taps = [second_ref[0, j : j + 1, lanes] for j in range(3)]
        older, last = rims_ref[6:7, lanes], rims_ref[7:8, lanes]
        mends = [spread(taps[1] * last + taps[2] * older), spread(taps[2] * last)]
        gain = spread(gain_ref[:, lanes])
        incoming = [spread(state_ref[part, r : r + 1, :]) for r in range(MODES)]
        rate = [spread(rates[r : r + 1]) for r in range(MODES)]
        decay = [spread(decays[r : r + 1]) for r in range(MODES)]

        def half(count, length, start, enter_ref, own_ref, first_row):
            carry = [
                enter_ref[r, :, lanes]
                + jnp.exp(-(rate[r] * (segment * float(length) + start))) * incoming[r]
                for r in range(MODES)
            ]
            for k in range(count):
                carry = [decay[r] * carry[r] for r in range(MODES)]
                total = rows_of(own_ref, k, lanes)
                for value in carry:
                    total = total + value
                query = query2_ref[pl.ds(first_row + SEG * k, SEG), lanes]
                if first_row == 0 and k < 2:
                    query = query + jnp.where(top, mends[k], 0.0)
                mixed = query * total
                rows = pl.ds(first_row + SEG * k, SEG)
                squares_t[rows, :] = squares_t[rows, :] + mixed * mixed
                mixed_out[part, pl.ds(first_row + k, SEG, stride=length), :] = mixed * gain

        half(HEAD, HEAD, 0.0, enter_head_ref, own_head_ref, 0)
        half(MAIN, MAIN, float(HEAD_ROWS), enter_main_ref, own_main_ref, HEAD_ROWS)

    @pl.when(step == pl.num_programs(0) - 1)
    def _():
        sums = jnp.sum(squares_t[...], axis=1, keepdims=True)
        squares_t[...] = jnp.broadcast_to(sums, squares_t.shape)
        head = [squares_t[pl.ds(i, HEAD, stride=SEG), :] for i in range(SEG)]
        main = [squares_t[pl.ds(HEAD_ROWS + i, MAIN, stride=SEG), :] for i in range(SEG)]
        ordered = jnp.concatenate(head + main, 0)
        squares_out[...] = ordered.T[0:8, :]


def scale_kernel(mixed_ref, scale_ref, out_ref):
    for part in range(mixed_ref.shape[0]):
        out_ref[pl.ds(LANES * part, LANES), :] = mixed_ref[part].T * scale_ref[...]


def from_behind(block):
    count = lax.axis_size("seq")
    return lax.ppermute(block, "seq", [(i, i + 1) for i in range(count - 1)])


def call(kernel, grid, in_specs, out_specs, out_shape, scratch, flops, size, name):
    return pl.pallas_call(
        kernel,
        grid=grid,
        in_specs=in_specs,
        out_specs=out_specs,
        out_shape=out_shape,
        scratch_shapes=scratch,
        compiler_params=pltpu.CompilerParams(vmem_limit_bytes=LIMIT),
        cost_estimate=pl.CostEstimate(flops=flops, bytes_accessed=size, transcendentals=0),
        name=name,
    )


def local(
    query_proj,
    key_proj,
    value_proj,
    second_query,
    second_key,
    short_filter,
    second_short,
    medium_filter,
    decay_rate,
    residue,
    skip_gain,
    norm_gain,
):
    channels = query_proj.shape[0]
    count = lax.axis_size("seq")
    tiles = channels // LANES
    width = min(256, channels)
    steps = channels // width
    per_step = width // LANES
    short_t = jnp.transpose(short_filter, (0, 2, 1))
    second_t = jnp.transpose(second_short, (0, 2, 1))
    rate_t = decay_rate.T
    amplitude = residue.T * jnp.sqrt(-jnp.expm1(-2.0 * rate_t))
    skip = skip_gain[None, :]
    gain = norm_gain[None, :]
    forward, spectrum, inverse, halo_forward, halo_inverse = tables()

    def struct(*shape):
        return jax.ShapeDtypeStruct(shape, F32)

    def by_row(columns):
        return pl.BlockSpec((width, columns), lambda i: (i, 0))

    def by_lane(rows):
        return pl.BlockSpec((rows, width), lambda i: (0, i))

    def by_lane3(planes, rows):
        return pl.BlockSpec((planes, rows, width), lambda i: (0, 0, i))

    def whole(array):
        return pl.BlockSpec(array.shape, lambda i: (0,) * array.ndim)

    state_spec = pl.BlockSpec((per_step, MODES, LANES), lambda i: (i, 0, 0))
    mixed_spec = pl.BlockSpec((per_step, T, LANES), lambda i: (i, 0, 0))

    tail = call(
        tail_kernel,
        (steps,),
        [by_row(T), by_row(T), by_lane3(3, 3)],
        by_row(LANES),
        struct(channels, LANES),
        [pltpu.VMEM((8, width), F32)],
        channels * T * 8,
        channels * T * 10,
        "tail",
    )(key_proj, value_proj, short_t)
    halo = from_behind(tail)

    (
        taps,
        tap_spectrum,
        medium,
        query,
        key2,
        query2,
        own_main,
        enter_main,
        leave_main,
        first_rows,
        rims,
    ) = call(
        local_kernel,
        (steps,),
        [by_row(T)] * 5
        + [by_lane3(3, 3), by_lane3(3, 3), by_row(TAPS), by_lane(MODES), by_lane(MODES), by_lane(1)]
        + [whole(forward), whole(spectrum), whole(inverse)],
        [
            by_lane(HEAD_ROWS),
            by_lane(384),
            by_lane(HEAD_ROWS),
            by_lane(T),
            by_lane(T),
            by_lane(T),
            by_lane(MAIN_ROWS),
            by_lane3(MODES, SEG),
            by_lane(MODES),
            by_lane(8),
            by_lane(RIMS),
        ],
        [
            struct(HEAD_ROWS, channels),
            struct(384, channels),
            struct(HEAD_ROWS, channels),
            struct(T, channels),
            struct(T, channels),
            struct(T, channels),
            struct(MAIN_ROWS, channels),
            struct(MODES, SEG, channels),
            struct(MODES, channels),
            struct(8, channels),
            struct(RIMS, channels),
        ],
        [pltpu.VMEM((per_step, T, LANES), F32)] * 5
        + [pltpu.VMEM((per_step, HEAD_ROWS, LANES), F32)]
        + [pltpu.VMEM((T, width), F32)] * 2,
        channels * T * 8000,
        channels * T * 60,
        "local",
    )(
        key_proj,
        value_proj,
        query_proj,
        second_query,
        second_key,
        short_t,
        second_t,
        medium_filter,
        rate_t,
        amplitude,
        skip,
        forward,
        spectrum,
        inverse,
    )
    border = from_behind(rims)

    own_head, enter_head, enter_main, state = call(
        join_kernel,
        (steps,),
        [
            by_row(LANES),
            by_lane(RIMS),
            by_lane(384),
            by_lane(HEAD_ROWS),
            by_lane(HEAD_ROWS),
            by_lane(HEAD_ROWS),
            by_lane(HEAD_ROWS),
            by_lane(8),
            by_lane3(MODES, SEG),
            by_lane(MODES),
            by_lane3(3, 3),
            by_lane3(3, 3),
            by_lane(MODES),
            by_lane(MODES),
            by_lane(1),
            whole(halo_forward),
            whole(halo_inverse),
        ],
        [by_lane(HEAD_ROWS), by_lane3(MODES, SEG), by_lane3(MODES, SEG), state_spec],
        [
            struct(HEAD_ROWS, channels),
            struct(MODES, SEG, channels),
            struct(MODES, SEG, channels),
            struct(tiles, MODES, LANES),
        ],
        [pltpu.VMEM((HEAD_ROWS + 8, width), F32)],
        channels * T * 2000,
        channels * T * 20,
        "join",
    )(
        halo,
        border,
        tap_spectrum,
        medium,
        taps,
        query,
        key2,
        first_rows,
        enter_main,
        leave_main,
        short_t,
        second_t,
        rate_t,
        amplitude,
        skip,
        halo_forward,
        halo_inverse,
    )

    place = lax.axis_index("seq")
    own_rate = lax.dynamic_slice(
        rate_t, (place % MODES, (place // MODES) * LANES), (1, LANES)
    )
    gathered = lax.all_to_all(
        state.reshape(count, 1, LANES), "seq", split_axis=0, concat_axis=0, tiled=True
    )
    scanned = call(
        scan_kernel,
        (1,),
        [pl.BlockSpec((count, LANES), lambda i: (0, 0)), pl.BlockSpec((1, LANES), lambda i: (0, 0))],
        pl.BlockSpec((count, LANES), lambda i: (0, 0)),
        struct(count, LANES),
        [],
        count * LANES * 30,
        count * LANES * 8,
        "scan",
    )(gathered.reshape(count, LANES), own_rate)
    incoming = lax.all_to_all(
        scanned.reshape(count, 1, LANES), "seq", split_axis=0, concat_axis=0, tiled=True
    ).reshape(tiles, MODES, LANES)

    mixed, squares = call(
        finish_kernel,
        (steps,),
        [
            state_spec,
            by_lane(HEAD_ROWS),
            by_lane(MAIN_ROWS),
            by_lane3(MODES, SEG),
            by_lane3(MODES, SEG),
            by_lane(T),
            by_lane(RIMS),
            by_lane3(3, 3),
            by_lane(MODES),
            by_lane(1),
        ],
        [mixed_spec, pl.BlockSpec((8, T), lambda i: (0, 0))],
        [struct(tiles, T, LANES), struct(8, T)],
        [pltpu.VMEM((T, LANES), F32)],
        channels * T * 40,
        channels * T * 16,
        "finish",
    )(
        incoming,
        own_head,
        own_main,
        enter_head,
        enter_main,
        query2,
        border,
        second_t,
        rate_t,
        gain,
    )
    total = lax.psum(squares[0], "chan")
    scale = lax.rsqrt(total / (channels * lax.axis_size("chan")) + norm_eps)
    return call(
        scale_kernel,
        (steps,),
        [mixed_spec, pl.BlockSpec((1, T), lambda i: (0, 0))],
        by_row(T),
        struct(channels, T),
        [],
        channels * T,
        channels * T * 8,
        "scale",
    )(mixed, scale[None, :])


def solution(mesh):
    return jax.shard_map(
        local,
        mesh=mesh,
        in_specs=(
            P("chan", "seq"),
            P("chan", "seq"),
            P("chan", "seq"),
            P("chan", "seq"),
            P("chan", "seq"),
            P(None, "chan", None),
            P(None, "chan", None),
            P("chan", None),
            P("chan", None),
            P("chan", None),
            P("chan"),
            P("chan"),
        ),
        out_specs=P("chan", "seq"),
        check_vma=False,
    )
```

profile of v0, /device:TPU:1, one launch (start us, length us, event | category | flops | bytes accessed | tf_op | source)
XLA Modules:
  0.0 113.0 jit_solution(13469003481864954477)
XLA Ops:
  0.0 0.0 copy-start
  0.0 1.6 %copy-done = f32[2048,256]{1,0:T(8,128)S(1)} copy-done((f32[2048,256]{1,0:T(8,128)S(1)}, f32[2048,256]{1,0:T(8,128)}, u32[]{:S(2)}) %copy-start) | copy-done | bytes 2097176
  1.6 0.0 copy-start.1
  1.6 1.6 %copy-done.1 = f32[2048,256]{1,0:T(8,128)S(1)} copy-done((f32[2048,256]{1,0:T(8,128)S(1)}, f32[2048,256]{1,0:T(8,128)}, u32[]{:S(2)}) %copy-start.1) | copy-done | bytes 2097176
  3.2 0.0 copy-start.12
  3.2 0.9 copy-done.12
  4.1 0.0 copy-start.6
  4.1 0.0 copy-start.22
  4.1 0.0 copy-start.11
  4.1 0.0 copy-start.16
  4.1 0.0 copy-start.18
  4.1 0.0 copy-start.19
  4.1 0.0 copy-start.20
  4.1 0.0 copy-start.21
  4.1 4.9 %tail.1 = f32[2048,128]{1,0:T(8,128)S(1)} custom-call(f32[2048,256]{1,0:T(8,128)S(1)} %copy-done, f32[2048,256]{1,0:T(8,128)S(1)} %copy-done.1, f32[3,3,2048]{2,1,0:T(4,128)S(1)} %bitcast.26), custom_call_target="tpu_custom_call" | custom-call | flops 4194304 | bytes 5242880 | tf_op jit(solution)/shard_map/tail/pallas_call | solution.py:559
  9.0 4.4 %collective-permute-start = (f32[2048,128]{1,0:T(8,128)S(1)}, f32[2048,128]{1,0:T(8,128)S(1)}, u32[]{:S(2)}, u32[]{:S(2)}) collective-permute-start(f32[2048,128]{1,0:T(8,128)S(1)} %tail.1), channel_id=1, source_target_pairs={{0,2},{2,4},{4,6},{6,8},{8,10},{10,12},{12,14},{14,16},{16,18},{18... | collective-permute-start | bytes 3145736 | tf_op jit(solution)/shard_map/ppermute | solution.py:496
  13.4 0.0 copy-done.6
  13.5 0.0 copy-done.22
  13.5 0.0 copy-done.11
  13.5 0.0 copy-done.16
  13.5 0.0 copy-done.18
  13.6 0.0 copy-done.19
  13.6 0.0 copy-done.20
  13.6 0.0 copy-done.21
  13.6 0.0 copy-start.13
  13.6 0.0 copy-start.14
  13.6 0.0 copy-start.15
  13.6 15.8 %local.1 = (f32[136,2048]{1,0:T(8,128)S(1)}, f32[384,2048]{1,0:T(8,128)}, f32[136,2048]{1,0:T(8,128)}, f32[256,2048]{1,0:T(8,128)}, f32[256,2048]{1,0:T(8,128)},...) custom-call(f32[2048,256]{1,0:T(8,128)} %key_ref.3, ...), custom_call_target="tpu_custom_call" | custom-call | flops 4194304000 | bytes 31457280 | tf_op jit(solution)/shard_map/local/pallas_call | solution.py:584
  29.4 0.0 copy-start.2
  29.4 1.1 copy-done.2
  30.5 0.0 copy-start.4
  30.5 1.0 copy-done.4
  31.4 3.5 %collective-permute-start.1 = (f32[16,2048]{1,0:T(8,128)S(1)}, f32[16,2048]{1,0:T(8,128)S(1)}, u32[]{:S(2)}, u32[]{:S(2)}) collective-permute-start(f32[16,2048]{1,0:T(8,128)S(1)} %get-tuple-element.22), channel_id=1, source_target_pairs={{0,2},{2,4},{4,6},{6,8},{8,10},{10,12},{12,14},{14,16},{16,18},{18... | collective-permute-start | bytes 393224 | tf_op jit(solution)/shard_map/ppermute | solution.py:496
  34.9 3.4 %collective-permute-done.1.rims_ref = f32[16,2048]{1,0:T(8,128)S(1)} collective-permute-done((f32[16,2048]{1,0:T(8,128)S(1)}, f32[16,2048]{1,0:T(8,128)S(1)}, u32[]{:S(2)}, u32[]{:S(2)}) %collective-permute-start.1) | collective-permute-done | bytes 131104 | tf_op jit(solution)/shard_map/ppermute | solution.py:496
  38.3 0.0 collective-permute-done.halo_ref
  38.3 0.0 copy-done.13
  38.3 0.0 copy-done.14
  38.3 0.0 copy-done.15
  38.3 0.0 copy-start.3
  38.3 1.2 %copy-done.3 = f32[136,2048]{1,0:T(8,128)S(1)} copy-done((f32[136,2048]{1,0:T(8,128)S(1)}, f32[136,2048]{1,0:T(8,128)}, u32[]{:S(2)}) %copy-start.3) | copy-done | bytes 1114136
  39.5 0.0 copy-start.17
  39.5 9.6 %join.1 = (f32[136,2048]{1,0:T(8,128)S(1)}, f32[8,8,2048]{2,1,0:T(8,128)S(1)}, f32[8,8,2048]{2,1,0:T(8,128)S(1)}, f32[16,8,128]{2,1,0:T(8,128)}) custom-call(f32[2048,128]{1,0:T(8,128)S(1)} %collective-permute-done.halo_ref, f32[16,2048]{1,0:T(8,128)S(1)} %collective-permute-done.1.rims_ref, f32[384,2048]{1,0:T(8,128)} %get-tuple-element.23.spectrum_ref, ...), custom_call_target="tpu_custom_call" | custom-call | flops 1048576000 | bytes 10485760 | tf_op jit(solution)/shard_map/join/pallas_call | solution.py:640
  49.2 0.0 copy-start.7
  49.2 0.8 copy-done.7
  50.0 0.0 copy-start.9
  50.0 0.8 copy-done.9
  50.8 17.0 %all-to-all-start = ((f32[128,1,128]{2,1,0:T(1,128)}), f32[128,1,128]{2,1,0:T(1,128)S(1)}, u32[]{:S(2)}, u32[]{:S(2)}) async-start(f32[128,1,128]{2,1,0:T(1,128)} %bitcast.6), calls=%async_computation | async-start | bytes 131072 | tf_op jit(solution)/shard_map/all_to_all | solution.py:697
  67.8 0.1 dynamic-slice_bitcast_fusion.rate_ref
  67.9 10.4 %all-to-all-done = f32[128,1,128]{2,1,0:T(1,128)S(1)} async-done(((f32[128,1,128]{2,1,0:T(1,128)}), f32[128,1,128]{2,1,0:T(1,128)S(1)}, u32[]{:S(2)}, u32[]{:S(2)}) %all-to-all-start) | async-done | bytes 65568 | tf_op jit(solution)/shard_map/all_to_all | solution.py:697
  78.4 0.1 scan.1
  78.4 16.1 %all_to_all.10 = f32[128,1,128]{2,1,0:T(1,128)S(1)} all-to-all(f32[128,1,128]{2,1,0:T(1,128)S(1)} %bitcast.31), channel_id=1, replica_groups=mesh['seq'=128,'chan'=2] {'seq'}, dimensions={0} | all-to-all | bytes 131072 | tf_op jit(solution)/shard_map/all_to_all | solution.py:711
  94.5 0.0 copy-done.17
  94.5 0.0 copy-start.5
  94.5 1.2 %copy-done.5 = f32[120,2048]{1,0:T(8,128)S(1)} copy-done((f32[120,2048]{1,0:T(8,128)S(1)}, f32[120,2048]{1,0:T(8,128)}, u32[]{:S(2)}) %copy-start.5) | copy-done | bytes 983064
  95.7 0.0 copy-start.8
  95.7 1.0 copy-done.8
  96.8 0.0 copy-start.10
  96.8 1.0 copy-done.10
  97.8 5.4 %finish.1 = (f32[16,256,128]{2,1,0:T(8,128)S(1)}, f32[8,256]{1,0:T(8,128)S(1)}) custom-call(f32[16,8,128]{2,1,0:T(8,128)S(1)} %bitcast.29, f32[136,2048]{1,0:T(8,128)S(1)} %get-tuple-element.32.own_head_ref, f32[120,2048]{1,0:T(8,128)S(1)} %copy-done.5, f32[8,8,2048]{2,1,0:T(8,128)S(1)} %copy-done.8, f32[8,8,2048]{2,1,0:T(8,128)S(1)} %copy-done.10, ...), custom_call_target="tpu_custom_call" | custom-call | flops 20971520 | bytes 8388608 | tf_op jit(solution)/shard_map/finish/pallas_call | solution.py:715
  103.2 6.3 %psum.7 = f32[256]{0:T(256)S(1)} all-reduce(f32[256]{0:T(256)S(1)} %bitcast.36), channel_id=1, replica_groups=mesh['seq'=128,'chan'=2] {'chan'}, use_global_device_ids=true, to_apply=%region_0.1 | all-reduce | flops 256 | bytes 2048 | tf_op jit(solution)/shard_map/psum | solution.py:748
  109.5 3.5 %scale.1 = f32[2048,256]{1,0:T(8,128)} custom-call(f32[16,256,128]{2,1,0:T(8,128)S(1)} %get-tuple-element.37.mixed_ref, f32[1,256]{1,0:T(1,128)S(1)} %bitcast.35), custom_call_target="tpu_custom_call" | custom-call | flops 524288 | bytes 4194304 | tf_op jit(solution)/shard_map/scale/pallas_call | solution.py:750
  (3 shorter events, 0.1 us)
Async XLA Ops:
  0.0 1.6 %copy-start = (f32[2048,256]{1,0:T(8,128)S(1)}, f32[2048,256]{1,0:T(8,128)}, u32[]{:S(2)}) copy-start(f32[2048,256]{1,0:T(8,128)} %key_ref.3) | copy-start | bytes 6291460
  1.6 1.6 %copy-start.1 = (f32[2048,256]{1,0:T(8,128)S(1)}, f32[2048,256]{1,0:T(8,128)}, u32[]{:S(2)}) copy-start(f32[2048,256]{1,0:T(8,128)} %value_ref.3) | copy-start | bytes 6291460
  3.2 0.9 copy-start.12
  4.1 9.4 %copy-start.6 = (f32[2048,8]{0,1:T(8,128)S(1)}, f32[2048,8]{0,1:T(8,128)}, u32[]{:S(2)}) copy-start(f32[2048,8]{0,1:T(8,128)} %param.25) | copy-start | bytes 196612
  4.1 9.4 %copy-start.22 = (f32[2048,8]{0,1:T(8,128)S(1)}, f32[2048,8]{0,1:T(8,128)}, u32[]{:S(2)}) copy-start(f32[2048,8]{0,1:T(8,128)} %param.26) | copy-start | bytes 196612
  4.1 9.4 %copy-start.11 = (f32[3,2048,3]{1,2,0:T(4,128)S(1)}, f32[3,2048,3]{1,2,0:T(4,128)}, u32[]{:S(2)}) copy-start(f32[3,2048,3]{1,2,0:T(4,128)} %param.23) | copy-start | bytes 221188
  4.1 9.5 %copy-start.16 = (f32[2048]{0:T(1024)S(1)}, f32[2048]{0:T(1024)}, u32[]{:S(2)}) copy-start(f32[2048]{0:T(1024)} %param.27) | copy-start | bytes 24580
  4.1 9.5 %copy-start.18 = (f32[2048,128]{1,0:T(8,128)S(1)}, f32[2048,128]{1,0:T(8,128)}, u32[]{:S(2)}) copy-start(f32[2048,128]{1,0:T(8,128)} %medium_ref.1) | copy-start | bytes 3145732
  4.1 9.5 %copy-start.19 = (bf16[512,768]{1,0:T(8,128)(2,1)S(1)}, bf16[512,768]{1,0:T(8,128)(2,1)}, u32[]{:S(2)}) copy-start(bf16[512,768]{1,0:T(8,128)(2,1)} %constant.54.clone.forward_ref) | copy-start | bytes 2359300
  4.1 9.5 %copy-start.20 = (bf16[256,1536]{1,0:T(8,128)(2,1)S(1)}, bf16[256,1536]{1,0:T(8,128)(2,1)}, u32[]{:S(2)}) copy-start(bf16[256,1536]{1,0:T(8,128)(2,1)} %constant.56.clone.inverse_ref) | copy-start | bytes 2359300
  4.1 9.5 %copy-start.21 = (bf16[384,384]{1,0:T(8,128)(2,1)S(1)}, bf16[384,384]{1,0:T(8,128)(2,1)}, u32[]{:S(2)}) copy-start(bf16[384,384]{1,0:T(8,128)(2,1)} %constant.55.clone.spectrum_ref) | copy-start | bytes 884740
  9.0 29.3 %collective-permute-start = (f32[2048,128]{1,0:T(8,128)S(1)}, f32[2048,128]{1,0:T(8,128)S(1)}, u32[]{:S(2)}, u32[]{:S(2)}) collective-permute-start(f32[2048,128]{1,0:T(8,128)S(1)} %tail.1), channel_id=1, source_target_pairs={{0,2},{2,4},{4,6},{6,8},{8,10},{10,12},{12,14},{14,16},{16,18},{18... | collective-permute-start | bytes 3145736 | tf_op jit(solution)/shard_map/ppermute | solution.py:496
  13.6 24.7 %copy-start.13 = (f32[3,2048,3]{1,2,0:T(4,128)S(1)}, f32[3,2048,3]{1,2,0:T(4,128)}, u32[]{:S(2)}) copy-start(f32[3,2048,3]{1,2,0:T(4,128)} %param.22) | copy-start | bytes 221188
  13.6 24.7 %copy-start.14 = (bf16[144,768]{1,0:T(8,128)(2,1)S(1)}, bf16[144,768]{1,0:T(8,128)(2,1)}, u32[]{:S(2)}) copy-start(bf16[144,768]{1,0:T(8,128)(2,1)} %constant.58.clone.inverse_ref) | copy-start | bytes 663556
  13.6 24.7 %copy-start.15 = (bf16[256,384]{1,0:T(8,128)(2,1)S(1)}, bf16[256,384]{1,0:T(8,128)(2,1)}, u32[]{:S(2)}) copy-start(bf16[256,384]{1,0:T(8,128)(2,1)} %constant.57.clone.forward_ref) | copy-start | bytes 589828
  29.4 1.1 copy-start.2
  30.5 1.0 copy-start.4
  31.4 6.8 %collective-permute-start.1 = (f32[16,2048]{1,0:T(8,128)S(1)}, f32[16,2048]{1,0:T(8,128)S(1)}, u32[]{:S(2)}, u32[]{:S(2)}) collective-permute-start(f32[16,2048]{1,0:T(8,128)S(1)} %get-tuple-element.22), channel_id=1, source_target_pairs={{0,2},{2,4},{4,6},{6,8},{8,10},{10,12},{12,14},{14,16},{16,18},{18... | collective-permute-start | bytes 393224 | tf_op jit(solution)/shard_map/ppermute | solution.py:496
  38.3 1.2 %copy-start.3 = (f32[136,2048]{1,0:T(8,128)S(1)}, f32[136,2048]{1,0:T(8,128)}, u32[]{:S(2)}) copy-start(f32[136,2048]{1,0:T(8,128)} %get-tuple-element.24.medium_ref) | copy-start | bytes 3342340
  39.5 55.0 %copy-start.17 = (f32[2048]{0:T(1024)S(1)}, f32[2048]{0:T(1024)}, u32[]{:S(2)}) copy-start(f32[2048]{0:T(1024)} %param.28) | copy-start | bytes 24580
  49.2 0.8 copy-start.7
  50.0 0.8 copy-start.9
  50.8 27.6 %all-to-all-start = ((f32[128,1,128]{2,1,0:T(1,128)}), f32[128,1,128]{2,1,0:T(1,128)S(1)}, u32[]{:S(2)}, u32[]{:S(2)}) async-start(f32[128,1,128]{2,1,0:T(1,128)} %bitcast.6), calls=%async_computation | async-start | bytes 131072 | tf_op jit(solution)/shard_map/all_to_all | solution.py:697
  94.5 1.2 %copy-start.5 = (f32[120,2048]{1,0:T(8,128)S(1)}, f32[120,2048]{1,0:T(8,128)}, u32[]{:S(2)}) copy-start(f32[120,2048]{1,0:T(8,128)} %copy-done.4) | copy-start | bytes 2949124
  95.7 1.0 copy-start.8
  96.8 1.0 copy-start.10
where the time goes:
time: 114 us; the launch traced here: 113 us
  Pallas kernels  39.2 us (34%)
  starting transfers between devices  24.9 us (22%)
  blocking collectives  22.4 us (20%)
  waiting for transfers between devices  13.8 us (12%)
  local copies, waits for them, and re-layouts  12.4 us (11%)
    all_to_all x1, starting transfers between devices, local(): lax.all_to_all(state.reshape(count, 1, LANES), 'seq', split_axis=0, conca...  17 us
    all_to_all x1, blocking collectives, local(): lax.all_to_all(scanned.reshape(count, 1, LANES), 'seq', split_axis=0, con...  16.1 us
    pallas_call x1, Pallas kernels, local(): call(local_kernel, (steps,), [by_row(T)] * 5 + [by_lane3(3, 3), by_lane3(...  15.8 us
    unnamed x46, local copies, waits for them, and re-layouts  12.3 us
    all_to_all x1, waiting for transfers between devices, local(): lax.all_to_all(state.reshape(count, 1, LANES), 'seq', split_axis=0, conca...  10.4 us
    pallas_call x1, Pallas kernels, local(): call(join_kernel, (steps,), [by_row(LANES), by_lane(RIMS), by_lane(384),...  9.64 us
    ppermute x2, starting transfers between devices, from_behind(): return lax.ppermute(block, 'seq', [(i, i + 1) for i in range(count - 1)])  7.91 us
    psum x1, blocking collectives, local(): total = lax.psum(squares[0], 'chan')  6.32 us
  transfers between devices with their start and end apart: 3, of which 2 were waited for; matrix products, arithmetic and copies ran while one was open for 0% of the time, Pallas kernels for 14%

commit v1 on v0

v1 whole, which is shorter than its diff:
```python
import functools

import jax
import jax.numpy as jnp
import ml_dtypes
import numpy as np
from jax import lax
from jax.experimental import pallas as pl
from jax.experimental.pallas import tpu as pltpu
from jax.sharding import PartitionSpec as P

norm_eps = 1e-06

T = 256
TAPS = 128
MODES = 8
LANES = 128
SEG = 8
HEAD = 17
MAIN = 15
HEAD_ROWS = HEAD * SEG
MAIN_ROWS = MAIN * SEG
RIMS = 16
LIMIT = 24 * 1024 * 1024

F32 = jnp.float32
BF16 = jnp.bfloat16


def row_times():
    head = [HEAD * i + k for k in range(HEAD) for i in range(SEG)]
    main = [HEAD_ROWS + MAIN * i + k for k in range(MAIN) for i in range(SEG)]
    return np.array(head + main)


def packed_forward(slots):
    k = np.arange(128)[:, None]
    angle = 2.0 * np.pi * k * np.asarray(slots)[None, :] / 256.0
    imag = -np.sin(angle)
    imag[0] = np.cos(np.pi * np.asarray(slots))
    return np.concatenate([np.cos(angle), imag], 0)


def packed_inverse(slots):
    k = np.arange(128)[None, :]
    angle = 2.0 * np.pi * k * np.asarray(slots)[:, None] / 256.0
    real = 2.0 * np.cos(angle)
    real[:, 0] = 1.0
    imag = -2.0 * np.sin(angle)
    imag[:, 0] = np.cos(np.pi * np.asarray(slots))
    return np.concatenate([real, imag], 1) / 256.0


def three_pass(matrix):
    high = matrix.astype(ml_dtypes.bfloat16)
    low = (matrix - high.astype(np.float64)).astype(ml_dtypes.bfloat16)
    return np.concatenate([high, low, high], 1)


def tables():
    times = row_times()
    first = packed_forward(times + 128) * (times < 128)[None, :]
    second = packed_forward(times)
    forward = np.concatenate([first, second], 0)
    taps = packed_forward(np.arange(TAPS))
    real, imag = taps[:128], taps[128:].copy()
    cross = real.copy()
    cross[0] = imag[0]
    imag[0] = 0.0
    spectrum = np.concatenate([real, imag, cross], 0)
    inverse = np.concatenate(
        [
            packed_inverse(times + 128) * (times < 128)[:, None],
            packed_inverse(times) * (times >= 128)[:, None],
        ],
        1,
    )
    halo = packed_forward(np.arange(128))
    halo[:, :2] = 0.0
    head_times = np.concatenate([times[:HEAD_ROWS], [-2, -1], np.full(6, 255)])
    halo_back = packed_inverse(head_times + 128) * (head_times < 128)[:, None]
    return [three_pass(m) for m in (forward, spectrum, inverse, halo, halo_back)]


def halves(x):
    high = x.astype(BF16)
    low = (x - high.astype(F32)).astype(BF16)
    return high, low


def matmul3(matrix, x):
    high, low = halves(x)
    stacked = jnp.concatenate([high, high, low], 0)
    return jnp.dot(matrix, stacked, preferred_element_type=F32)


def spectral_product(x, taps):
    real, imag = x[:128], x[128:]
    tap_real, tap_imag, tap_cross = taps[:128], taps[128:256], taps[256:]
    return jnp.concatenate(
        [real * tap_real - imag * tap_imag, real * tap_imag + imag * tap_cross], 0
    )


def sublane(shape):
    return lax.broadcasted_iota(jnp.int32, shape, 0)


def down(x, distance=1):
    return pltpu.roll(x, distance, axis=0)


def fir3(slabs, taps):
    return [
        taps[0] * slabs[k + 2] + taps[1] * slabs[k + 1] + taps[2] * slabs[k]
        for k in range(len(slabs) - 2)
    ]


def with_rims(head, main, rims=None):
    top = sublane(head[0].shape) == 0
    zero = jnp.zeros_like(head[0])
    before = (zero, zero) if rims is None else rims
    ends = [down(head[HEAD - 2]), down(head[HEAD - 1])]
    head_all = [jnp.where(top, before[k], ends[k]) for k in range(2)] + head
    if main is None:
        return head_all, None
    main_all = [jnp.where(top, ends[k], down(main[MAIN - 2 + k])) for k in range(2)] + main
    return head_all, main_all


def rows_of(ref, k, lanes):
    return ref[pl.ds(SEG * k, SEG), lanes]


def spread(row):
    return jnp.broadcast_to(row, (SEG, row.shape[1]))


def recurrence(inputs, decays, gains, skip):
    states = [gains[r] * inputs[0] for r in range(MODES)]
    outs = []
    for k, value in enumerate(inputs):
        if k:
            states = [decays[r] * states[r] + gains[r] * value for r in range(MODES)]
        total = skip * value
        for state in states:
            total = total + state
        outs.append(total)
    return outs, states


def segment_powers(rates, step):
    return [jnp.exp(-(step * distance) * rates) for distance in (1, 2, 4)]


def prefix(state, powers, mode):
    place = sublane(state.shape)
    total = state
    for power, distance in zip(powers, (1, 2, 4)):
        moved = jnp.where(place >= distance, down(total, distance), 0.0)
        total = total + spread(power[mode : mode + 1]) * moved
    return jnp.where(place >= 1, down(total), 0.0), total[SEG - 1 :]


def turned(block):
    return block.T


def tail_kernel(key_hbm, value_hbm, short_ref, tail_ref, key_in, value_in, key_sem, value_sem):
    chunks = key_sem.shape[0]
    rows = key_hbm.shape[0] // chunks
    copies = []
    for chunk in range(chunks):
        here = pl.ds(chunk * rows, rows)
        for source, target, sem in (
            (key_hbm, key_in, key_sem),
            (value_hbm, value_in, value_sem),
        ):
            copy = pltpu.make_async_copy(
                source.at[here, pl.ds(LANES, LANES)], target.at[here, :], sem.at[chunk]
            )
            copy.start()
            copies.append(copy)
    for chunk in range(chunks):
        copies[2 * chunk].wait()
        copies[2 * chunk + 1].wait()
        for tile in range(chunk * rows // LANES, (chunk + 1) * rows // LANES):
            lanes = pl.ds(tile * LANES, LANES)

            def feature(ref, index):
                here = turned(ref[lanes, :])
                taps = [short_ref[index, j : j + 1, lanes] for j in range(3)]
                return taps[0] * here + taps[1] * down(here) + taps[2] * down(here, 2)

            tail_ref[tile] = feature(key_in, 1) * feature(value_in, 2)


def prep_kernel(
    key_hbm,
    value_hbm,
    query_hbm,
    query2_hbm,
    key2_hbm,
    medium_hbm,
    short_ref,
    key_t,
    value_t,
    query_t,
    query2_t,
    key2_t,
    taps_t,
    rims_out,
    key_in,
    value_in,
    query_in,
    query2_in,
    key2_in,
    medium_in,
    sems,
):
    chunks = sems.shape[1]
    rows = key_hbm.shape[0] // chunks
    fields = (
        (key_hbm, key_in, key_t),
        (value_hbm, value_in, value_t),
        (query_hbm, query_in, query_t),
        (query2_hbm, query2_in, query2_t),
        (key2_hbm, key2_in, key2_t),
        (medium_hbm, medium_in, taps_t),
    )
    copies = []
    for chunk in range(chunks):
        here = pl.ds(chunk * rows, rows)
        for place, (source, target, _) in enumerate(fields):
            copy = pltpu.make_async_copy(
                source.at[here, :], target.at[here, :], sems.at[place, chunk]
            )
            copy.start()
            copies.append(copy)
    for chunk in range(chunks):
        for place in range(len(fields)):
            copies[chunk * len(fields) + place].wait()
        for tile in range(chunk * rows // LANES, (chunk + 1) * rows // LANES):
            lanes = pl.ds(tile * LANES, LANES)
            rims_out[tile] = jnp.zeros((RIMS, LANES), F32)
            for place, (_, source, target) in enumerate(fields):
                if place < 5:
                    target[tile] = turned(source[lanes, :])
                    rims_out[tile, 2 * place : 2 * place + 2, :] = target[tile, T - 2 : T, :]
                else:
                    target[tile, 0:TAPS, :] = turned(source[lanes, :])
                    target[tile, TAPS:HEAD_ROWS, :] = jnp.zeros((HEAD_ROWS - TAPS, LANES), F32)

            def feature(ref, index, time):
                return sum(
                    short_ref[index, j : j + 1, lanes] * ref[tile, time - j : time - j + 1, :]
                    for j in range(3)
                )

            for k in range(2):
                rims_out[tile, 10 + k : 11 + k, :] = feature(query_t, 0, T - 2 + k)
            for k in range(3):
                rims_out[tile, 12 + k : 13 + k, :] = feature(key_t, 1, T // 2 - 1 + k) * feature(
                    value_t, 2, T // 2 - 1 + k
                )


def local_kernel(
    key_t,
    value_t,
    query_t,
    query2_t,
    key2_t,
    taps_t,
    short_ref,
    second_ref,
    rate_ref,
    amplitude_ref,
    skip_ref,
    forward_ref,
    spectrum_ref,
    inverse_ref,
    taps_out,
    spectrum_out,
    medium_out,
    query_out,
    key2_out,
    query2_out,
    own_out,
    enter_out,
    leave_out,
    reach_head_out,
    reach_main_out,
    gated_t,
    medium_t,
    query_all,
    key2_all,
):
    tiles = key_t.shape[0]
    group = gated_t.shape[1] // LANES
    top = sublane((SEG, LANES)) == 0
    segment = sublane((SEG, LANES)).astype(F32)

    def slabs_of(ref, tile):
        head = [ref[tile, pl.ds(k, SEG, stride=HEAD), :] for k in range(HEAD)]
        main = [ref[tile, pl.ds(HEAD_ROWS + k, SEG, stride=MAIN), :] for k in range(MAIN)]
        return head, main

    def feature(ref, tile, taps_of, index, lanes):
        taps = [spread(taps_of[index, j : j + 1, lanes]) for j in range(3)]
        head, main = with_rims(*slabs_of(ref, tile))
        return fir3(head, taps) + fir3(main, taps)

    def body(step, _):
        for part in range(group):
            tile = step * group + part
            lanes = pl.ds(pl.multiple_of(tile * LANES, LANES), LANES)
            local = pl.ds(part * LANES, LANES)
            keys = feature(key_t, tile, short_ref, 1, lanes)
            values = feature(value_t, tile, short_ref, 2, lanes)
            for k in range(HEAD + MAIN):
                gated = keys[k] * values[k]
                if k < 2:
                    gated = jnp.where(top, 0.0, gated)
                gated_t[pl.ds(SEG * k, SEG), local] = gated
            for k, slab in enumerate(feature(query_t, tile, short_ref, 0, lanes)):
                query_all[part, pl.ds(SEG * k, SEG), :] = slab
            query_out[tile] = query_all[part, 0:HEAD_ROWS, :]
            for k, slab in enumerate(feature(key2_t, tile, second_ref, 1, lanes)):
                key2_all[part, pl.ds(SEG * k, SEG), :] = slab
            key2_out[tile] = key2_all[part, 0:HEAD_ROWS, :]
            for k, slab in enumerate(feature(query2_t, tile, second_ref, 0, lanes)):
                query2_out[tile, pl.ds(SEG * k, SEG), :] = slab
            for k in range(HEAD):
                taps_out[tile, pl.ds(SEG * k, SEG), :] = taps_t[
                    tile, pl.ds(k, SEG, stride=HEAD), :
                ]

        filters = [taps_t[step * group + part, 0:TAPS, :] for part in range(group)]
        spectrum = matmul3(spectrum_ref[...], jnp.concatenate(filters, 1))
        both = matmul3(forward_ref[...], gated_t[...])
        first = spectral_product(both[:T], spectrum)
        second = spectral_product(both[T:], spectrum)
        medium_t[...] = matmul3(inverse_ref[...], jnp.concatenate([first, second], 0))

        for part in range(group):
            tile = step * group + part
            lanes = pl.ds(pl.multiple_of(tile * LANES, LANES), LANES)
            local = pl.ds(part * LANES, LANES)
            spectrum_out[tile] = spectrum[:, part * LANES : (part + 1) * LANES]
            medium_out[tile] = medium_t[0:HEAD_ROWS, local]
            taps = [spread(second_ref[2, j : j + 1, lanes]) for j in range(3)]
            firsts = [
                rows_of(medium_t, k, local) * query_all[part, pl.ds(SEG * k, SEG), :]
                for k in range(HEAD - 2, HEAD + MAIN)
            ]
            ends = [down(firsts[0]), down(firsts[1])]
            main = firsts[2:]
            main_all = [jnp.where(top, ends[k], down(main[MAIN - 2 + k])) for k in range(2)] + main
            values2 = fir3(main_all, taps)
            inputs = [
                key2_all[part, pl.ds(SEG * (HEAD + k), SEG), :] * values2[k] for k in range(MAIN)
            ]
            rates, gains = rate_ref[:, lanes], amplitude_ref[:, lanes]
            decays = jnp.exp(-rates)
            outs, ends = recurrence(
                inputs,
                [spread(decays[r : r + 1]) for r in range(MODES)],
                [spread(gains[r : r + 1]) for r in range(MODES)],
                spread(skip_ref[:, lanes]),
            )
            for k in range(MAIN):
                own_out[tile, pl.ds(SEG * k, SEG), :] = outs[k]
            powers = segment_powers(rates, float(MAIN))
            for r in range(MODES):
                enter, leave = prefix(ends[r], powers, r)
                enter_out[tile, r] = enter
                leave_out[tile, r : r + 1, :] = leave
                rate = spread(rates[r : r + 1])
                reach_head_out[tile, r] = jnp.exp(-(rate * (segment * float(HEAD))))
                reach_main_out[tile, r] = jnp.exp(-(rate * (segment * float(MAIN))))
        return _

    lax.fori_loop(0, tiles // group, body, 0)


def join_kernel(
    halo_ref,
    rims_ref,
    spectrum_ref,
    medium_ref,
    taps_ref,
    query_ref,
    key2_ref,
    key_t,
    value_t,
    enter_main_ref,
    leave_main_ref,
    reach_main_ref,
    short_ref,
    second_ref,
    rate_ref,
    amplitude_ref,
    skip_ref,
    forward_ref,
    inverse_ref,
    own_out,
    enter_out,
    enter_main_out,
    state_out,
    medium_t,
):
    tiles = halo_ref.shape[0]
    group = medium_t.shape[1] // LANES
    top = sublane((SEG, LANES)) == 0

    def body(step, _):
        tile_list = [step * group + part for part in range(group)]
        halo = matmul3(
            forward_ref[...], jnp.concatenate([halo_ref[tile] for tile in tile_list], 1)
        )
        filters = jnp.concatenate([spectrum_ref[tile] for tile in tile_list], 1)
        medium_t[...] = matmul3(inverse_ref[...], spectral_product(halo, filters))
        for part, tile in enumerate(tile_list):
            one(tile, pl.ds(part * LANES, LANES))
        return _

    def one(tile, local):
        lanes = pl.ds(pl.multiple_of(tile * LANES, LANES), LANES)

        def rim(k):
            return rims_ref[tile, k : k + 1, :]

        def taps_of(ref, index):
            return [ref[index, j : j + 1, lanes] for j in range(3)]

        def early(ref, place, index):
            taps = taps_of(short_ref, index)
            zero, one = ref[tile, 0:1, :], ref[tile, 1:2, :]
            older, last = rim(2 * place), rim(2 * place + 1)
            return (
                taps[0] * zero + taps[1] * last + taps[2] * older,
                taps[0] * one + taps[1] * zero + taps[2] * last,
            )

        def mended(ref, place, taps):
            slabs = [ref[tile, pl.ds(SEG * k, SEG), :] for k in range(HEAD)]
            older, last = rim(2 * place), rim(2 * place + 1)
            slabs[0] = slabs[0] + jnp.where(top, spread(taps[1] * last + taps[2] * older), 0.0)
            slabs[1] = slabs[1] + jnp.where(top, spread(taps[2] * last), 0.0)
            return slabs

        def tap(j):
            row = SEG * (j % HEAD) + j // HEAD
            return taps_ref[tile, row : row + 1, :]

        keys, values = early(key_t, 0, 1), early(value_t, 1, 2)
        gated = [spread(keys[k] * values[k]) for k in range(2)]
        taps = [taps_ref[tile, pl.ds(SEG * k, SEG), :] for k in range(HEAD)]
        shifted = [jnp.where(top, 0.0, down(taps[HEAD - 1]))] + taps
        query = mended(query_ref, 2, taps_of(short_ref, 0))
        key2 = mended(key2_ref, 4, taps_of(second_ref, 1))
        mediums = [
            medium_ref[tile, pl.ds(SEG * k, SEG), :]
            + rows_of(medium_t, k, local)
            + taps[k] * gated[0]
            + shifted[k] * gated[1]
            for k in range(HEAD)
        ]
        far, farther, farthest = rim(14), rim(13), rim(12)
        mediums[0] = mediums[0] + jnp.where(top, spread(tap(127) * far), 0.0)
        older = medium_t[HEAD_ROWS : HEAD_ROWS + 1, local] + (
            tap(125) * far + tap(126) * farther + tap(127) * farthest
        )
        last = medium_t[HEAD_ROWS + 1 : HEAD_ROWS + 2, local] + (
            tap(126) * far + tap(127) * farther
        )
        firsts = [query[k] * mediums[k] for k in range(HEAD)]
        firsts_all, _ = with_rims(firsts, None, (spread(rim(10) * older), spread(rim(11) * last)))
        values2 = fir3(firsts_all, [spread(t) for t in taps_of(second_ref, 2)])
        inputs = [key2[k] * values2[k] for k in range(HEAD)]
        rates, gains = rate_ref[:, lanes], amplitude_ref[:, lanes]
        decays = jnp.exp(-rates)
        outs, ends = recurrence(
            inputs,
            [spread(decays[r : r + 1]) for r in range(MODES)],
            [spread(gains[r : r + 1]) for r in range(MODES)],
            spread(skip_ref[:, lanes]),
        )
        for k in range(HEAD):
            own_out[tile, pl.ds(SEG * k, SEG), :] = outs[k]
        powers = segment_powers(rates, float(HEAD))
        whole = jnp.exp(-float(MAIN_ROWS) * rates)
        for r in range(MODES):
            enter, leave = prefix(ends[r], powers, r)
            enter_out[tile, r] = enter
            enter_main_out[tile, r] = enter_main_ref[tile, r] + reach_main_ref[tile, r] * spread(
                leave
            )
            state_out[tile, r : r + 1, :] = (
                leave_main_ref[tile, r : r + 1, :] + leave * whole[r : r + 1]
            )

    lax.fori_loop(0, tiles // group, body, 0)


def scan_kernel(place_ref, state_ref, rate_ref, out_ref):
    blocks = state_ref.shape[0]
    position = sublane(state_ref.shape)
    index = place_ref[0]
    lanes = pl.ds(pl.multiple_of((index // MODES) * LANES, LANES), LANES)
    rates = rate_ref[:, lanes]
    mine = sublane(rates.shape) == lax.rem(index, MODES)
    rate = jnp.sum(jnp.where(mine, rates, 0.0), axis=0, keepdims=True)
    total = state_ref[...]
    distance = 1
    while distance < blocks:
        moved = jnp.where(position >= distance, down(total, distance), 0.0)
        total = total + jnp.exp(-(float(T) * distance) * rate) * moved
        distance *= 2
    out_ref[...] = jnp.where(position >= 1, down(total), 0.0)


def finish_kernel(
    state_ref,
    own_head_ref,
    own_main_ref,
    enter_head_ref,
    enter_main_ref,
    reach_head_ref,
    reach_main_ref,
    query2_ref,
    rims_ref,
    second_ref,
    rate_ref,
    gain_ref,
    mixed_out,
    squares_out,
    squares_t,
):
    squares_t[...] = jnp.zeros_like(squares_t)
    top = sublane((SEG, LANES)) == 0

    def body(tile, _):
        lanes = pl.ds(pl.multiple_of(tile * LANES, LANES), LANES)
        rates = rate_ref[:, lanes]
        decays = jnp.exp(-rates)
        start = jnp.exp(-float(HEAD_ROWS) * rates)
        taps = [second_ref[0, j : j + 1, lanes] for j in range(3)]
        older, last = rims_ref[tile, 6:7, :], rims_ref[tile, 7:8, :]
        mends = [spread(taps[1] * last + taps[2] * older), spread(taps[2] * last)]
        gain = spread(gain_ref[:, lanes])
        states = state_ref[tile]
        later = states * start
        decay = [spread(decays[r : r + 1]) for r in range(MODES)]

        def half(length, incoming, reach_ref, enter_ref, own_ref, first_row):
            carry = [
                enter_ref[tile, r] + reach_ref[tile, r] * spread(incoming[r : r + 1])
                for r in range(MODES)
            ]
            for k in range(length):
                carry = [decay[r] * carry[r] for r in range(MODES)]
                total = own_ref[tile, pl.ds(SEG * k, SEG), :]
                for value in carry:
                    total = total + value
                rows = pl.ds(first_row + SEG * k, SEG)
                query = query2_ref[tile, rows, :]
                if first_row == 0 and k < 2:
                    query = query + jnp.where(top, mends[k], 0.0)
                mixed = query * total
                squares_t[rows, :] = squares_t[rows, :] + mixed * mixed
                mixed_out[tile, pl.ds(first_row + k, SEG, stride=length), :] = mixed * gain

        half(HEAD, states, reach_head_ref, enter_head_ref, own_head_ref, 0)
        half(MAIN, later, reach_main_ref, enter_main_ref, own_main_ref, HEAD_ROWS)
        return _

    lax.fori_loop(0, query2_ref.shape[0], body, 0)
    sums = jnp.sum(squares_t[...], axis=1, keepdims=True)
    squares_t[...] = jnp.broadcast_to(sums, squares_t.shape)
    head = [squares_t[pl.ds(i, HEAD, stride=SEG), :] for i in range(SEG)]
    main = [squares_t[pl.ds(HEAD_ROWS + i, MAIN, stride=SEG), :] for i in range(SEG)]
    ordered = jnp.concatenate(head + main, 0)
    squares_out[...] = ordered.T[0:1, :]


def scale_kernel(divisor, mixed_ref, squares_ref, out_hbm, out_t, sems):
    scale = lax.rsqrt(squares_ref[...] / divisor + norm_eps)
    chunks = sems.shape[0]
    tiles = mixed_ref.shape[0] // chunks
    copies = []
    for chunk in range(chunks):
        for tile in range(chunk * tiles, (chunk + 1) * tiles):
            out_t[pl.ds(tile * LANES, LANES), :] = mixed_ref[tile].T * scale
        rows = pl.ds(chunk * tiles * LANES, tiles * LANES)
        copy = pltpu.make_async_copy(out_t.at[rows, :], out_hbm.at[rows, :], sems.at[chunk])
        copy.start()
        copies.append(copy)
    for copy in copies:
        copy.wait()


def from_behind(block):
    count = lax.axis_size("seq")
    return lax.ppermute(block, "seq", [(i, i + 1) for i in range(count - 1)])


def in_hbm(x):
    return pltpu.with_memory_space_constraint(x, pltpu.HBM)


def call(kernel, in_specs, out_specs, out_shape, scratch, flops, size, name):
    return pl.pallas_call(
        kernel,
        in_specs=in_specs,
        out_specs=out_specs,
        out_shape=out_shape,
        scratch_shapes=scratch,
        compiler_params=pltpu.CompilerParams(vmem_limit_bytes=LIMIT),
        cost_estimate=pl.CostEstimate(flops=flops, bytes_accessed=size, transcendentals=0),
        name=name,
    )


def exchange(rows):
    count, lanes = rows.shape
    return lax.all_to_all(
        rows.reshape(count, 1, lanes), "seq", split_axis=0, concat_axis=0, tiled=True
    ).reshape(count, lanes)


def local(
    query_proj,
    key_proj,
    value_proj,
    second_query,
    second_key,
    short_filter,
    second_short,
    medium_filter,
    decay_rate,
    residue,
    skip_gain,
    norm_gain,
):
    channels = query_proj.shape[0]
    count = lax.axis_size("seq")
    tiles = channels // LANES
    group = min(2, tiles)
    chunks = min(4, tiles)
    short_t = jnp.transpose(short_filter, (0, 2, 1))
    second_t = jnp.transpose(second_short, (0, 2, 1))
    rate_t = decay_rate.T
    amplitude = residue.T * jnp.sqrt(-jnp.expm1(-2.0 * rate_t))
    skip = skip_gain[None, :]
    gain = norm_gain[None, :]
    forward, spectrum, inverse, halo_forward, halo_inverse = tables()
    held = pl.BlockSpec(memory_space=pltpu.VMEM)
    outside = pl.BlockSpec(memory_space=pl.ANY)
    words = channels * T

    def struct(*shape):
        return jax.ShapeDtypeStruct(shape, F32)

    fields = [
        in_hbm(x) for x in (key_proj, value_proj, query_proj, second_query, second_key, medium_filter)
    ]
    tail = call(
        tail_kernel,
        [outside, outside, held],
        held,
        struct(tiles, TAPS, LANES),
        [pltpu.VMEM((channels, LANES), F32)] * 2 + [pltpu.SemaphoreType.DMA((chunks,))] * 2,
        words * 8,
        words * 6,
        "tail",
    )(fields[0], fields[1], short_t)
    halo = from_behind(tail)

    *turned_fields, taps_t, rims = call(
        prep_kernel,
        [outside] * 6 + [held],
        [held] * 7,
        [struct(tiles, T, LANES)] * 5
        + [struct(tiles, HEAD_ROWS, LANES), struct(tiles, RIMS, LANES)],
        [pltpu.VMEM((channels, T), F32)] * 5
        + [pltpu.VMEM((channels, TAPS), F32), pltpu.SemaphoreType.DMA((6, chunks))],
        words * 20,
        words * 40,
        "prep",
    )(*fields, short_t)
    border = from_behind(rims)

    (
        taps,
        tap_spectrum,
        medium,
        query,
        key2,
        query2,
        own_main,
        enter_main,
        leave_main,
        reach_head,
        reach_main,
    ) = call(
        local_kernel,
        [held] * 14,
        [held] * 11,
        [
            struct(tiles, HEAD_ROWS, LANES),
            struct(tiles, 384, LANES),
            struct(tiles, HEAD_ROWS, LANES),
            struct(tiles, HEAD_ROWS, LANES),
            struct(tiles, HEAD_ROWS, LANES),
            struct(tiles, T, LANES),
            struct(tiles, MAIN_ROWS, LANES),
            struct(tiles, MODES, SEG, LANES),
            struct(tiles, MODES, LANES),
            struct(tiles, MODES, SEG, LANES),
            struct(tiles, MODES, SEG, LANES),
        ],
        [pltpu.VMEM((T, group * LANES), F32)] * 2 + [pltpu.VMEM((group, T, LANES), F32)] * 2,
        words * 8000,
        words * 60,
        "local",
    )(
        *turned_fields,
        taps_t,
        short_t,
        second_t,
        rate_t,
        amplitude,
        skip,
        forward,
        spectrum,
        inverse,
    )

    own_head, enter_head, enter_main, state = call(
        join_kernel,
        [held] * 19,
        [held] * 4,
        [
            struct(tiles, HEAD_ROWS, LANES),
            struct(tiles, MODES, SEG, LANES),
            struct(tiles, MODES, SEG, LANES),
            struct(tiles, MODES, LANES),
        ],
        [pltpu.VMEM((HEAD_ROWS + 8, group * LANES), F32)],
        words * 2000,
        words * 20,
        "join",
    )(
        halo,
        border,
        tap_spectrum,
        medium,
        taps,
        query,
        key2,
        turned_fields[0],
        turned_fields[1],
        enter_main,
        leave_main,
        reach_main,
        short_t,
        second_t,
        rate_t,
        amplitude,
        skip,
        halo_forward,
        halo_inverse,
    )

    place = lax.axis_index("seq").astype(jnp.int32).reshape(1)
    scanned = call(
        scan_kernel,
        [pl.BlockSpec(memory_space=pltpu.SMEM), held, held],
        held,
        struct(count, LANES),
        [],
        count * LANES * 30,
        count * LANES * 8,
        "scan",
    )(place, exchange(state.reshape(count, LANES)), rate_t)
    incoming = exchange(scanned).reshape(tiles, MODES, LANES)

    mixed, squares = call(
        finish_kernel,
        [held] * 12,
        [held] * 2,
        [struct(tiles, T, LANES), struct(1, T)],
        [pltpu.VMEM((T, LANES), F32)],
        words * 40,
        words * 16,
        "finish",
    )(
        incoming,
        own_head,
        own_main,
        enter_head,
        enter_main,
        reach_head,
        reach_main,
        query2,
        border,
        second_t,
        rate_t,
        gain,
    )
    total = lax.psum(squares, "chan")
    return call(
        functools.partial(scale_kernel, float(channels * lax.axis_size("chan"))),
        [held, held],
        outside,
        struct(channels, T),
        [pltpu.VMEM((channels, T), F32), pltpu.SemaphoreType.DMA((chunks,))],
        words,
        words * 8,
        "scale",
    )(mixed, total)


def solution(mesh):
    return jax.shard_map(
        local,
        mesh=mesh,
        in_specs=(
            P("chan", "seq"),
            P("chan", "seq"),
            P("chan", "seq"),
            P("chan", "seq"),
            P("chan", "seq"),
            P(None, "chan", None),
            P(None, "chan", None),
            P("chan", None),
            P("chan", None),
            P("chan", None),
            P("chan"),
            P("chan"),
        ),
        out_specs=P("chan", "seq"),
        check_vma=False,
    )
```

time: 114 us -> 102 us (0.89)
  Pallas kernels: 39.2 us -> 29.6 us
  local copies, waits for them, and re-layouts: 12.4 us -> 9.71 us
    pallas_call x6 -> x7, Pallas kernels: 39.2 us -> 29.6 us  [the longest x1 11.7 us: local(): call(local_kernel, [held] * 14, [held] * 11, [struct(tiles, HEAD_ROWS, LA...]
    unnamed x46 -> x42, local copies, waits for them, and re-layouts: 12.3 us -> 9.71 us
  transfers between devices with their start and end apart: 3 -> 3, of which waited for: 2 -> 2; matrix products, arithmetic and copies ran while one was open for 0% -> 0% of each run, Pallas kernels for 14% -> 17%
where the time goes in v1:
time: 102 us
  Pallas kernels  29.6 us (29%)
  starting transfers between devices  25.3 us (25%)
  blocking collectives  22.4 us (22%)
  waiting for transfers between devices  14.4 us (14%)
  local copies, waits for them, and re-layouts  9.71 us (10%)
    all_to_all x1, starting transfers between devices, exchange(): lax.all_to_all(rows.reshape(count, 1, lanes), 'seq', split_axis=0, concat...  17.3 us
    all_to_all x1, blocking collectives, exchange(): lax.all_to_all(rows.reshape(count, 1, lanes), 'seq', split_axis=0, concat...  16.1 us
    pallas_call x1, Pallas kernels, local(): call(local_kernel, [held] * 14, [held] * 11, [struct(tiles, HEAD_ROWS, LA...  11.7 us
    all_to_all x1, waiting for transfers between devices, exchange(): lax.all_to_all(rows.reshape(count, 1, lanes), 'seq', split_axis=0, concat...  10.5 us
    unnamed x42, local copies, waits for them, and re-layouts  9.71 us
    ppermute x2, starting transfers between devices, from_behind(): return lax.ppermute(block, 'seq', [(i, i + 1) for i in range(count - 1)])  8.06 us
    pallas_call x1, Pallas kernels, local(): call(join_kernel, [held] * 19, [held] * 4, [struct(tiles, HEAD_ROWS, LANE...  7 us
    psum x1, blocking collectives, local(): total = lax.psum(squares, 'chan')  6.34 us
  transfers between devices with their start and end apart: 3, of which 2 were waited for; matrix products, arithmetic and copies ran while one was open for 0% of the time, Pallas kernels for 17%

profile of v1, /device:TPU:1, one launch (start us, length us, event | category | flops | bytes accessed | tf_op | source)
XLA Modules:
  0.0 101.7 jit_solution(7997966700930655064)
XLA Ops:
  0.0 0.0 copy-start.7
  0.0 0.9 copy-done.7
  0.9 2.0 %tail.1 = f32[16,128,128]{2,1,0:T(8,128)S(1)} custom-call(f32[2048,256]{1,0:T(8,128)} %key_hbm.3, f32[2048,256]{1,0:T(8,128)} %value_hbm.3, f32[3,3,2048]{2,1,0:T(4,128)S(1)} %bitcast.21), custom_call_target="tpu_custom_call" | custom-call | flops 4194304 | bytes 3145728 | tf_op jit(solution)/shard_map/tail/pallas_call | solution.py:670
  2.9 0.0 copy-start.4
  3.0 0.0 copy-start.20
  3.0 0.0 copy-start.12
  3.0 0.0 copy-start.15
  3.0 0.0 copy-start.17
  3.0 0.0 copy-start.18
  3.0 0.0 copy-start.19
  3.0 4.6 %collective-permute-start = (f32[16,128,128]{2,1,0:T(8,128)S(1)}, f32[16,128,128]{2,1,0:T(8,128)S(1)}, u32[]{:S(2)}, u32[]{:S(2)}) collective-permute-start(f32[16,128,128]{2,1,0:T(8,128)S(1)} %tail.1), channel_id=1, source_target_pairs={{0,2},{2,4},{4,6},{6,8},{8,10},{10,12},{12,14},{14,16},{16,18},{18... | collective-permute-start | bytes 3145736 | tf_op jit(solution)/shard_map/ppermute | solution.py:607
  7.6 5.4 %prep.1 = (f32[16,256,128]{2,1,0:T(8,128)S(1)}, f32[16,256,128]{2,1,0:T(8,128)S(1)}, f32[16,256,128]{2,1,0:T(8,128)S(1)}, f32[16,256,128]{2,1,0:T(8,128)S(1)}, f...) custom-call(f32[2048,256]{1,0:T(8,128)} %key_hbm.3, f32[2048,256]{1,0:T(8,128)} %value_hbm.3, ...), custom_call_target="tpu_custom_call" | custom-call | flops 10485760 | bytes 20971520 | tf_op jit(solution)/shard_map/prep/pallas_call | solution.py:682
  13.0 3.5 %collective-permute-start.1 = (f32[16,16,128]{2,1,0:T(8,128)S(1)}, f32[16,16,128]{2,1,0:T(8,128)S(1)}, u32[]{:S(2)}, u32[]{:S(2)}) collective-permute-start(f32[16,16,128]{2,1,0:T(8,128)S(1)} %get-tuple-element.29), channel_id=1, source_target_pairs={{0,2},{2,4},{4,6},{6,8},{8,10},{10,12},{12,14},{14,16},{16,18},{18... | collective-permute-start | bytes 393224 | tf_op jit(solution)/shard_map/ppermute | solution.py:607
  16.5 0.0 copy-done.4
  16.5 0.0 copy-done.20
  16.6 0.0 copy-done.12
  16.6 0.0 copy-done.15
  16.6 0.0 copy-done.17
  16.6 0.0 copy-done.18
  16.6 0.0 copy-done.19
  16.6 0.0 copy-start.13
  16.6 0.0 copy-start.14
  16.6 11.7 %local.1 = (f32[16,136,128]{2,1,0:T(8,128)S(1)}, f32[16,384,128]{2,1,0:T(8,128)S(1)}, f32[16,136,128]{2,1,0:T(8,128)S(1)}, f32[16,136,128]{2,1,0:T(8,128)S(1)}, ...) custom-call(f32[16,256,128]{2,1,0:T(8,128)S(1)} %get-tuple-element.3, ...), custom_call_target="tpu_custom_call" | custom-call | flops 4194304000 | bytes 31457280 | tf_op jit(solution)/shard_map/local/pallas_call | solution.py:708
  28.3 0.0 copy-start
  28.3 0.0 copy-start.5
  28.3 3.8 %collective-permute-done.1.rims_ref = f32[16,16,128]{2,1,0:T(8,128)S(1)} collective-permute-done((f32[16,16,128]{2,1,0:T(8,128)S(1)}, f32[16,16,128]{2,1,0:T(8,128)S(1)}, u32[]{:S(2)}, u32[]{:S(2)}) %collective-permute-start.1) | collective-permute-done | bytes 131104 | tf_op jit(solution)/shard_map/ppermute | solution.py:607
  32.2 0.0 collective-permute-done.halo_ref
  32.2 0.0 copy-done.13
  32.2 0.0 copy-done.14
  32.2 0.0 copy-start.16
  32.2 7.0 %join.1 = (f32[16,136,128]{2,1,0:T(8,128)S(1)}, f32[16,8,8,128]{3,2,1,0:T(8,128)S(1)}, f32[16,8,8,128]{3,2,1,0:T(8,128)S(1)}, f32[16,8,128]{2,1,0:T(8,128)}) custom-call(f32[16,128,128]{2,1,0:T(8,128)S(1)} %collective-permute-done.halo_ref, f32[16,16,128]{2,1,0:T(8,128)S(1)} %collective-permute-done.1.rims_ref, ...), custom_call_target="tpu_custom_call" | custom-call | flops 1048576000 | bytes 10485760 | tf_op jit(solution)/shard_map/join/pallas_call | solution.py:742
  39.2 0.0 copy-done
  39.2 0.0 copy-done.5
  39.2 0.0 copy-start.2
  39.2 1.0 copy-done.2
  40.2 0.0 copy-start.8
  40.2 0.8 copy-done.8
  41.0 0.0 copy-start.10
  41.0 0.8 copy-done.10
  41.8 17.3 %all-to-all-start = ((f32[128,1,128]{2,1,0:T(1,128)}), f32[128,1,128]{2,1,0:T(1,128)S(1)}, u32[]{:S(2)}, u32[]{:S(2)}) async-start(f32[128,1,128]{2,1,0:T(1,128)} %bitcast.7), calls=%async_computation | async-start | bytes 131072 | tf_op jit(solution)/shard_map/all_to_all | solution.py:629
  59.1 10.5 %all-to-all-done = f32[128,1,128]{2,1,0:T(1,128)S(1)} async-done(((f32[128,1,128]{2,1,0:T(1,128)}), f32[128,1,128]{2,1,0:T(1,128)S(1)}, u32[]{:S(2)}, u32[]{:S(2)}) %all-to-all-start) | async-done | bytes 65568 | tf_op jit(solution)/shard_map/all_to_all | solution.py:629
  69.6 0.1 scan.1
  69.7 16.1 %all_to_all.10 = f32[128,1,128]{2,1,0:T(1,128)S(1)} all-to-all(f32[128,1,128]{2,1,0:T(1,128)S(1)} %bitcast.30), channel_id=1, replica_groups=mesh['seq'=128,'chan'=2] {'seq'}, dimensions={0} | all-to-all | bytes 131072 | tf_op jit(solution)/shard_map/all_to_all | solution.py:629
  85.8 0.0 copy-done.16
  85.8 0.0 copy-start.1
  85.8 1.6 %copy-done.1 = f32[16,256,128]{2,1,0:T(8,128)S(1)} copy-done((f32[16,256,128]{2,1,0:T(8,128)S(1)}, f32[16,256,128]{2,1,0:T(8,128)}, u32[]{:S(2)}) %copy-start.1) | copy-done | bytes 2097176
  87.4 0.0 copy-start.3
  87.4 1.2 %copy-done.3 = f32[16,136,128]{2,1,0:T(8,128)S(1)} copy-done((f32[16,136,128]{2,1,0:T(8,128)S(1)}, f32[16,136,128]{2,1,0:T(8,128)}, u32[]{:S(2)}) %copy-start.3) | copy-done | bytes 1114136
  88.6 0.0 copy-start.6
  88.6 1.2 %copy-done.6 = f32[16,120,128]{2,1,0:T(8,128)S(1)} copy-done((f32[16,120,128]{2,1,0:T(8,128)S(1)}, f32[16,120,128]{2,1,0:T(8,128)}, u32[]{:S(2)}) %copy-start.6) | copy-done | bytes 983064
  89.8 0.0 copy-start.9
  89.8 1.0 %copy-done.9 = f32[16,8,8,128]{3,2,1,0:T(8,128)S(1)} copy-done((f32[16,8,8,128]{3,2,1,0:T(8,128)S(1)}, f32[16,8,8,128]{3,2,1,0:T(8,128)}, u32[]{:S(2)}) %copy-start.9) | copy-done | bytes 524312
  90.9 0.0 copy-start.11
  90.9 1.0 %copy-done.11 = f32[16,8,8,128]{3,2,1,0:T(8,128)S(1)} copy-done((f32[16,8,8,128]{3,2,1,0:T(8,128)S(1)}, f32[16,8,8,128]{3,2,1,0:T(8,128)}, u32[]{:S(2)}) %copy-start.11) | copy-done | bytes 524312
  91.9 1.9 %finish.1 = (f32[16,256,128]{2,1,0:T(8,128)S(1)}, f32[1,256]{1,0:T(1,128)S(1)}) custom-call(f32[16,8,128]{2,1,0:T(8,128)S(1)} %bitcast.28, f32[16,136,128]{2,1,0:T(8,128)S(1)} %copy-done.3, f32[16,120,128]{2,1,0:T(8,128)S(1)} %copy-done.6, f32[16,8,8,128]{3,2,1,0:T(8,128)S(1)} %copy-done.9, f32[16,8,8,128]{3,2,1,0:T(8,128)S(1)} %copy-done.11, ...), custom_call_target="tpu_custom_call" | custom-call | flops 20971520 | bytes 8388608 | tf_op jit(solution)/shard_map/finish/pallas_call | solution.py:791
  93.8 6.3 %psum.7.squares_ref = f32[1,256]{1,0:T(1,128)S(1)} all-reduce(f32[1,256]{1,0:T(1,128)S(1)} %get-tuple-element.52), channel_id=1, replica_groups=mesh['seq'=128,'chan'=2] {'chan'}, use_global_device_ids=true, to_apply=%region_0.0 | all-reduce | flops 256 | bytes 2048 | tf_op jit(solution)/shard_map/psum | solution.py:814
  100.1 1.5 %scale.1 = f32[2048,256]{1,0:T(8,128)} custom-call(f32[16,256,128]{2,1,0:T(8,128)S(1)} %get-tuple-element.51.mixed_ref, f32[1,256]{1,0:T(1,128)S(1)} %psum.7.squares_ref), custom_call_target="tpu_custom_call" | custom-call | flops 524288 | bytes 4194304 | tf_op jit(solution)/shard_map/scale/pallas_call | solution.py:815
  (1 shorter events, 0.0 us)
Async XLA Ops:
  0.0 0.9 copy-start.7
  2.9 13.6 %copy-start.4 = (f32[2048,8]{0,1:T(8,128)S(1)}, f32[2048,8]{0,1:T(8,128)}, u32[]{:S(2)}) copy-start(f32[2048,8]{0,1:T(8,128)} %param.25) | copy-start | bytes 196612
  3.0 13.6 %copy-start.20 = (f32[2048,8]{0,1:T(8,128)S(1)}, f32[2048,8]{0,1:T(8,128)}, u32[]{:S(2)}) copy-start(f32[2048,8]{0,1:T(8,128)} %param.26) | copy-start | bytes 196612
  3.0 13.6 %copy-start.12 = (f32[3,2048,3]{1,2,0:T(4,128)S(1)}, f32[3,2048,3]{1,2,0:T(4,128)}, u32[]{:S(2)}) copy-start(f32[3,2048,3]{1,2,0:T(4,128)} %param.23) | copy-start | bytes 221188
  3.0 13.6 %copy-start.15 = (f32[2048]{0:T(1024)S(1)}, f32[2048]{0:T(1024)}, u32[]{:S(2)}) copy-start(f32[2048]{0:T(1024)} %param.27) | copy-start | bytes 24580
  3.0 13.6 %copy-start.17 = (bf16[512,768]{1,0:T(8,128)(2,1)S(1)}, bf16[512,768]{1,0:T(8,128)(2,1)}, u32[]{:S(2)}) copy-start(bf16[512,768]{1,0:T(8,128)(2,1)} %constant.18.clone.forward_ref) | copy-start | bytes 2359300
  3.0 13.6 %copy-start.18 = (bf16[256,1536]{1,0:T(8,128)(2,1)S(1)}, bf16[256,1536]{1,0:T(8,128)(2,1)}, u32[]{:S(2)}) copy-start(bf16[256,1536]{1,0:T(8,128)(2,1)} %constant.20.clone.inverse_ref) | copy-start | bytes 2359300
  3.0 13.6 %copy-start.19 = (bf16[384,384]{1,0:T(8,128)(2,1)S(1)}, bf16[384,384]{1,0:T(8,128)(2,1)}, u32[]{:S(2)}) copy-start(bf16[384,384]{1,0:T(8,128)(2,1)} %constant.19.clone.spectrum_ref) | copy-start | bytes 884740
  3.0 29.1 %collective-permute-start = (f32[16,128,128]{2,1,0:T(8,128)S(1)}, f32[16,128,128]{2,1,0:T(8,128)S(1)}, u32[]{:S(2)}, u32[]{:S(2)}) collective-permute-start(f32[16,128,128]{2,1,0:T(8,128)S(1)} %tail.1), channel_id=1, source_target_pairs={{0,2},{2,4},{4,6},{6,8},{8,10},{10,12},{12,14},{14,16},{16,18},{18... | collective-permute-start | bytes 3145736 | tf_op jit(solution)/shard_map/ppermute | solution.py:607
  13.0 19.2 %collective-permute-start.1 = (f32[16,16,128]{2,1,0:T(8,128)S(1)}, f32[16,16,128]{2,1,0:T(8,128)S(1)}, u32[]{:S(2)}, u32[]{:S(2)}) collective-permute-start(f32[16,16,128]{2,1,0:T(8,128)S(1)} %get-tuple-element.29), channel_id=1, source_target_pairs={{0,2},{2,4},{4,6},{6,8},{8,10},{10,12},{12,14},{14,16},{16,18},{18... | collective-permute-start | bytes 393224 | tf_op jit(solution)/shard_map/ppermute | solution.py:607
  16.6 15.5 %copy-start.13 = (bf16[144,768]{1,0:T(8,128)(2,1)S(1)}, bf16[144,768]{1,0:T(8,128)(2,1)}, u32[]{:S(2)}) copy-start(bf16[144,768]{1,0:T(8,128)(2,1)} %constant.22.clone.inverse_ref) | copy-start | bytes 663556
  16.6 15.5 %copy-start.14 = (bf16[256,384]{1,0:T(8,128)(2,1)S(1)}, bf16[256,384]{1,0:T(8,128)(2,1)}, u32[]{:S(2)}) copy-start(bf16[256,384]{1,0:T(8,128)(2,1)} %constant.21.clone.forward_ref) | copy-start | bytes 589828
  28.3 10.9 %copy-start = (f32[16,256,128]{2,1,0:T(8,128)}, f32[16,256,128]{2,1,0:T(8,128)S(1)}, u32[]{:S(2)}) copy-start(f32[16,256,128]{2,1,0:T(8,128)S(1)} %get-tuple-element.50.query2_ref) | copy-start | bytes 6291460
  28.3 10.9 %copy-start.5 = (f32[16,120,128]{2,1,0:T(8,128)}, f32[16,120,128]{2,1,0:T(8,128)S(1)}, u32[]{:S(2)}) copy-start(f32[16,120,128]{2,1,0:T(8,128)S(1)} %get-tuple-element.46.own_main_ref) | copy-start | bytes 2949124
  32.2 53.6 %copy-start.16 = (f32[2048]{0:T(1024)S(1)}, f32[2048]{0:T(1024)}, u32[]{:S(2)}) copy-start(f32[2048]{0:T(1024)} %param.28) | copy-start | bytes 24580
  39.2 1.0 %copy-start.2 = (f32[16,136,128]{2,1,0:T(8,128)}, f32[16,136,128]{2,1,0:T(8,128)S(1)}, u32[]{:S(2)}) copy-start(f32[16,136,128]{2,1,0:T(8,128)S(1)} %get-tuple-element.45.own_head_ref) | copy-start | bytes 3342340
  40.2 0.8 copy-start.8
  41.0 0.8 copy-start.10
  41.8 27.8 %all-to-all-start = ((f32[128,1,128]{2,1,0:T(1,128)}), f32[128,1,128]{2,1,0:T(1,128)S(1)}, u32[]{:S(2)}, u32[]{:S(2)}) async-start(f32[128,1,128]{2,1,0:T(1,128)} %bitcast.7), calls=%async_computation | async-start | bytes 131072 | tf_op jit(solution)/shard_map/all_to_all | solution.py:629
  85.8 1.6 %copy-start.1 = (f32[16,256,128]{2,1,0:T(8,128)S(1)}, f32[16,256,128]{2,1,0:T(8,128)}, u32[]{:S(2)}) copy-start(f32[16,256,128]{2,1,0:T(8,128)} %copy-done) | copy-start | bytes 6291460
  87.4 1.2 %copy-start.3 = (f32[16,136,128]{2,1,0:T(8,128)S(1)}, f32[16,136,128]{2,1,0:T(8,128)}, u32[]{:S(2)}) copy-start(f32[16,136,128]{2,1,0:T(8,128)} %copy-done.2) | copy-start | bytes 3342340
  88.6 1.2 %copy-start.6 = (f32[16,120,128]{2,1,0:T(8,128)S(1)}, f32[16,120,128]{2,1,0:T(8,128)}, u32[]{:S(2)}) copy-start(f32[16,120,128]{2,1,0:T(8,128)} %copy-done.5) | copy-start | bytes 2949124
  89.8 1.0 %copy-start.9 = (f32[16,8,8,128]{3,2,1,0:T(8,128)S(1)}, f32[16,8,8,128]{3,2,1,0:T(8,128)}, u32[]{:S(2)}) copy-start(f32[16,8,8,128]{3,2,1,0:T(8,128)} %copy-done.8) | copy-start | bytes 1572868
  90.9 1.0 %copy-start.11 = (f32[16,8,8,128]{3,2,1,0:T(8,128)S(1)}, f32[16,8,8,128]{3,2,1,0:T(8,128)}, u32[]{:S(2)}) copy-start(f32[16,8,8,128]{3,2,1,0:T(8,128)} %copy-done.10) | copy-start | bytes 1572868

commit v2 on v1

--- a/solution.py
+++ b/solution.py
@@ -167,10 +167,14 @@
     return block.T
 
 
-def tail_kernel(key_hbm, value_hbm, short_ref, tail_ref, key_in, value_in, key_sem, value_sem):
+def tail_kernel(
+    key_hbm, value_hbm, short_hbm, tail_ref, key_in, value_in, short_ref, key_sem, value_sem, short_sem
+):
     chunks = key_sem.shape[0]
     rows = key_hbm.shape[0] // chunks
     copies = []
+    filters = pltpu.make_async_copy(short_hbm, short_ref, short_sem)
+    filters.start()
     for chunk in range(chunks):
         here = pl.ds(chunk * rows, rows)
         for source, target, sem in (
@@ -182,6 +186,7 @@
             )
             copy.start()
             copies.append(copy)
+    filters.wait()
     for chunk in range(chunks):
         copies[2 * chunk].wait()
         copies[2 * chunk + 1].wait()
@@ -267,6 +272,7 @@
 
 
 def local_kernel(
+    place_ref,
     key_t,
     value_t,
     query_t,
@@ -286,17 +292,24 @@
     medium_out,
     query_out,
     key2_out,
-    query2_out,
-    own_out,
     enter_out,
     leave_out,
-    reach_head_out,
     reach_main_out,
+    own_rate_out,
+    late_hbm,
     gated_t,
     medium_t,
     query_all,
     key2_all,
+    late,
+    late_sem,
 ):
+    index = place_ref[0]
+    mine = pl.ds(pl.multiple_of((index // MODES) * LANES, LANES), LANES)
+    rates = rate_ref[:, mine]
+    chosen = sublane(rates.shape) == lax.rem(index, MODES)
+    own_rate_out[...] = jnp.sum(jnp.where(chosen, rates, 0.0), axis=0, keepdims=True)
+
     tiles = key_t.shape[0]
     group = gated_t.shape[1] // LANES
     top = sublane((SEG, LANES)) == 0
@@ -331,7 +344,7 @@
                 key2_all[part, pl.ds(SEG * k, SEG), :] = slab
             key2_out[tile] = key2_all[part, 0:HEAD_ROWS, :]
             for k, slab in enumerate(feature(query2_t, tile, second_ref, 0, lanes)):
-                query2_out[tile, pl.ds(SEG * k, SEG), :] = slab
+                late[tile, pl.ds(SEG * k, SEG), :] = slab
             for k in range(HEAD):
                 taps_out[tile, pl.ds(SEG * k, SEG), :] = taps_t[
                     tile, pl.ds(k, SEG, stride=HEAD), :
@@ -371,18 +384,20 @@
                 spread(skip_ref[:, lanes]),
             )
             for k in range(MAIN):
-                own_out[tile, pl.ds(SEG * k, SEG), :] = outs[k]
+                late[tile, pl.ds(T + SEG * k, SEG), :] = outs[k]
+            pltpu.make_async_copy(late.at[tile], late_hbm.at[tile], late_sem.at[tile]).start()
             powers = segment_powers(rates, float(MAIN))
             for r in range(MODES):
                 enter, leave = prefix(ends[r], powers, r)
                 enter_out[tile, r] = enter
                 leave_out[tile, r : r + 1, :] = leave
                 rate = spread(rates[r : r + 1])
-                reach_head_out[tile, r] = jnp.exp(-(rate * (segment * float(HEAD))))
                 reach_main_out[tile, r] = jnp.exp(-(rate * (segment * float(MAIN))))
         return _
 
     lax.fori_loop(0, tiles // group, body, 0)
+    for tile in range(tiles):
+        pltpu.make_async_copy(late.at[tile], late_hbm.at[tile], late_sem.at[tile]).wait()
 
 
 def join_kernel(
@@ -405,11 +420,11 @@
     skip_ref,
     forward_ref,
     inverse_ref,
-    own_out,
-    enter_out,
-    enter_main_out,
     state_out,
+    late_hbm,
     medium_t,
+    late,
+    late_sem,
 ):
     tiles = halo_ref.shape[0]
     group = medium_t.shape[1] // LANES
@@ -489,30 +504,29 @@
             spread(skip_ref[:, lanes]),
         )
         for k in range(HEAD):
-            own_out[tile, pl.ds(SEG * k, SEG), :] = outs[k]
+            late[tile, pl.ds(SEG * k, SEG), :] = outs[k]
         powers = segment_powers(rates, float(HEAD))
         whole = jnp.exp(-float(MAIN_ROWS) * rates)
         for r in range(MODES):
             enter, leave = prefix(ends[r], powers, r)
-            enter_out[tile, r] = enter
-            enter_main_out[tile, r] = enter_main_ref[tile, r] + reach_main_ref[tile, r] * spread(
-                leave
-            )
+            late[tile, pl.ds(HEAD_ROWS + SEG * r, SEG), :] = enter
+            late[tile, pl.ds(HEAD_ROWS + SEG * (MODES + r), SEG), :] = enter_main_ref[
+                tile, r
+            ] + reach_main_ref[tile, r] * spread(leave)
             state_out[tile, r : r + 1, :] = (
                 leave_main_ref[tile, r : r + 1, :] + leave * whole[r : r + 1]
             )
-
-    lax.fori_loop(0, tiles // group, body, 0)
-
-
-def scan_kernel(place_ref, state_ref, rate_ref, out_ref):
+        pltpu.make_async_copy(late.at[tile], late_hbm.at[tile], late_sem.at[tile]).start()
+
+    lax.fori_loop(0, tiles // group, body, 0, unroll=True)
+    for tile in range(tiles):
+        pltpu.make_async_copy(late.at[tile], late_hbm.at[tile], late_sem.at[tile]).wait()
+
+
+def scan_kernel(state_ref, rate_ref, out_ref):
     blocks = state_ref.shape[0]
     position = sublane(state_ref.shape)
-    index = place_ref[0]
-    lanes = pl.ds(pl.multiple_of((index // MODES) * LANES, LANES), LANES)
-    rates = rate_ref[:, lanes]
-    mine = sublane(rates.shape) == lax.rem(index, MODES)
-    rate = jnp.sum(jnp.where(mine, rates, 0.0), axis=0, keepdims=True)
+    rate = rate_ref[...]
     total = state_ref[...]
     distance = 1
     while distance < blocks:
@@ -524,60 +538,82 @@
 
 def finish_kernel(
     state_ref,
-    own_head_ref,
-    own_main_ref,
-    enter_head_ref,
-    enter_main_ref,
-    reach_head_ref,
-    reach_main_ref,
-    query2_ref,
+    early_hbm,
+    late_hbm,
     rims_ref,
     second_ref,
     rate_ref,
     gain_ref,
     mixed_out,
     squares_out,
+    early,
+    late,
+    reach,
     squares_t,
+    sems,
 ):
+    tiles = early_hbm.shape[0]
+    chunks = sems.shape[1]
+    count = tiles // chunks
+    copies = []
+    for chunk in range(chunks):
+        here = pl.ds(chunk * count, count)
+        for place, (source, target) in enumerate(((early_hbm, early), (late_hbm, late))):
+            copy = pltpu.make_async_copy(source.at[here], target.at[here], sems.at[place, chunk])
+            copy.start()
+            copies.append(copy)
     squares_t[...] = jnp.zeros_like(squares_t)
     top = sublane((SEG, LANES)) == 0
+    segment = sublane((SEG, LANES)).astype(F32)
+
+    def reaches(tile, _):
+        lanes = pl.ds(pl.multiple_of(tile * LANES, LANES), LANES)
+        for r in range(MODES):
+            rate = spread(rate_ref[r : r + 1, lanes])
+            reach[tile, r] = jnp.exp(-(rate * (segment * float(HEAD))))
+            reach[tile, MODES + r] = jnp.exp(-(rate * (segment * float(MAIN) + float(HEAD_ROWS))))
+        return _
+
+    lax.fori_loop(0, tiles, reaches, 0)
 
     def body(tile, _):
         lanes = pl.ds(pl.multiple_of(tile * LANES, LANES), LANES)
-        rates = rate_ref[:, lanes]
-        decays = jnp.exp(-rates)
-        start = jnp.exp(-float(HEAD_ROWS) * rates)
+        decays = jnp.exp(-rate_ref[:, lanes])
         taps = [second_ref[0, j : j + 1, lanes] for j in range(3)]
         older, last = rims_ref[tile, 6:7, :], rims_ref[tile, 7:8, :]
         mends = [spread(taps[1] * last + taps[2] * older), spread(taps[2] * last)]
         gain = spread(gain_ref[:, lanes])
         states = state_ref[tile]
-        later = states * start
         decay = [spread(decays[r : r + 1]) for r in range(MODES)]
 
-        def half(length, incoming, reach_ref, enter_ref, own_ref, first_row):
+        def half(length, half_index, own_ref, own_row, first_row):
+            enter_row = HEAD_ROWS + half_index * MODES * SEG
             carry = [
-                enter_ref[tile, r] + reach_ref[tile, r] * spread(incoming[r : r + 1])
+                late[tile, pl.ds(enter_row + SEG * r, SEG), :]
+                + reach[tile, half_index * MODES + r] * spread(states[r : r + 1])
                 for r in range(MODES)
             ]
             for k in range(length):
                 carry = [decay[r] * carry[r] for r in range(MODES)]
-                total = own_ref[tile, pl.ds(SEG * k, SEG), :]
+                total = own_ref[tile, pl.ds(own_row + SEG * k, SEG), :]
                 for value in carry:
                     total = total + value
                 rows = pl.ds(first_row + SEG * k, SEG)
-                query = query2_ref[tile, rows, :]
+                query = early[tile, rows, :]
                 if first_row == 0 and k < 2:
                     query = query + jnp.where(top, mends[k], 0.0)
                 mixed = query * total
                 squares_t[rows, :] = squares_t[rows, :] + mixed * mixed
                 mixed_out[tile, pl.ds(first_row + k, SEG, stride=length), :] = mixed * gain
 
-        half(HEAD, states, reach_head_ref, enter_head_ref, own_head_ref, 0)
-        half(MAIN, later, reach_main_ref, enter_main_ref, own_main_ref, HEAD_ROWS)
+        half(HEAD, 0, late, 0, 0)
+        half(MAIN, 1, early, T, HEAD_ROWS)
         return _
 
-    lax.fori_loop(0, query2_ref.shape[0], body, 0)
+    for chunk in range(chunks):
+        copies[2 * chunk].wait()
+        copies[2 * chunk + 1].wait()
+        lax.fori_loop(chunk * count, (chunk + 1) * count, body, 0)
     sums = jnp.sum(squares_t[...], axis=1, keepdims=True)
     squares_t[...] = jnp.broadcast_to(sums, squares_t.shape)
     head = [squares_t[pl.ds(i, HEAD, stride=SEG), :] for i in range(SEG)]
@@ -648,7 +684,8 @@
     channels = query_proj.shape[0]
     count = lax.axis_size("seq")
     tiles = channels // LANES
-    group = min(2, tiles)
+    group = min(4, tiles)
+    join_group = min(2, tiles)
     chunks = min(4, tiles)
     short_t = jnp.transpose(short_filter, (0, 2, 1))
     second_t = jnp.transpose(second_short, (0, 2, 1))
@@ -664,19 +701,25 @@
     def struct(*shape):
         return jax.ShapeDtypeStruct(shape, F32)
 
+    def hbm(*shape):
+        return pltpu.HBM(shape, F32)
+
     fields = [
         in_hbm(x) for x in (key_proj, value_proj, query_proj, second_query, second_key, medium_filter)
     ]
     tail = call(
         tail_kernel,
-        [outside, outside, held],
+        [outside] * 3,
         held,
         struct(tiles, TAPS, LANES),
-        [pltpu.VMEM((channels, LANES), F32)] * 2 + [pltpu.SemaphoreType.DMA((chunks,))] * 2,
+        [pltpu.VMEM((channels, LANES), F32)] * 2
+        + [pltpu.VMEM((3, 3, channels), F32)]
+        + [pltpu.SemaphoreType.DMA((chunks,))] * 2
+        + [pltpu.SemaphoreType.DMA],
         words * 8,
         words * 6,
         "tail",
-    )(fields[0], fields[1], short_t)
+    )(fields[0], fields[1], in_hbm(short_t))
     halo = from_behind(tail)
 
     *turned_fields, taps_t, rims = call(
@@ -693,40 +736,42 @@
     )(*fields, short_t)
     border = from_behind(rims)
 
+    place = lax.axis_index("seq").astype(jnp.int32).reshape(1)
     (
         taps,
         tap_spectrum,
         medium,
         query,
         key2,
-        query2,
-        own_main,
         enter_main,
         leave_main,
-        reach_head,
         reach_main,
+        own_rate,
+        early,
     ) = call(
         local_kernel,
-        [held] * 14,
-        [held] * 11,
+        [pl.BlockSpec(memory_space=pltpu.SMEM)] + [held] * 14,
+        [held] * 9 + [outside],
         [
             struct(tiles, HEAD_ROWS, LANES),
             struct(tiles, 384, LANES),
             struct(tiles, HEAD_ROWS, LANES),
             struct(tiles, HEAD_ROWS, LANES),
             struct(tiles, HEAD_ROWS, LANES),
-            struct(tiles, T, LANES),
-            struct(tiles, MAIN_ROWS, LANES),
             struct(tiles, MODES, SEG, LANES),
             struct(tiles, MODES, LANES),
             struct(tiles, MODES, SEG, LANES),
-            struct(tiles, MODES, SEG, LANES),
+            struct(1, LANES),
+            hbm(tiles, T + MAIN_ROWS, LANES),
         ],
-        [pltpu.VMEM((T, group * LANES), F32)] * 2 + [pltpu.VMEM((group, T, LANES), F32)] * 2,
+        [pltpu.VMEM((T, group * LANES), F32)] * 2
+        + [pltpu.VMEM((group, T, LANES), F32)] * 2
+        + [pltpu.VMEM((tiles, T + MAIN_ROWS, LANES), F32), pltpu.SemaphoreType.DMA((tiles,))],
         words * 8000,
         words * 60,
         "local",
     )(
+        place,
         *turned_fields,
         taps_t,
         short_t,
@@ -739,17 +784,17 @@
         inverse,
     )
 
-    own_head, enter_head, enter_main, state = call(
+    late_rows = HEAD_ROWS + 2 * MODES * SEG
+    state, late = call(
         join_kernel,
         [held] * 19,
-        [held] * 4,
+        [held, outside],
+        [struct(tiles, MODES, LANES), hbm(tiles, late_rows, LANES)],
         [
-            struct(tiles, HEAD_ROWS, LANES),
-            struct(tiles, MODES, SEG, LANES),
-            struct(tiles, MODES, SEG, LANES),
-            struct(tiles, MODES, LANES),
+            pltpu.VMEM((HEAD_ROWS + 8, join_group * LANES), F32),
+            pltpu.VMEM((tiles, late_rows, LANES), F32),
+            pltpu.SemaphoreType.DMA((tiles,)),
         ],
-        [pltpu.VMEM((HEAD_ROWS + 8, group * LANES), F32)],
         words * 2000,
         words * 20,
         "join",
@@ -775,42 +820,34 @@
         halo_inverse,
     )
 
-    place = lax.axis_index("seq").astype(jnp.int32).reshape(1)
     scanned = call(
         scan_kernel,
-        [pl.BlockSpec(memory_space=pltpu.SMEM), held, held],
+        [held] * 2,
         held,
         struct(count, LANES),
         [],
         count * LANES * 30,
         count * LANES * 8,
         "scan",
-    )(place, exchange(state.reshape(count, LANES)), rate_t)
+    )(exchange(state.reshape(count, LANES)), own_rate)
     incoming = exchange(scanned).reshape(tiles, MODES, LANES)
 
     mixed, squares = call(
         finish_kernel,
-        [held] * 12,
+        [held, outside, outside] + [held] * 4,
         [held] * 2,
         [struct(tiles, T, LANES), struct(1, T)],
-        [pltpu.VMEM((T, LANES), F32)],
+        [
+            pltpu.VMEM((tiles, T + MAIN_ROWS, LANES), F32),
+            pltpu.VMEM((tiles, late_rows, LANES), F32),
+            pltpu.VMEM((tiles, 2 * MODES, SEG, LANES), F32),
+            pltpu.VMEM((T, LANES), F32),
+            pltpu.SemaphoreType.DMA((2, chunks)),
+        ],
         words * 40,
         words * 16,
         "finish",
-    )(
-        incoming,
-        own_head,
-        own_main,
-        enter_head,
-        enter_main,
-        reach_head,
-        reach_main,
-        query2,
-        border,
-        second_t,
-        rate_t,
-        gain,
-    )
+    )(incoming, in_hbm(early), in_hbm(late), border, second_t, rate_t, gain)
     total = lax.psum(squares, "chan")
     return call(
         functools.partial(scale_kernel, float(channels * lax.axis_size("chan"))),

time: 102 us -> 103 us (level)
  blocking collectives: 22.4 us -> 46.3 us
  starting transfers between devices: 25.3 us -> 8.04 us
  waiting for transfers between devices: 14.4 us -> 0.01 us
  local copies, waits for them, and re-layouts: 9.71 us -> 17.1 us
    all_to_all x1 -> x2, blocking collectives: 16.1 us -> 40.3 us  [exchange(): lax.all_to_all(rows.reshape(count, 1, lanes), 'seq', split_axis=0, concat...]
    all_to_all x1 -> x0, starting transfers between devices: 17.3 us -> none  [exchange(): lax.all_to_all(rows.reshape(count, 1, lanes), 'seq', split_axis=0, concat...]
    all_to_all x1 -> x0, waiting for transfers between devices: 10.5 us -> none  [exchange(): lax.all_to_all(rows.reshape(count, 1, lanes), 'seq', split_axis=0, concat...]
    unnamed x42 -> x40, local copies, waits for them, and re-layouts: 9.71 us -> 17.1 us
    ppermute x2, waiting for transfers between devices: 3.83 us -> 0.01 us  [from_behind(): return lax.ppermute(block, 'seq', [(i, i + 1) for i in range(count - 1)])]
  transfers between devices with their start and end apart: 3 -> 2, of which waited for: 2 -> 0; matrix products, arithmetic and copies ran while one was open for 0% -> 1% of each run, Pallas kernels for 17% -> 16%
where the time goes in v2:
time: 103 us; the launch traced here: 102 us
  blocking collectives  46.3 us (45%)
  Pallas kernels  29.5 us (29%)
  local copies, waits for them, and re-layouts  17.1 us (17%)
  starting transfers between devices  8.04 us (8%)
    all_to_all x2, blocking collectives, exchange(): lax.all_to_all(rows.reshape(count, 1, lanes), 'seq', split_axis=0, concat...  40.3 us
    unnamed x40, local copies, waits for them, and re-layouts  17.1 us
    pallas_call x1, Pallas kernels, local(): call(local_kernel, [pl.BlockSpec(memory_space=pltpu.SMEM)] + [held] * 14,...  10.3 us
    ppermute x2, starting transfers between devices, from_behind(): return lax.ppermute(block, 'seq', [(i, i + 1) for i in range(count - 1)])  8.04 us
    pallas_call x1, Pallas kernels, local(): call(prep_kernel, [outside] * 6 + [held], [held] * 7, [struct(tiles, T, L...  6.04 us
    psum x1, blocking collectives, local(): total = lax.psum(squares, 'chan')  5.93 us
    pallas_call x1, Pallas kernels, local(): call(join_kernel, [held] * 19, [held, outside], [struct(tiles, MODES, LAN...  4.86 us
    pallas_call x1, Pallas kernels, local(): call(tail_kernel, [outside] * 3, held, struct(tiles, TAPS, LANES), [pltpu...  3.49 us
  transfers between devices with their start and end apart: 2, of which 0 were waited for; matrix products, arithmetic and copies ran while one was open for 1% of the time, Pallas kernels for 16%

profile of v2, /device:TPU:1, one launch (start us, length us, event | category | flops | bytes accessed | tf_op | source)
XLA Modules:
  0.0 102.2 jit_solution(10942627075250219007)
XLA Ops:
  0.0 0.0 copy-start.2
  0.0 3.5 %tail.1 = f32[16,128,128]{2,1,0:T(8,128)} custom-call(f32[2048,256]{1,0:T(8,128)} %key_hbm.3, f32[2048,256]{1,0:T(8,128)} %value_hbm.3, f32[3,3,2048]{2,1,0:T(4,128)} %bitcast.17), custom_call_target="tpu_custom_call" | custom-call | flops 4194304 | bytes 3145728 | tf_op jit(solution)/shard_map/tail/pallas_call | solution.py:710
  3.5 0.0 copy-start.3
  3.5 0.0 copy-start.4
  3.5 0.0 copy-start.7
  3.5 4.6 %collective-permute-start = (f32[16,128,128]{2,1,0:T(8,128)}, f32[16,128,128]{2,1,0:T(8,128)S(1)}, u32[]{:S(2)}, u32[]{:S(2)}) collective-permute-start(f32[16,128,128]{2,1,0:T(8,128)} %tail.1), channel_id=1, source_target_pairs={{0,2},{2,4},{4,6},{6,8},{8,10},{10,12},{12,14},{14,16},{16,18},{18... | collective-permute-start | bytes 3145736 | tf_op jit(solution)/shard_map/ppermute | solution.py:643
  8.1 0.0 copy-done.2
  8.1 6.0 %prep.1 = (f32[16,256,128]{2,1,0:T(8,128)S(1)}, f32[16,256,128]{2,1,0:T(8,128)S(1)}, f32[16,256,128]{2,1,0:T(8,128)S(1)}, f32[16,256,128]{2,1,0:T(8,128)S(1)}, f...) custom-call(f32[2048,256]{1,0:T(8,128)} %key_hbm.3, f32[2048,256]{1,0:T(8,128)} %value_hbm.3, ...), custom_call_target="tpu_custom_call" | custom-call | flops 10485760 | bytes 20971520 | tf_op jit(solution)/shard_map/prep/pallas_call | solution.py:725
  14.2 0.0 copy-start
  14.2 1.3 %copy-done = f32[16,256,128]{2,1,0:T(8,128)} copy-done((f32[16,256,128]{2,1,0:T(8,128)}, f32[16,256,128]{2,1,0:T(8,128)S(1)}, u32[]{:S(2)}) %copy-start) | copy-done | bytes 2097176
  15.5 0.0 copy-start.9
  15.5 1.3 %copy-done.9 = f32[16,256,128]{2,1,0:T(8,128)} copy-done((f32[16,256,128]{2,1,0:T(8,128)}, f32[16,256,128]{2,1,0:T(8,128)S(1)}, u32[]{:S(2)}) %copy-start.9) | copy-done | bytes 2097176
  16.8 0.0 copy-start.11
  16.8 1.3 %copy-done.11 = f32[16,256,128]{2,1,0:T(8,128)} copy-done((f32[16,256,128]{2,1,0:T(8,128)}, f32[16,256,128]{2,1,0:T(8,128)S(1)}, u32[]{:S(2)}) %copy-start.11) | copy-done | bytes 2097176
  18.1 0.0 copy-start.13
  18.1 1.3 %copy-done.13 = f32[16,256,128]{2,1,0:T(8,128)} copy-done((f32[16,256,128]{2,1,0:T(8,128)}, f32[16,256,128]{2,1,0:T(8,128)S(1)}, u32[]{:S(2)}) %copy-start.13) | copy-done | bytes 2097176
  19.5 0.0 copy-start.15
  19.5 1.0 copy-done.15
  20.4 3.5 %collective-permute-start.1 = (f32[16,16,128]{2,1,0:T(8,128)}, f32[16,16,128]{2,1,0:T(8,128)S(1)}, u32[]{:S(2)}, u32[]{:S(2)}) collective-permute-start(f32[16,16,128]{2,1,0:T(8,128)} %get-tuple-element.26), channel_id=1, source_target_pairs={{0,2},{2,4},{4,6},{6,8},{8,10},{10,12},{12,14},{14,16},{16,18},{18... | collective-permute-start | bytes 393224 | tf_op jit(solution)/shard_map/ppermute | solution.py:643
  23.9 0.0 copy-done.3
  23.9 0.9 bitcast_multiply_fusion.amplitude_ref
  24.8 0.0 copy-done.4
  24.8 0.0 copy-done.7
  24.9 0.0 copy-start.1
  24.9 1.6 %copy-done.1 = f32[16,256,128]{2,1,0:T(8,128)S(1)} copy-done((f32[16,256,128]{2,1,0:T(8,128)S(1)}, f32[16,256,128]{2,1,0:T(8,128)}, u32[]{:S(2)}) %copy-start.1) | copy-done | bytes 2097176
  26.4 0.0 copy-start.10
  26.4 1.6 %copy-done.10 = f32[16,256,128]{2,1,0:T(8,128)S(1)} copy-done((f32[16,256,128]{2,1,0:T(8,128)S(1)}, f32[16,256,128]{2,1,0:T(8,128)}, u32[]{:S(2)}) %copy-start.10) | copy-done | bytes 2097176
  28.0 0.0 copy-start.12
  28.0 1.6 %copy-done.12 = f32[16,256,128]{2,1,0:T(8,128)S(1)} copy-done((f32[16,256,128]{2,1,0:T(8,128)S(1)}, f32[16,256,128]{2,1,0:T(8,128)}, u32[]{:S(2)}) %copy-start.12) | copy-done | bytes 2097176
  29.6 0.0 copy-start.14
  29.6 1.6 %copy-done.14 = f32[16,256,128]{2,1,0:T(8,128)S(1)} copy-done((f32[16,256,128]{2,1,0:T(8,128)S(1)}, f32[16,256,128]{2,1,0:T(8,128)}, u32[]{:S(2)}) %copy-start.14) | copy-done | bytes 2097176
  31.2 0.0 copy-start.16
  31.2 1.2 %copy-done.16 = f32[16,136,128]{2,1,0:T(8,128)S(1)} copy-done((f32[16,136,128]{2,1,0:T(8,128)S(1)}, f32[16,136,128]{2,1,0:T(8,128)}, u32[]{:S(2)}) %copy-start.16) | copy-done | bytes 1114136
  32.5 0.0 copy-start.17
  32.5 1.1 %copy-done.17 = bf16[512,768]{1,0:T(8,128)(2,1)S(1)} copy-done((bf16[512,768]{1,0:T(8,128)(2,1)S(1)}, bf16[512,768]{1,0:T(8,128)(2,1)}, u32[]{:S(2)}) %copy-start.17) | copy-done | bytes 786456
  33.6 0.0 copy-start.18
  33.6 1.1 %copy-done.18 = bf16[256,1536]{1,0:T(8,128)(2,1)S(1)} copy-done((bf16[256,1536]{1,0:T(8,128)(2,1)S(1)}, bf16[256,1536]{1,0:T(8,128)(2,1)}, u32[]{:S(2)}) %copy-start.18) | copy-done | bytes 786456
  34.7 0.0 copy-start.19
  34.7 1.0 copy-done.19
  35.7 0.0 copy-start.5
  35.7 0.0 copy-start.6
  35.7 10.3 %local.1 = (f32[16,136,128]{2,1,0:T(8,128)S(1)}, f32[16,384,128]{2,1,0:T(8,128)S(1)}, f32[16,136,128]{2,1,0:T(8,128)S(1)}, f32[16,136,128]{2,1,0:T(8,128)S(1)}, ...) custom-call(s32[1]{0:T(128)} %bitcast.1.place_ref, ...), custom_call_target="tpu_custom_call" | custom-call | flops 4194304000 | bytes 31457280 | tf_op jit(solution)/shard_map/local/pallas_call | solution.py:751
  46.0 0.0 collective-permute-done.1.rims_ref
  46.0 0.0 collective-permute-done.halo_ref
  46.0 0.0 copy-done.5
  46.0 0.0 copy-done.6
  46.0 0.0 copy-start.8
  46.1 4.9 %join.1 = (f32[16,8,128]{2,1,0:T(8,128)S(1)}, f32[16,264,128]{2,1,0:T(8,128)}) custom-call(f32[16,128,128]{2,1,0:T(8,128)S(1)} %collective-permute-done.halo_ref, f32[16,16,128]{2,1,0:T(8,128)S(1)} %collective-permute-done.1.rims_ref, f32[16,384,128]{2,1,0:T(8,128)S(1)} %get-tuple-element.33.spectrum_ref, f32[16,136,128]{2,1,0:T(8,128)S(1)} %get-tuple-element.34.medium_ref, ...), custom_call_target="tpu_custom_call" | custom-call | flops 1048576000 | bytes 10485760 | tf_op jit(solution)/shard_map/join/pallas_call | solution.py:788
  50.9 24.1 %all_to_all.10 = f32[128,1,128]{2,1,0:T(1,128)S(1)} all-to-all(f32[128,1,128]{2,1,0:T(1,128)S(1)} %bitcast.30), channel_id=1, replica_groups=mesh['seq'=128,'chan'=2] {'seq'}, dimensions={0} | all-to-all | bytes 131072 | tf_op jit(solution)/shard_map/all_to_all | solution.py:665
  75.0 0.1 scan.1
  75.1 16.3 %all_to_all.11 = f32[128,1,128]{2,1,0:T(1,128)S(1)} all-to-all(f32[128,1,128]{2,1,0:T(1,128)S(1)} %bitcast.29), channel_id=1, replica_groups=mesh['seq'=128,'chan'=2] {'seq'}, dimensions={0} | all-to-all | bytes 131072 | tf_op jit(solution)/shard_map/all_to_all | solution.py:665
  91.3 0.0 copy-done.8
  91.3 3.2 %finish.1 = (f32[16,256,128]{2,1,0:T(8,128)S(1)}, f32[1,256]{1,0:T(1,128)S(1)}) custom-call(f32[16,8,128]{2,1,0:T(8,128)S(1)} %bitcast.27, f32[16,376,128]{2,1,0:T(8,128)} %get-tuple-element.43.early_hbm, f32[16,264,128]{2,1,0:T(8,128)} %get-tuple-element.44.late_hbm, f32[16,16,128]{2,1,0:T(8,128)S(1)} %collective-permute-done.1.rims_ref, ...), custom_call_target="tpu_custom_call" | custom-call | flops 20971520 | bytes 8388608 | tf_op jit(solution)/shard_map/finish/pallas_call | solution.py:835
  94.6 5.9 %psum.7.squares_ref = f32[1,256]{1,0:T(1,128)S(1)} all-reduce(f32[1,256]{1,0:T(1,128)S(1)} %get-tuple-element.46), channel_id=1, replica_groups=mesh['seq'=128,'chan'=2] {'chan'}, use_global_device_ids=true, to_apply=%region_0.0 | all-reduce | flops 256 | bytes 2048 | tf_op jit(solution)/shard_map/psum | solution.py:851
  100.5 1.5 %scale.1 = f32[2048,256]{1,0:T(8,128)} custom-call(f32[16,256,128]{2,1,0:T(8,128)S(1)} %get-tuple-element.45.mixed_ref, f32[1,256]{1,0:T(1,128)S(1)} %psum.7.squares_ref), custom_call_target="tpu_custom_call" | custom-call | flops 524288 | bytes 4194304 | tf_op jit(solution)/shard_map/scale/pallas_call | solution.py:852
Async XLA Ops:
  0.0 8.1 %copy-start.2 = (f32[3,2048,3]{1,2,0:T(4,128)S(1)}, f32[3,2048,3]{1,2,0:T(4,128)}, u32[]{:S(2)}) copy-start(f32[3,2048,3]{1,2,0:T(4,128)} %param.22) | copy-start | bytes 221188
  3.5 20.4 %copy-start.3 = (f32[2048,8]{0,1:T(8,128)S(1)}, f32[2048,8]{0,1:T(8,128)}, u32[]{:S(2)}) copy-start(f32[2048,8]{0,1:T(8,128)} %param.25) | copy-start | bytes 196612
  3.5 21.3 %copy-start.4 = (f32[3,2048,3]{1,2,0:T(4,128)S(1)}, f32[3,2048,3]{1,2,0:T(4,128)}, u32[]{:S(2)}) copy-start(f32[3,2048,3]{1,2,0:T(4,128)} %param.23) | copy-start | bytes 221188
  3.5 21.3 %copy-start.7 = (f32[2048]{0:T(1024)S(1)}, f32[2048]{0:T(1024)}, u32[]{:S(2)}) copy-start(f32[2048]{0:T(1024)} %param.27) | copy-start | bytes 24580
  3.5 42.5 %collective-permute-start = (f32[16,128,128]{2,1,0:T(8,128)}, f32[16,128,128]{2,1,0:T(8,128)S(1)}, u32[]{:S(2)}, u32[]{:S(2)}) collective-permute-start(f32[16,128,128]{2,1,0:T(8,128)} %tail.1), channel_id=1, source_target_pairs={{0,2},{2,4},{4,6},{6,8},{8,10},{10,12},{12,14},{14,16},{16,18},{18... | collective-permute-start | bytes 3145736 | tf_op jit(solution)/shard_map/ppermute | solution.py:643
  14.2 1.3 %copy-start = (f32[16,256,128]{2,1,0:T(8,128)}, f32[16,256,128]{2,1,0:T(8,128)S(1)}, u32[]{:S(2)}) copy-start(f32[16,256,128]{2,1,0:T(8,128)S(1)} %get-tuple-element.28.value_t) | copy-start | bytes 6291460
  15.5 1.3 %copy-start.9 = (f32[16,256,128]{2,1,0:T(8,128)}, f32[16,256,128]{2,1,0:T(8,128)S(1)}, u32[]{:S(2)}) copy-start(f32[16,256,128]{2,1,0:T(8,128)S(1)} %get-tuple-element.29.query_t) | copy-start | bytes 6291460
  16.8 1.3 %copy-start.11 = (f32[16,256,128]{2,1,0:T(8,128)}, f32[16,256,128]{2,1,0:T(8,128)S(1)}, u32[]{:S(2)}) copy-start(f32[16,256,128]{2,1,0:T(8,128)S(1)} %get-tuple-element.30.query2_t) | copy-start | bytes 6291460
  18.1 1.3 %copy-start.13 = (f32[16,256,128]{2,1,0:T(8,128)}, f32[16,256,128]{2,1,0:T(8,128)S(1)}, u32[]{:S(2)}) copy-start(f32[16,256,128]{2,1,0:T(8,128)S(1)} %get-tuple-element.31.key2_t) | copy-start | bytes 6291460
  19.5 1.0 copy-start.15
  20.4 25.6 %collective-permute-start.1 = (f32[16,16,128]{2,1,0:T(8,128)}, f32[16,16,128]{2,1,0:T(8,128)S(1)}, u32[]{:S(2)}, u32[]{:S(2)}) collective-permute-start(f32[16,16,128]{2,1,0:T(8,128)} %get-tuple-element.26), channel_id=1, source_target_pairs={{0,2},{2,4},{4,6},{6,8},{8,10},{10,12},{12,14},{14,16},{16,18},{18... | collective-permute-start | bytes 393224 | tf_op jit(solution)/shard_map/ppermute | solution.py:643
  24.9 1.6 %copy-start.1 = (f32[16,256,128]{2,1,0:T(8,128)S(1)}, f32[16,256,128]{2,1,0:T(8,128)}, u32[]{:S(2)}) copy-start(f32[16,256,128]{2,1,0:T(8,128)} %copy-done) | copy-start | bytes 6291460
  26.4 1.6 %copy-start.10 = (f32[16,256,128]{2,1,0:T(8,128)S(1)}, f32[16,256,128]{2,1,0:T(8,128)}, u32[]{:S(2)}) copy-start(f32[16,256,128]{2,1,0:T(8,128)} %copy-done.9) | copy-start | bytes 6291460
  28.0 1.6 %copy-start.12 = (f32[16,256,128]{2,1,0:T(8,128)S(1)}, f32[16,256,128]{2,1,0:T(8,128)}, u32[]{:S(2)}) copy-start(f32[16,256,128]{2,1,0:T(8,128)} %copy-done.11) | copy-start | bytes 6291460
  29.6 1.6 %copy-start.14 = (f32[16,256,128]{2,1,0:T(8,128)S(1)}, f32[16,256,128]{2,1,0:T(8,128)}, u32[]{:S(2)}) copy-start(f32[16,256,128]{2,1,0:T(8,128)} %copy-done.13) | copy-start | bytes 6291460
  31.2 1.2 %copy-start.16 = (f32[16,136,128]{2,1,0:T(8,128)S(1)}, f32[16,136,128]{2,1,0:T(8,128)}, u32[]{:S(2)}) copy-start(f32[16,136,128]{2,1,0:T(8,128)} %copy-done.15) | copy-start | bytes 3342340
  32.5 1.1 %copy-start.17 = (bf16[512,768]{1,0:T(8,128)(2,1)S(1)}, bf16[512,768]{1,0:T(8,128)(2,1)}, u32[]{:S(2)}) copy-start(bf16[512,768]{1,0:T(8,128)(2,1)} %constant.18.clone.forward_ref) | copy-start | bytes 2359300
  33.6 1.1 %copy-start.18 = (bf16[256,1536]{1,0:T(8,128)(2,1)S(1)}, bf16[256,1536]{1,0:T(8,128)(2,1)}, u32[]{:S(2)}) copy-start(bf16[256,1536]{1,0:T(8,128)(2,1)} %constant.20.clone.inverse_ref) | copy-start | bytes 2359300
  34.7 1.0 copy-start.19
  35.7 10.3 %copy-start.5 = (bf16[144,768]{1,0:T(8,128)(2,1)S(1)}, bf16[144,768]{1,0:T(8,128)(2,1)}, u32[]{:S(2)}) copy-start(bf16[144,768]{1,0:T(8,128)(2,1)} %constant.22.clone.inverse_ref) | copy-start | bytes 663556
  35.7 10.3 %copy-start.6 = (bf16[256,384]{1,0:T(8,128)(2,1)S(1)}, bf16[256,384]{1,0:T(8,128)(2,1)}, u32[]{:S(2)}) copy-start(bf16[256,384]{1,0:T(8,128)(2,1)} %constant.21.clone.forward_ref) | copy-start | bytes 589828
  46.0 45.3 %copy-start.8 = (f32[2048]{0:T(1024)S(1)}, f32[2048]{0:T(1024)}, u32[]{:S(2)}) copy-start(f32[2048]{0:T(1024)} %param.28) | copy-start | bytes 24580

commit v3 on v2

--- a/solution.py
+++ b/solution.py
@@ -168,13 +168,31 @@
 
 
 def tail_kernel(
-    key_hbm, value_hbm, short_hbm, tail_ref, key_in, value_in, short_ref, key_sem, value_sem, short_sem
+    place_ref,
+    key_hbm,
+    value_hbm,
+    short_hbm,
+    rate_hbm,
+    tail_ref,
+    own_rate_out,
+    key_in,
+    value_in,
+    short_ref,
+    rates_in,
+    key_sem,
+    value_sem,
+    short_sem,
+    rate_sem,
 ):
     chunks = key_sem.shape[0]
     rows = key_hbm.shape[0] // chunks
     copies = []
     filters = pltpu.make_async_copy(short_hbm, short_ref, short_sem)
     filters.start()
+    index = place_ref[0]
+    mine = pl.ds(pl.multiple_of((index // MODES) * LANES, LANES), LANES)
+    rates = pltpu.make_async_copy(rate_hbm.at[:, mine], rates_in, rate_sem)
+    rates.start()
     for chunk in range(chunks):
         here = pl.ds(chunk * rows, rows)
         for source, target, sem in (
@@ -199,6 +217,9 @@
                 return taps[0] * here + taps[1] * down(here) + taps[2] * down(here, 2)
 
             tail_ref[tile] = feature(key_in, 1) * feature(value_in, 2)
+    rates.wait()
+    chosen = sublane(rates_in.shape) == lax.rem(index, MODES)
+    own_rate_out[...] = jnp.sum(jnp.where(chosen, rates_in[...], 0.0), axis=0, keepdims=True)
 
 
 def prep_kernel(
@@ -272,7 +293,6 @@
 
 
 def local_kernel(
-    place_ref,
     key_t,
     value_t,
     query_t,
@@ -295,7 +315,6 @@
     enter_out,
     leave_out,
     reach_main_out,
-    own_rate_out,
     late_hbm,
     gated_t,
     medium_t,
@@ -304,11 +323,6 @@
     late,
     late_sem,
 ):
-    index = place_ref[0]
-    mine = pl.ds(pl.multiple_of((index // MODES) * LANES, LANES), LANES)
-    rates = rate_ref[:, mine]
-    chosen = sublane(rates.shape) == lax.rem(index, MODES)
-    own_rate_out[...] = jnp.sum(jnp.where(chosen, rates, 0.0), axis=0, keepdims=True)
 
     tiles = key_t.shape[0]
     group = gated_t.shape[1] // LANES
@@ -707,19 +721,20 @@
     fields = [
         in_hbm(x) for x in (key_proj, value_proj, query_proj, second_query, second_key, medium_filter)
     ]
-    tail = call(
+    place = lax.axis_index("seq").astype(jnp.int32).reshape(1)
+    tail, own_rate = call(
         tail_kernel,
-        [outside] * 3,
-        held,
-        struct(tiles, TAPS, LANES),
+        [pl.BlockSpec(memory_space=pltpu.SMEM)] + [outside] * 4,
+        [held] * 2,
+        [struct(tiles, TAPS, LANES), struct(1, LANES)],
         [pltpu.VMEM((channels, LANES), F32)] * 2
-        + [pltpu.VMEM((3, 3, channels), F32)]
+        + [pltpu.VMEM((3, 3, channels), F32), pltpu.VMEM((MODES, LANES), F32)]
         + [pltpu.SemaphoreType.DMA((chunks,))] * 2
-        + [pltpu.SemaphoreType.DMA],
+        + [pltpu.SemaphoreType.DMA] * 2,
         words * 8,
         words * 6,
         "tail",
-    )(fields[0], fields[1], in_hbm(short_t))
+    )(place, fields[0], fields[1], in_hbm(short_t), in_hbm(rate_t))
     halo = from_behind(tail)
 
     *turned_fields, taps_t, rims = call(
@@ -736,7 +751,6 @@
     )(*fields, short_t)
     border = from_behind(rims)
 
-    place = lax.axis_index("seq").astype(jnp.int32).reshape(1)
     (
         taps,
         tap_spectrum,
@@ -746,12 +760,11 @@
         enter_main,
         leave_main,
         reach_main,
-        own_rate,
         early,
     ) = call(
         local_kernel,
-        [pl.BlockSpec(memory_space=pltpu.SMEM)] + [held] * 14,
-        [held] * 9 + [outside],
+        [held] * 14,
+        [held] * 8 + [outside],
         [
             struct(tiles, HEAD_ROWS, LANES),
             struct(tiles, 384, LANES),
@@ -761,7 +774,6 @@
             struct(tiles, MODES, SEG, LANES),
             struct(tiles, MODES, LANES),
             struct(tiles, MODES, SEG, LANES),
-            struct(1, LANES),
             hbm(tiles, T + MAIN_ROWS, LANES),
         ],
         [pltpu.VMEM((T, group * LANES), F32)] * 2
@@ -771,7 +783,6 @@
         words * 60,
         "local",
     )(
-        place,
         *turned_fields,
         taps_t,
         short_t,

time: 103 us -> 91.9 us (0.89)
  local copies, waits for them, and re-layouts: 17.1 us -> 0.07 us
  waiting for transfers between devices: 0.01 us -> 5.32 us
  blocking collectives: 46.3 us -> 50.2 us
  Pallas kernels: 29.5 us -> 27.7 us
    unnamed x40 -> x22, local copies, waits for them, and re-layouts: 17.1 us -> 0.07 us
    ppermute x2, waiting for transfers between devices: 0.01 us -> 5.32 us  [from_behind(): return lax.ppermute(block, 'seq', [(i, i + 1) for i in range(count - 1)])]
    all_to_all x2, blocking collectives: 40.3 us -> 43.9 us  [exchange(): lax.all_to_all(rows.reshape(count, 1, lanes), 'seq', split_axis=0, concat...]
    pallas_call x2, Pallas kernels: 13.8 us -> 12.6 us  [the longest x1 10.2 us: local(): call(local_kernel, [held] * 14, [held] * 8 + [outside], [struct(tiles, HE...]
  transfers between devices with their start and end apart: 2 -> 2, of which waited for: 0 -> 1; matrix products, arithmetic and copies ran while one was open for 1% -> 0% of each run, Pallas kernels for 16% -> 17%
where the time goes in v3:
time: 91.9 us; the launch traced here: 91.7 us
  blocking collectives  50.2 us (55%)
  Pallas kernels  27.7 us (30%)
  starting transfers between devices  8.06 us (9%)
  waiting for transfers between devices  5.32 us (6%)
    all_to_all x2, blocking collectives, exchange(): lax.all_to_all(rows.reshape(count, 1, lanes), 'seq', split_axis=0, concat...  43.9 us
    pallas_call x1, Pallas kernels, local(): call(local_kernel, [held] * 14, [held] * 8 + [outside], [struct(tiles, HE...  10.2 us
    ppermute x2, starting transfers between devices, from_behind(): return lax.ppermute(block, 'seq', [(i, i + 1) for i in range(count - 1)])  8.06 us
    psum x1, blocking collectives, local(): total = lax.psum(squares, 'chan')  6.25 us
    pallas_call x1, Pallas kernels, local(): call(prep_kernel, [outside] * 6 + [held], [held] * 7, [struct(tiles, T, L...  5.39 us
    ppermute x2, waiting for transfers between devices, from_behind(): return lax.ppermute(block, 'seq', [(i, i + 1) for i in range(count - 1)])  5.32 us
    pallas_call x1, Pallas kernels, local(): call(join_kernel, [held] * 19, [held, outside], [struct(tiles, MODES, LAN...  4.83 us
    pallas_call x1, Pallas kernels, local(): call(finish_kernel, [held, outside, outside] + [held] * 4, [held] * 2, [s...  3.23 us
  transfers between devices with their start and end apart: 2, of which 1 were waited for; matrix products, arithmetic and copies ran while one was open for 0% of the time, Pallas kernels for 17%

profile of v3, /device:TPU:1, one launch (start us, length us, event | category | flops | bytes accessed | tf_op | source)
XLA Modules:
  0.0 91.7 jit_solution(2089880691412129461)
XLA Ops:
  0.0 0.0 copy-start.1
  0.0 2.4 %tail.1 = (f32[16,128,128]{2,1,0:T(8,128)S(1)}, f32[1,128]{1,0:T(1,128)S(1)}) custom-call(s32[1]{0:T(128)} %bitcast.place_ref, f32[2048,256]{1,0:T(8,128)} %key_hbm.3, f32[2048,256]{1,0:T(8,128)} %value_hbm.3, f32[3,3,2048]{2,1,0:T(4,128)} %bitcast.21, f32[8,2048]{1,0:T(8,128)} %bitcast.17), custom_call_target="tpu_custom_call" | custom-call | flops 4194304 | bytes 3145728 | tf_op jit(solution)/shard_map/tail/pallas_call | solution.py:725
  2.5 0.0 copy-start
  2.5 0.0 copy-start.10
  2.5 0.0 copy-start.2
  2.5 0.0 copy-start.5
  2.5 0.0 copy-start.7
  2.5 0.0 copy-start.8
  2.5 0.0 copy-start.9
  2.5 4.6 %collective-permute-start = (f32[16,128,128]{2,1,0:T(8,128)S(1)}, f32[16,128,128]{2,1,0:T(8,128)S(1)}, u32[]{:S(2)}, u32[]{:S(2)}) collective-permute-start(f32[16,128,128]{2,1,0:T(8,128)S(1)} %get-tuple-element.27), channel_id=1, source_target_pairs={{0,2},{2,4},{4,6},{6,8},{8,10},{10,12},{12,14},{14,16},{16,18},{18... | collective-permute-start | bytes 3145736 | tf_op jit(solution)/shard_map/ppermute | solution.py:657
  7.1 0.0 copy-done.1
  7.1 5.4 %prep.1 = (f32[16,256,128]{2,1,0:T(8,128)S(1)}, f32[16,256,128]{2,1,0:T(8,128)S(1)}, f32[16,256,128]{2,1,0:T(8,128)S(1)}, f32[16,256,128]{2,1,0:T(8,128)S(1)}, f...) custom-call(f32[2048,256]{1,0:T(8,128)} %key_hbm.3, f32[2048,256]{1,0:T(8,128)} %value_hbm.3, ...), custom_call_target="tpu_custom_call" | custom-call | flops 10485760 | bytes 20971520 | tf_op jit(solution)/shard_map/prep/pallas_call | solution.py:740
  12.5 3.5 %collective-permute-start.1 = (f32[16,16,128]{2,1,0:T(8,128)S(1)}, f32[16,16,128]{2,1,0:T(8,128)S(1)}, u32[]{:S(2)}, u32[]{:S(2)}) collective-permute-start(f32[16,16,128]{2,1,0:T(8,128)S(1)} %get-tuple-element.28), channel_id=1, source_target_pairs={{0,2},{2,4},{4,6},{6,8},{8,10},{10,12},{12,14},{14,16},{16,18},{18... | collective-permute-start | bytes 393224 | tf_op jit(solution)/shard_map/ppermute | solution.py:657
  16.0 0.0 copy-done
  16.0 0.0 copy-done.10
  16.1 0.0 copy-done.2
  16.1 0.0 copy-done.5
  16.1 0.0 copy-done.7
  16.1 0.0 copy-done.8
  16.1 0.0 copy-done.9
  16.1 0.0 copy-start.3
  16.2 0.0 copy-start.4
  16.2 10.2 %local.1 = (f32[16,136,128]{2,1,0:T(8,128)S(1)}, f32[16,384,128]{2,1,0:T(8,128)S(1)}, f32[16,136,128]{2,1,0:T(8,128)S(1)}, f32[16,136,128]{2,1,0:T(8,128)S(1)}, ...) custom-call(f32[16,256,128]{2,1,0:T(8,128)S(1)} %get-tuple-element.2, ...), custom_call_target="tpu_custom_call" | custom-call | flops 4194304000 | bytes 31457280 | tf_op jit(solution)/shard_map/local/pallas_call | solution.py:764
  26.4 5.3 %collective-permute-done.1.rims_ref = f32[16,16,128]{2,1,0:T(8,128)S(1)} collective-permute-done((f32[16,16,128]{2,1,0:T(8,128)S(1)}, f32[16,16,128]{2,1,0:T(8,128)S(1)}, u32[]{:S(2)}, u32[]{:S(2)}) %collective-permute-start.1) | collective-permute-done | bytes 131104 | tf_op jit(solution)/shard_map/ppermute | solution.py:657
  31.7 0.0 collective-permute-done.halo_ref
  31.7 0.0 copy-done.3
  31.7 0.0 copy-done.4
  31.7 0.0 copy-start.6
  31.7 4.8 %join.1 = (f32[16,8,128]{2,1,0:T(8,128)S(1)}, f32[16,264,128]{2,1,0:T(8,128)}) custom-call(f32[16,128,128]{2,1,0:T(8,128)S(1)} %collective-permute-done.halo_ref, f32[16,16,128]{2,1,0:T(8,128)S(1)} %collective-permute-done.1.rims_ref, f32[16,384,128]{2,1,0:T(8,128)S(1)} %get-tuple-element.35.spectrum_ref, f32[16,136,128]{2,1,0:T(8,128)S(1)} %get-tuple-element.36.medium_ref, ...), custom_call_target="tpu_custom_call" | custom-call | flops 1048576000 | bytes 10485760 | tf_op jit(solution)/shard_map/join/pallas_call | solution.py:799
  36.5 27.6 %all_to_all.10 = f32[128,1,128]{2,1,0:T(1,128)S(1)} all-to-all(f32[128,1,128]{2,1,0:T(1,128)S(1)} %bitcast.31), channel_id=1, replica_groups=mesh['seq'=128,'chan'=2] {'seq'}, dimensions={0} | all-to-all | bytes 131072 | tf_op jit(solution)/shard_map/all_to_all | solution.py:679
  64.2 0.1 scan.1
  64.2 16.3 %all_to_all.11 = f32[128,1,128]{2,1,0:T(1,128)S(1)} all-to-all(f32[128,1,128]{2,1,0:T(1,128)S(1)} %bitcast.30), channel_id=1, replica_groups=mesh['seq'=128,'chan'=2] {'seq'}, dimensions={0} | all-to-all | bytes 131072 | tf_op jit(solution)/shard_map/all_to_all | solution.py:679
  80.5 0.0 copy-done.6
  80.5 3.2 %finish.1 = (f32[16,256,128]{2,1,0:T(8,128)S(1)}, f32[1,256]{1,0:T(1,128)S(1)}) custom-call(f32[16,8,128]{2,1,0:T(8,128)S(1)} %bitcast.28, f32[16,376,128]{2,1,0:T(8,128)} %get-tuple-element.45.early_hbm, f32[16,264,128]{2,1,0:T(8,128)} %get-tuple-element.46.late_hbm, f32[16,16,128]{2,1,0:T(8,128)S(1)} %collective-permute-done.1.rims_ref, ...), custom_call_target="tpu_custom_call" | custom-call | flops 20971520 | bytes 8388608 | tf_op jit(solution)/shard_map/finish/pallas_call | solution.py:846
  83.7 6.3 %psum.7.squares_ref = f32[1,256]{1,0:T(1,128)S(1)} all-reduce(f32[1,256]{1,0:T(1,128)S(1)} %get-tuple-element.48), channel_id=1, replica_groups=mesh['seq'=128,'chan'=2] {'chan'}, use_global_device_ids=true, to_apply=%region_0.0 | all-reduce | flops 256 | bytes 2048 | tf_op jit(solution)/shard_map/psum | solution.py:862
  90.0 1.5 %scale.1 = f32[2048,256]{1,0:T(8,128)} custom-call(f32[16,256,128]{2,1,0:T(8,128)S(1)} %get-tuple-element.47.mixed_ref, f32[1,256]{1,0:T(1,128)S(1)} %psum.7.squares_ref), custom_call_target="tpu_custom_call" | custom-call | flops 524288 | bytes 4194304 | tf_op jit(solution)/shard_map/scale/pallas_call | solution.py:863
  (1 shorter events, 0.0 us)
Async XLA Ops:
  0.0 7.1 %copy-start.1 = (f32[3,2048,3]{1,2,0:T(4,128)S(1)}, f32[3,2048,3]{1,2,0:T(4,128)}, u32[]{:S(2)}) copy-start(f32[3,2048,3]{1,2,0:T(4,128)} %param.22) | copy-start | bytes 221188
  2.5 13.6 %copy-start = (f32[2048,8]{0,1:T(8,128)S(1)}, f32[2048,8]{0,1:T(8,128)}, u32[]{:S(2)}) copy-start(f32[2048,8]{0,1:T(8,128)} %param.25) | copy-start | bytes 196612
  2.5 13.6 %copy-start.10 = (f32[2048,8]{0,1:T(8,128)S(1)}, f32[2048,8]{0,1:T(8,128)}, u32[]{:S(2)}) copy-start(f32[2048,8]{0,1:T(8,128)} %param.26) | copy-start | bytes 196612
  2.5 13.6 %copy-start.2 = (f32[3,2048,3]{1,2,0:T(4,128)S(1)}, f32[3,2048,3]{1,2,0:T(4,128)}, u32[]{:S(2)}) copy-start(f32[3,2048,3]{1,2,0:T(4,128)} %param.23) | copy-start | bytes 221188
  2.5 13.6 %copy-start.5 = (f32[2048]{0:T(1024)S(1)}, f32[2048]{0:T(1024)}, u32[]{:S(2)}) copy-start(f32[2048]{0:T(1024)} %param.27) | copy-start | bytes 24580
  2.5 13.6 %copy-start.7 = (bf16[512,768]{1,0:T(8,128)(2,1)S(1)}, bf16[512,768]{1,0:T(8,128)(2,1)}, u32[]{:S(2)}) copy-start(bf16[512,768]{1,0:T(8,128)(2,1)} %constant.18.clone.forward_ref) | copy-start | bytes 2359300
  2.5 13.6 %copy-start.8 = (bf16[256,1536]{1,0:T(8,128)(2,1)S(1)}, bf16[256,1536]{1,0:T(8,128)(2,1)}, u32[]{:S(2)}) copy-start(bf16[256,1536]{1,0:T(8,128)(2,1)} %constant.20.clone.inverse_ref) | copy-start | bytes 2359300
  2.5 13.6 %copy-start.9 = (bf16[384,384]{1,0:T(8,128)(2,1)S(1)}, bf16[384,384]{1,0:T(8,128)(2,1)}, u32[]{:S(2)}) copy-start(bf16[384,384]{1,0:T(8,128)(2,1)} %constant.19.clone.spectrum_ref) | copy-start | bytes 884740
  2.5 29.1 %collective-permute-start = (f32[16,128,128]{2,1,0:T(8,128)S(1)}, f32[16,128,128]{2,1,0:T(8,128)S(1)}, u32[]{:S(2)}, u32[]{:S(2)}) collective-permute-start(f32[16,128,128]{2,1,0:T(8,128)S(1)} %get-tuple-element.27), channel_id=1, source_target_pairs={{0,2},{2,4},{4,6},{6,8},{8,10},{10,12},{12,14},{14,16},{16,18},{18... | collective-permute-start | bytes 3145736 | tf_op jit(solution)/shard_map/ppermute | solution.py:657
  12.5 19.1 %collective-permute-start.1 = (f32[16,16,128]{2,1,0:T(8,128)S(1)}, f32[16,16,128]{2,1,0:T(8,128)S(1)}, u32[]{:S(2)}, u32[]{:S(2)}) collective-permute-start(f32[16,16,128]{2,1,0:T(8,128)S(1)} %get-tuple-element.28), channel_id=1, source_target_pairs={{0,2},{2,4},{4,6},{6,8},{8,10},{10,12},{12,14},{14,16},{16,18},{18... | collective-permute-start | bytes 393224 | tf_op jit(solution)/shard_map/ppermute | solution.py:657
  16.1 15.5 %copy-start.3 = (bf16[144,768]{1,0:T(8,128)(2,1)S(1)}, bf16[144,768]{1,0:T(8,128)(2,1)}, u32[]{:S(2)}) copy-start(bf16[144,768]{1,0:T(8,128)(2,1)} %constant.22.clone.inverse_ref) | copy-start | bytes 663556
  16.2 15.5 %copy-start.4 = (bf16[256,384]{1,0:T(8,128)(2,1)S(1)}, bf16[256,384]{1,0:T(8,128)(2,1)}, u32[]{:S(2)}) copy-start(bf16[256,384]{1,0:T(8,128)(2,1)} %constant.21.clone.forward_ref) | copy-start | bytes 589828
  31.7 48.8 %copy-start.6 = (f32[2048]{0:T(1024)S(1)}, f32[2048]{0:T(1024)}, u32[]{:S(2)}) copy-start(f32[2048]{0:T(1024)} %param.28) | copy-start | bytes 24580

commit v4 on v3

--- a/solution.py
+++ b/solution.py
@@ -21,6 +21,7 @@
 HEAD_ROWS = HEAD * SEG
 MAIN_ROWS = MAIN * SEG
 RIMS = 16
+RING = 8
 LIMIT = 24 * 1024 * 1024
 
 F32 = jnp.float32
@@ -190,9 +191,14 @@
     filters = pltpu.make_async_copy(short_hbm, short_ref, short_sem)
     filters.start()
     index = place_ref[0]
-    mine = pl.ds(pl.multiple_of((index // MODES) * LANES, LANES), LANES)
-    rates = pltpu.make_async_copy(rate_hbm.at[:, mine], rates_in, rate_sem)
-    rates.start()
+    share = rates_in.shape[0]
+    first = lax.rem(index, RING) * (share * LANES)
+    rates = []
+    for part in range(share):
+        mine = pl.ds(pl.multiple_of(first + part * LANES, LANES), LANES)
+        copy = pltpu.make_async_copy(rate_hbm.at[:, mine], rates_in.at[part], rate_sem.at[part])
+        copy.start()
+        rates.append(copy)
     for chunk in range(chunks):
         here = pl.ds(chunk * rows, rows)
         for source, target, sem in (
@@ -217,9 +223,9 @@
                 return taps[0] * here + taps[1] * down(here) + taps[2] * down(here, 2)
 
             tail_ref[tile] = feature(key_in, 1) * feature(value_in, 2)
-    rates.wait()
-    chosen = sublane(rates_in.shape) == lax.rem(index, MODES)
-    own_rate_out[...] = jnp.sum(jnp.where(chosen, rates_in[...], 0.0), axis=0, keepdims=True)
+    for copy in rates:
+        copy.wait()
+    own_rate_out[...] = rates_in[...]
 
 
 def prep_kernel(
@@ -537,17 +543,32 @@
         pltpu.make_async_copy(late.at[tile], late_hbm.at[tile], late_sem.at[tile]).wait()
 
 
-def scan_kernel(state_ref, rate_ref, out_ref):
-    blocks = state_ref.shape[0]
-    position = sublane(state_ref.shape)
-    rate = rate_ref[...]
-    total = state_ref[...]
-    distance = 1
-    while distance < blocks:
-        moved = jnp.where(position >= distance, down(total, distance), 0.0)
-        total = total + jnp.exp(-(float(T) * distance) * rate) * moved
-        distance *= 2
-    out_ref[...] = jnp.where(position >= 1, down(total), 0.0)
+def ring_kernel(states_hbm, rate_ref, out_ref, states, sem):
+    copy = pltpu.make_async_copy(states_hbm, states, sem)
+    copy.start()
+    decay = jnp.exp(-float(T) * rate_ref[...])
+    copy.wait()
+    total = states[0]
+    for k in range(1, states.shape[0]):
+        total = decay * total + states[k]
+    for k in range(out_ref.shape[0]):
+        out_ref[k] = total
+
+
+def scan_kernel(place_ref, states_hbm, rings_ref, rate_ref, out_ref, states, sem):
+    copy = pltpu.make_async_copy(states_hbm, states, sem)
+    copy.start()
+    ring = place_ref[0] // RING
+    rates = rate_ref[...]
+    decay = jnp.exp(-float(T) * rates)
+    around = jnp.exp(-float(T * RING) * rates)
+    entering = jnp.zeros_like(rates)
+    for k in range(rings_ref.shape[0] - 1):
+        entering = jnp.where(k < ring, around * entering + rings_ref[k], entering)
+    copy.wait()
+    for k in range(states.shape[0]):
+        out_ref[k] = entering
+        entering = decay * entering + states[k]
 
 
 def finish_kernel(
@@ -674,11 +695,10 @@
     )
 
 
-def exchange(rows):
-    count, lanes = rows.shape
+def exchange(rows, groups):
     return lax.all_to_all(
-        rows.reshape(count, 1, lanes), "seq", split_axis=0, concat_axis=0, tiled=True
-    ).reshape(count, lanes)
+        rows, "seq", split_axis=0, concat_axis=0, axis_index_groups=groups, tiled=True
+    )
 
 
 def local(
@@ -721,16 +741,20 @@
     fields = [
         in_hbm(x) for x in (key_proj, value_proj, query_proj, second_query, second_key, medium_filter)
     ]
+    rings = count // RING
+    share = tiles // RING
+    ring_groups = [[ring * RING + k for k in range(RING)] for ring in range(rings)]
+    across_groups = [[ring * RING + k for ring in range(rings)] for k in range(RING)]
     place = lax.axis_index("seq").astype(jnp.int32).reshape(1)
     tail, own_rate = call(
         tail_kernel,
         [pl.BlockSpec(memory_space=pltpu.SMEM)] + [outside] * 4,
         [held] * 2,
-        [struct(tiles, TAPS, LANES), struct(1, LANES)],
+        [struct(tiles, TAPS, LANES), struct(share, MODES, LANES)],
         [pltpu.VMEM((channels, LANES), F32)] * 2
-        + [pltpu.VMEM((3, 3, channels), F32), pltpu.VMEM((MODES, LANES), F32)]
+        + [pltpu.VMEM((3, 3, channels), F32), pltpu.VMEM((share, MODES, LANES), F32)]
         + [pltpu.SemaphoreType.DMA((chunks,))] * 2
-        + [pltpu.SemaphoreType.DMA] * 2,
+        + [pltpu.SemaphoreType.DMA, pltpu.SemaphoreType.DMA((share,))],
         words * 8,
         words * 6,
         "tail",
@@ -831,17 +855,29 @@
         halo_inverse,
     )
 
+    share_shape = (RING, share, MODES, LANES)
+    ring_states = in_hbm(exchange(state.reshape(share_shape), ring_groups))
+    totals = call(
+        ring_kernel,
+        [outside, held],
+        held,
+        struct(rings, share, MODES, LANES),
+        [pltpu.VMEM(share_shape, F32), pltpu.SemaphoreType.DMA],
+        count * LANES * 30,
+        count * LANES * 8,
+        "ring",
+    )(ring_states, own_rate)
     scanned = call(
         scan_kernel,
-        [held] * 2,
+        [pl.BlockSpec(memory_space=pltpu.SMEM), outside, held, held],
         held,
-        struct(count, LANES),
-        [],
+        struct(*share_shape),
+        [pltpu.VMEM(share_shape, F32), pltpu.SemaphoreType.DMA],
         count * LANES * 30,
         count * LANES * 8,
         "scan",
-    )(exchange(state.reshape(count, LANES)), own_rate)
-    incoming = exchange(scanned).reshape(tiles, MODES, LANES)
+    )(place, ring_states, exchange(totals, across_groups), own_rate)
+    incoming = exchange(scanned, ring_groups).reshape(tiles, MODES, LANES)
 
     mixed, squares = call(
         finish_kernel,

time: 91.9 us -> 91.2 us (level)
  blocking collectives: 50.2 us -> 47.8 us
  Pallas kernels: 27.7 us -> 29.3 us
    all_to_all x2 -> x3, blocking collectives: 43.9 us -> 40.2 us  [exchange(): lax.all_to_all(rows, 'seq', split_axis=0, concat_axis=0, axis_index_group...]
    pallas_call x1 -> x2, Pallas kernels: 0.06 us -> 1.73 us  [the longest x1 0.87 us: local(): call(ring_kernel, [outside, held], held, struct(rings, share, MODES, LANE...]
    psum x1, blocking collectives: 6.25 us -> 7.58 us  [local(): total = lax.psum(squares, 'chan')]
where the time goes in v4:
time: 91.2 us; the launch traced here: 90.9 us
  blocking collectives  47.8 us (52%)
  Pallas kernels  29.3 us (32%)
  starting transfers between devices  8.06 us (9%)
  waiting for transfers between devices  5.35 us (6%)
    all_to_all x3, blocking collectives, exchange(): lax.all_to_all(rows, 'seq', split_axis=0, concat_axis=0, axis_index_group...  40.2 us
    pallas_call x1, Pallas kernels, local(): call(local_kernel, [held] * 14, [held] * 8 + [outside], [struct(tiles, HE...  10.1 us
    ppermute x2, starting transfers between devices, from_behind(): return lax.ppermute(block, 'seq', [(i, i + 1) for i in range(count - 1)])  8.06 us
    psum x1, blocking collectives, local(): total = lax.psum(squares, 'chan')  7.58 us
    pallas_call x1, Pallas kernels, local(): call(prep_kernel, [outside] * 6 + [held], [held] * 7, [struct(tiles, T, L...  5.39 us
    ppermute x2, waiting for transfers between devices, from_behind(): return lax.ppermute(block, 'seq', [(i, i + 1) for i in range(count - 1)])  5.35 us
    pallas_call x1, Pallas kernels, local(): call(join_kernel, [held] * 19, [held, outside], [struct(tiles, MODES, LAN...  4.83 us
    pallas_call x1, Pallas kernels, local(): call(finish_kernel, [held, outside, outside] + [held] * 4, [held] * 2, [s...  3.23 us
  transfers between devices with their start and end apart: 2, of which 1 were waited for; matrix products, arithmetic and copies ran while one was open for 0% of the time, Pallas kernels for 17%

profile of v4, /device:TPU:1, one launch (start us, length us, event | category | flops | bytes accessed | tf_op | source)
XLA Modules:
  0.0 90.9 jit_solution(11555589980151256393)
XLA Ops:
  0.0 0.0 copy-start.1
  0.0 2.5 %tail.1 = (f32[16,128,128]{2,1,0:T(8,128)S(1)}, f32[2,8,128]{2,1,0:T(8,128)S(1)}) custom-call(s32[1]{0:T(128)} %bitcast.place_ref, f32[2048,256]{1,0:T(8,128)} %key_hbm.3, f32[2048,256]{1,0:T(8,128)} %value_hbm.3, f32[3,3,2048]{2,1,0:T(4,128)} %bitcast.15, f32[8,2048]{1,0:T(8,128)} %bitcast.11), custom_call_target="tpu_custom_call" | custom-call | flops 4194304 | bytes 3145728 | tf_op jit(solution)/shard_map/tail/pallas_call | solution.py:749
  2.5 0.0 copy-start
  2.5 0.0 copy-start.10
  2.5 0.0 copy-start.2
  2.5 0.0 copy-start.5
  2.5 0.0 copy-start.7
  2.5 0.0 copy-start.8
  2.5 0.0 copy-start.9
  2.6 4.6 %collective-permute-start = (f32[16,128,128]{2,1,0:T(8,128)S(1)}, f32[16,128,128]{2,1,0:T(8,128)S(1)}, u32[]{:S(2)}, u32[]{:S(2)}) collective-permute-start(f32[16,128,128]{2,1,0:T(8,128)S(1)} %get-tuple-element.27), channel_id=1, source_target_pairs={{0,2},{2,4},{4,6},{6,8},{8,10},{10,12},{12,14},{14,16},{16,18},{18... | collective-permute-start | bytes 3145736 | tf_op jit(solution)/shard_map/ppermute | solution.py:678
  7.1 0.0 copy-done.1
  7.1 5.4 %prep.1 = (f32[16,256,128]{2,1,0:T(8,128)S(1)}, f32[16,256,128]{2,1,0:T(8,128)S(1)}, f32[16,256,128]{2,1,0:T(8,128)S(1)}, f32[16,256,128]{2,1,0:T(8,128)S(1)}, f...) custom-call(f32[2048,256]{1,0:T(8,128)} %key_hbm.3, f32[2048,256]{1,0:T(8,128)} %value_hbm.3, ...), custom_call_target="tpu_custom_call" | custom-call | flops 10485760 | bytes 20971520 | tf_op jit(solution)/shard_map/prep/pallas_call | solution.py:764
  12.5 3.5 %collective-permute-start.1 = (f32[16,16,128]{2,1,0:T(8,128)S(1)}, f32[16,16,128]{2,1,0:T(8,128)S(1)}, u32[]{:S(2)}, u32[]{:S(2)}) collective-permute-start(f32[16,16,128]{2,1,0:T(8,128)S(1)} %get-tuple-element.28), channel_id=1, source_target_pairs={{0,2},{2,4},{4,6},{6,8},{8,10},{10,12},{12,14},{14,16},{16,18},{18... | collective-permute-start | bytes 393224 | tf_op jit(solution)/shard_map/ppermute | solution.py:678
  16.0 0.0 copy-done
  16.0 0.0 copy-done.10
  16.1 0.0 copy-done.2
  16.1 0.0 copy-done.5
  16.1 0.0 copy-done.7
  16.1 0.0 copy-done.8
  16.2 0.0 copy-done.9
  16.2 0.0 copy-start.3
  16.2 0.0 copy-start.4
  16.2 10.1 %local.1 = (f32[16,136,128]{2,1,0:T(8,128)S(1)}, f32[16,384,128]{2,1,0:T(8,128)S(1)}, f32[16,136,128]{2,1,0:T(8,128)S(1)}, f32[16,136,128]{2,1,0:T(8,128)S(1)}, ...) custom-call(f32[16,256,128]{2,1,0:T(8,128)S(1)} %get-tuple-element.2, ...), custom_call_target="tpu_custom_call" | custom-call | flops 4194304000 | bytes 31457280 | tf_op jit(solution)/shard_map/local/pallas_call | solution.py:788
  26.3 5.4 %collective-permute-done.1.rims_ref = f32[16,16,128]{2,1,0:T(8,128)S(1)} collective-permute-done((f32[16,16,128]{2,1,0:T(8,128)S(1)}, f32[16,16,128]{2,1,0:T(8,128)S(1)}, u32[]{:S(2)}, u32[]{:S(2)}) %collective-permute-start.1) | collective-permute-done | bytes 131104 | tf_op jit(solution)/shard_map/ppermute | solution.py:678
  31.7 0.0 collective-permute-done.halo_ref
  31.7 0.0 copy-done.3
  31.7 0.0 copy-done.4
  31.7 0.0 copy-start.6
  31.7 4.8 %join.1 = (f32[16,8,128]{2,1,0:T(8,128)S(1)}, f32[16,264,128]{2,1,0:T(8,128)}) custom-call(f32[16,128,128]{2,1,0:T(8,128)S(1)} %collective-permute-done.halo_ref, f32[16,16,128]{2,1,0:T(8,128)S(1)} %collective-permute-done.1.rims_ref, f32[16,384,128]{2,1,0:T(8,128)S(1)} %get-tuple-element.35.spectrum_ref, f32[16,136,128]{2,1,0:T(8,128)S(1)} %get-tuple-element.36.medium_ref, ...), custom_call_target="tpu_custom_call" | custom-call | flops 1048576000 | bytes 10485760 | tf_op jit(solution)/shard_map/join/pallas_call | solution.py:823
  36.5 17.2 %all_to_all.15.states_hbm = f32[8,2,8,128]{3,2,1,0:T(8,128)} all-to-all(f32[8,2,8,128]{3,2,1,0:T(8,128)S(1)} %bitcast.23), channel_id=1, replica_groups={{0,2,4,6,8,10,12,14},{16,18,20,22,24,26,28,30},{32,34,36,38,40,42,44,46..., dimensions={0} | all-to-all | bytes 131072 | tf_op jit(solution)/shard_map/all_to_all | solution.py:699
  53.7 0.9 ring.1
  54.6 13.4 %all_to_all.16.rings_ref = f32[16,2,8,128]{3,2,1,0:T(8,128)S(1)} all-to-all(f32[16,2,8,128]{3,2,1,0:T(8,128)S(1)} %ring.1), channel_id=1, replica_groups={{0,16,32,48,64,80,96,112,128,144,160,176,192,208,224,240},{2,18,34,50,6..., dimensions={0} | all-to-all | bytes 262144 | tf_op jit(solution)/shard_map/all_to_all | solution.py:699
  68.0 0.9 scan.1
  68.9 9.6 %all_to_all.17 = f32[8,2,8,128]{3,2,1,0:T(8,128)S(1)} all-to-all(f32[8,2,8,128]{3,2,1,0:T(8,128)S(1)} %scan.1), channel_id=1, replica_groups={{0,2,4,6,8,10,12,14},{16,18,20,22,24,26,28,30},{32,34,36,38,40,42,44,46..., dimensions={0} | all-to-all | bytes 131072 | tf_op jit(solution)/shard_map/all_to_all | solution.py:699
  78.5 0.0 copy-done.6
  78.5 3.2 %finish.1 = (f32[16,256,128]{2,1,0:T(8,128)S(1)}, f32[1,256]{1,0:T(1,128)S(1)}) custom-call(f32[16,8,128]{2,1,0:T(8,128)S(1)} %bitcast.22, f32[16,376,128]{2,1,0:T(8,128)} %get-tuple-element.45.early_hbm, f32[16,264,128]{2,1,0:T(8,128)} %get-tuple-element.46.late_hbm, f32[16,16,128]{2,1,0:T(8,128)S(1)} %collective-permute-done.1.rims_ref, ...), custom_call_target="tpu_custom_call" | custom-call | flops 20971520 | bytes 8388608 | tf_op jit(solution)/shard_map/finish/pallas_call | solution.py:882
  81.7 7.6 %psum.7.squares_ref = f32[1,256]{1,0:T(1,128)S(1)} all-reduce(f32[1,256]{1,0:T(1,128)S(1)} %get-tuple-element.48), channel_id=1, replica_groups=mesh['seq'=128,'chan'=2] {'chan'}, use_global_device_ids=true, to_apply=%region_0.0 | all-reduce | flops 256 | bytes 2048 | tf_op jit(solution)/shard_map/psum | solution.py:898
  89.3 1.5 %scale.1 = f32[2048,256]{1,0:T(8,128)} custom-call(f32[16,256,128]{2,1,0:T(8,128)S(1)} %get-tuple-element.47.mixed_ref, f32[1,256]{1,0:T(1,128)S(1)} %psum.7.squares_ref), custom_call_target="tpu_custom_call" | custom-call | flops 524288 | bytes 4194304 | tf_op jit(solution)/shard_map/scale/pallas_call | solution.py:899
  (1 shorter events, 0.0 us)
Async XLA Ops:
  0.0 7.1 %copy-start.1 = (f32[3,2048,3]{1,2,0:T(4,128)S(1)}, f32[3,2048,3]{1,2,0:T(4,128)}, u32[]{:S(2)}) copy-start(f32[3,2048,3]{1,2,0:T(4,128)} %param.22) | copy-start | bytes 221188
  2.5 13.6 %copy-start = (f32[2048,8]{0,1:T(8,128)S(1)}, f32[2048,8]{0,1:T(8,128)}, u32[]{:S(2)}) copy-start(f32[2048,8]{0,1:T(8,128)} %param.25) | copy-start | bytes 196612
  2.5 13.6 %copy-start.10 = (f32[2048,8]{0,1:T(8,128)S(1)}, f32[2048,8]{0,1:T(8,128)}, u32[]{:S(2)}) copy-start(f32[2048,8]{0,1:T(8,128)} %param.26) | copy-start | bytes 196612
  2.5 13.6 %copy-start.2 = (f32[3,2048,3]{1,2,0:T(4,128)S(1)}, f32[3,2048,3]{1,2,0:T(4,128)}, u32[]{:S(2)}) copy-start(f32[3,2048,3]{1,2,0:T(4,128)} %param.23) | copy-start | bytes 221188
  2.5 13.6 %copy-start.5 = (f32[2048]{0:T(1024)S(1)}, f32[2048]{0:T(1024)}, u32[]{:S(2)}) copy-start(f32[2048]{0:T(1024)} %param.27) | copy-start | bytes 24580
  2.5 13.6 %copy-start.7 = (bf16[512,768]{1,0:T(8,128)(2,1)S(1)}, bf16[512,768]{1,0:T(8,128)(2,1)}, u32[]{:S(2)}) copy-start(bf16[512,768]{1,0:T(8,128)(2,1)} %constant.18.clone.forward_ref) | copy-start | bytes 2359300
  2.5 13.6 %copy-start.8 = (bf16[256,1536]{1,0:T(8,128)(2,1)S(1)}, bf16[256,1536]{1,0:T(8,128)(2,1)}, u32[]{:S(2)}) copy-start(bf16[256,1536]{1,0:T(8,128)(2,1)} %constant.20.clone.inverse_ref) | copy-start | bytes 2359300
  2.5 13.6 %copy-start.9 = (bf16[384,384]{1,0:T(8,128)(2,1)S(1)}, bf16[384,384]{1,0:T(8,128)(2,1)}, u32[]{:S(2)}) copy-start(bf16[384,384]{1,0:T(8,128)(2,1)} %constant.19.clone.spectrum_ref) | copy-start | bytes 884740
  2.6 29.1 %collective-permute-start = (f32[16,128,128]{2,1,0:T(8,128)S(1)}, f32[16,128,128]{2,1,0:T(8,128)S(1)}, u32[]{:S(2)}, u32[]{:S(2)}) collective-permute-start(f32[16,128,128]{2,1,0:T(8,128)S(1)} %get-tuple-element.27), channel_id=1, source_target_pairs={{0,2},{2,4},{4,6},{6,8},{8,10},{10,12},{12,14},{14,16},{16,18},{18... | collective-permute-start | bytes 3145736 | tf_op jit(solution)/shard_map/ppermute | solution.py:678
  12.5 19.1 %collective-permute-start.1 = (f32[16,16,128]{2,1,0:T(8,128)S(1)}, f32[16,16,128]{2,1,0:T(8,128)S(1)}, u32[]{:S(2)}, u32[]{:S(2)}) collective-permute-start(f32[16,16,128]{2,1,0:T(8,128)S(1)} %get-tuple-element.28), channel_id=1, source_target_pairs={{0,2},{2,4},{4,6},{6,8},{8,10},{10,12},{12,14},{14,16},{16,18},{18... | collective-permute-start | bytes 393224 | tf_op jit(solution)/shard_map/ppermute | solution.py:678
  16.2 15.5 %copy-start.3 = (bf16[144,768]{1,0:T(8,128)(2,1)S(1)}, bf16[144,768]{1,0:T(8,128)(2,1)}, u32[]{:S(2)}) copy-start(bf16[144,768]{1,0:T(8,128)(2,1)} %constant.22.clone.inverse_ref) | copy-start | bytes 663556
  16.2 15.5 %copy-start.4 = (bf16[256,384]{1,0:T(8,128)(2,1)S(1)}, bf16[256,384]{1,0:T(8,128)(2,1)}, u32[]{:S(2)}) copy-start(bf16[256,384]{1,0:T(8,128)(2,1)} %constant.21.clone.forward_ref) | copy-start | bytes 589828
  31.7 46.8 %copy-start.6 = (f32[2048]{0:T(1024)S(1)}, f32[2048]{0:T(1024)}, u32[]{:S(2)}) copy-start(f32[2048]{0:T(1024)} %param.28) | copy-start | bytes 24580

commit v5 on v4

--- a/solution.py
+++ b/solution.py
@@ -186,7 +186,7 @@
     rate_sem,
 ):
     chunks = key_sem.shape[0]
-    rows = key_hbm.shape[0] // chunks
+    rows = key_in.shape[0] // chunks
     copies = []
     filters = pltpu.make_async_copy(short_hbm, short_ref, short_sem)
     filters.start()
@@ -236,6 +236,7 @@
     key2_hbm,
     medium_hbm,
     short_ref,
+    _,
     key_t,
     value_t,
     query_t,
@@ -243,6 +244,7 @@
     key2_t,
     taps_t,
     rims_out,
+    tail_out,
     key_in,
     value_in,
     query_in,
@@ -290,6 +292,14 @@
                     for j in range(3)
                 )
 
+            late = tile - (key_t.shape[0] - tail_out.shape[0])
+            if late >= 0:
+                gated = 1.0
+                for ref, index in ((key_t, 1), (value_t, 2)):
+                    here = ref[tile, T // 2 : T, :]
+                    taps = [short_ref[index, j : j + 1, lanes] for j in range(3)]
+                    gated = gated * (taps[0] * here + taps[1] * down(here) + taps[2] * down(here, 2))
+                tail_out[late] = gated
             for k in range(2):
                 rims_out[tile, 10 + k : 11 + k, :] = feature(query_t, 0, T - 2 + k)
             for k in range(3):
@@ -421,6 +431,7 @@
 
 
 def join_kernel(
+    base,
     halo_ref,
     rims_ref,
     spectrum_ref,
@@ -440,26 +451,28 @@
     skip_ref,
     forward_ref,
     inverse_ref,
-    state_out,
-    late_hbm,
-    medium_t,
-    late,
-    late_sem,
+    *rest,
 ):
+    *before, state_out, late_hbm, medium_t, late, late_sem = rest
     tiles = halo_ref.shape[0]
     group = medium_t.shape[1] // LANES
     top = sublane((SEG, LANES)) == 0
+    for ref in before:
+        state_out[0:base] = ref[...]
 
     def body(step, _):
-        tile_list = [step * group + part for part in range(group)]
+        tile_list = [base + step * group + part for part in range(group)]
         halo = matmul3(
-            forward_ref[...], jnp.concatenate([halo_ref[tile] for tile in tile_list], 1)
+            forward_ref[...], jnp.concatenate([halo_ref[tile - base] for tile in tile_list], 1)
         )
         filters = jnp.concatenate([spectrum_ref[tile] for tile in tile_list], 1)
         medium_t[...] = matmul3(inverse_ref[...], spectral_product(halo, filters))
         for part, tile in enumerate(tile_list):
             one(tile, pl.ds(part * LANES, LANES))
         return _
+
+    def copy_of(tile):
+        return pltpu.make_async_copy(late.at[tile], late_hbm.at[tile], late_sem.at[tile])
 
     def one(tile, local):
         lanes = pl.ds(pl.multiple_of(tile * LANES, LANES), LANES)
@@ -524,23 +537,23 @@
             spread(skip_ref[:, lanes]),
         )
         for k in range(HEAD):
-            late[tile, pl.ds(SEG * k, SEG), :] = outs[k]
+            late[tile - base, pl.ds(SEG * k, SEG), :] = outs[k]
         powers = segment_powers(rates, float(HEAD))
         whole = jnp.exp(-float(MAIN_ROWS) * rates)
         for r in range(MODES):
             enter, leave = prefix(ends[r], powers, r)
-            late[tile, pl.ds(HEAD_ROWS + SEG * r, SEG), :] = enter
-            late[tile, pl.ds(HEAD_ROWS + SEG * (MODES + r), SEG), :] = enter_main_ref[
+            late[tile - base, pl.ds(HEAD_ROWS + SEG * r, SEG), :] = enter
+            late[tile - base, pl.ds(HEAD_ROWS + SEG * (MODES + r), SEG), :] = enter_main_ref[
                 tile, r
             ] + reach_main_ref[tile, r] * spread(leave)
             state_out[tile, r : r + 1, :] = (
                 leave_main_ref[tile, r : r + 1, :] + leave * whole[r : r + 1]
             )
-        pltpu.make_async_copy(late.at[tile], late_hbm.at[tile], late_sem.at[tile]).start()
+        copy_of(tile - base).start()
 
     lax.fori_loop(0, tiles // group, body, 0, unroll=True)
     for tile in range(tiles):
-        pltpu.make_async_copy(late.at[tile], late_hbm.at[tile], late_sem.at[tile]).wait()
+        copy_of(tile).wait()
 
 
 def ring_kernel(states_hbm, rate_ref, out_ref, states, sem):
@@ -575,6 +588,7 @@
     state_ref,
     early_hbm,
     late_hbm,
+    later_hbm,
     rims_ref,
     second_ref,
     rate_ref,
@@ -593,8 +607,13 @@
     copies = []
     for chunk in range(chunks):
         here = pl.ds(chunk * count, count)
-        for place, (source, target) in enumerate(((early_hbm, early), (late_hbm, late))):
-            copy = pltpu.make_async_copy(source.at[here], target.at[here], sems.at[place, chunk])
+        first = chunk * count
+        if first < late_hbm.shape[0]:
+            joined = late_hbm.at[here]
+        else:
+            joined = later_hbm.at[pl.ds(first - late_hbm.shape[0], count)]
+        for place, (source, target) in enumerate(((early_hbm.at[here], early), (joined, late))):
+            copy = pltpu.make_async_copy(source, target.at[here], sems.at[place, chunk])
             copy.start()
             copies.append(copy)
     squares_t[...] = jnp.zeros_like(squares_t)
@@ -721,6 +740,7 @@
     group = min(4, tiles)
     join_group = min(2, tiles)
     chunks = min(4, tiles)
+    parts = (tiles - tiles // chunks, tiles // chunks)
     short_t = jnp.transpose(short_filter, (0, 2, 1))
     second_t = jnp.transpose(second_short, (0, 2, 1))
     rate_t = decay_rate.T
@@ -750,10 +770,10 @@
         tail_kernel,
         [pl.BlockSpec(memory_space=pltpu.SMEM)] + [outside] * 4,
         [held] * 2,
-        [struct(tiles, TAPS, LANES), struct(share, MODES, LANES)],
-        [pltpu.VMEM((channels, LANES), F32)] * 2
+        [struct(parts[0], TAPS, LANES), struct(share, MODES, LANES)],
+        [pltpu.VMEM((parts[0] * LANES, LANES), F32)] * 2
         + [pltpu.VMEM((3, 3, channels), F32), pltpu.VMEM((share, MODES, LANES), F32)]
-        + [pltpu.SemaphoreType.DMA((chunks,))] * 2
+        + [pltpu.SemaphoreType.DMA((parts[0] // (tiles // chunks),))] * 2
         + [pltpu.SemaphoreType.DMA, pltpu.SemaphoreType.DMA((share,))],
         words * 8,
         words * 6,
@@ -761,19 +781,21 @@
     )(place, fields[0], fields[1], in_hbm(short_t), in_hbm(rate_t))
     halo = from_behind(tail)
 
-    *turned_fields, taps_t, rims = call(
+    *turned_fields, taps_t, rims, tail_two = call(
         prep_kernel,
-        [outside] * 6 + [held],
-        [held] * 7,
+        [outside] * 6 + [held] * 2,
+        [held] * 8,
         [struct(tiles, T, LANES)] * 5
-        + [struct(tiles, HEAD_ROWS, LANES), struct(tiles, RIMS, LANES)],
+        + [struct(tiles, HEAD_ROWS, LANES), struct(tiles, RIMS, LANES)]
+        + [struct(parts[1], TAPS, LANES)],
         [pltpu.VMEM((channels, T), F32)] * 5
         + [pltpu.VMEM((channels, TAPS), F32), pltpu.SemaphoreType.DMA((6, chunks))],
         words * 20,
         words * 40,
         "prep",
-    )(*fields, short_t)
+    )(*fields, short_t, own_rate)
     border = from_behind(rims)
+    halo_two = from_behind(tail_two)
 
     (
         taps,
@@ -820,40 +842,46 @@
     )
 
     late_rows = HEAD_ROWS + 2 * MODES * SEG
-    state, late = call(
-        join_kernel,
-        [held] * 19,
-        [held, outside],
-        [struct(tiles, MODES, LANES), hbm(tiles, late_rows, LANES)],
-        [
-            pltpu.VMEM((HEAD_ROWS + 8, join_group * LANES), F32),
-            pltpu.VMEM((tiles, late_rows, LANES), F32),
-            pltpu.SemaphoreType.DMA((tiles,)),
-        ],
-        words * 2000,
-        words * 20,
-        "join",
-    )(
-        halo,
-        border,
-        tap_spectrum,
-        medium,
-        taps,
-        query,
-        key2,
-        turned_fields[0],
-        turned_fields[1],
-        enter_main,
-        leave_main,
-        reach_main,
-        short_t,
-        second_t,
-        rate_t,
-        amplitude,
-        skip,
-        halo_forward,
-        halo_inverse,
-    )
+    state, late = (), []
+    for base, part in zip((0, parts[0]), (halo, halo_two)):
+        count_here = part.shape[0]
+        *state, joined = call(
+            functools.partial(join_kernel, base),
+            [held] * (19 + len(state)),
+            [held, outside],
+            [struct(base + count_here, MODES, LANES), hbm(count_here, late_rows, LANES)],
+            [
+                pltpu.VMEM((HEAD_ROWS + 8, join_group * LANES), F32),
+                pltpu.VMEM((count_here, late_rows, LANES), F32),
+                pltpu.SemaphoreType.DMA((count_here,)),
+            ],
+            count_here * 500 * T * LANES,
+            count_here * 20 * T * LANES,
+            "join",
+        )(
+            part,
+            border,
+            tap_spectrum,
+            medium,
+            taps,
+            query,
+            key2,
+            turned_fields[0],
+            turned_fields[1],
+            enter_main,
+            leave_main,
+            reach_main,
+            short_t,
+            second_t,
+            rate_t,
+            amplitude,
+            skip,
+            halo_forward,
+            halo_inverse,
+            *state,
+        )
+        late.append(in_hbm(joined))
+    (state,) = state
 
     share_shape = (RING, share, MODES, LANES)
     ring_states = in_hbm(exchange(state.reshape(share_shape), ring_groups))
@@ -881,7 +909,7 @@
 
     mixed, squares = call(
         finish_kernel,
-        [held, outside, outside] + [held] * 4,
+        [held] + [outside] * 3 + [held] * 4,
         [held] * 2,
         [struct(tiles, T, LANES), struct(1, T)],
         [
@@ -894,7 +922,7 @@
         words * 40,
         words * 16,
         "finish",
-    )(incoming, in_hbm(early), in_hbm(late), border, second_t, rate_t, gain)
+    )(incoming, in_hbm(early), *late, border, second_t, rate_t, gain)
     total = lax.psum(squares, "chan")
     return call(
         functools.partial(scale_kernel, float(channels * lax.axis_size("chan"))),

time: 91.2 us -> 87.7 us (0.962)
  waiting for transfers between devices: 5.35 us -> 0.01 us
  starting transfers between devices: 8.06 us -> 11.5 us
  blocking collectives: 47.8 us -> 45.4 us
    ppermute x2 -> x3, waiting for transfers between devices: 5.35 us -> 0.01 us  [from_behind(): return lax.ppermute(block, 'seq', [(i, i + 1) for i in range(count - 1)])]
    ppermute x2 -> x3, starting transfers between devices: 8.06 us -> 11.5 us  [from_behind(): return lax.ppermute(block, 'seq', [(i, i + 1) for i in range(count - 1)])]
    all_to_all x3, blocking collectives: 40.2 us -> 37.8 us  [exchange(): lax.all_to_all(rows, 'seq', split_axis=0, concat_axis=0, axis_index_group...]
    pallas_call x3 -> x4, Pallas kernels: 13.5 us -> 14.5 us  [the longest x2 5.79 us: local(): call(functools.partial(join_kernel, base), [held] * (19 + len(state)), [h...]
  transfers between devices with their start and end apart: 2 -> 3, of which waited for: 1 -> 0; matrix products, arithmetic and copies ran while one was open for 0% -> 0% of each run, Pallas kernels for 17% -> 22%
where the time goes in v5:
time: 87.7 us; the launch traced here: 87.3 us
  blocking collectives  45.4 us (52%)
  Pallas kernels  30 us (34%)
  starting transfers between devices  11.5 us (13%)
    all_to_all x3, blocking collectives, exchange(): lax.all_to_all(rows, 'seq', split_axis=0, concat_axis=0, axis_index_group...  37.8 us
    ppermute x3, starting transfers between devices, from_behind(): return lax.ppermute(block, 'seq', [(i, i + 1) for i in range(count - 1)])  11.5 us
    pallas_call x1, Pallas kernels, local(): call(local_kernel, [held] * 14, [held] * 8 + [outside], [struct(tiles, HE...  10.2 us
    psum x1, blocking collectives, local(): total = lax.psum(squares, 'chan')  7.57 us
    pallas_call x2, Pallas kernels, local(): call(functools.partial(join_kernel, base), [held] * (19 + len(state)), [h...  5.79 us
    pallas_call x1, Pallas kernels, local(): call(prep_kernel, [outside] * 6 + [held] * 2, [held] * 8, [struct(tiles,...  5.52 us
    pallas_call x1, Pallas kernels, local(): call(finish_kernel, [held] + [outside] * 3 + [held] * 4, [held] * 2, [str...  3.23 us
    pallas_call x1, Pallas kernels, local(): call(tail_kernel, [pl.BlockSpec(memory_space=pltpu.SMEM)] + [outside] * 4...  2.05 us
  transfers between devices with their start and end apart: 3, of which 0 were waited for; matrix products, arithmetic and copies ran while one was open for 0% of the time, Pallas kernels for 22%

profile of v5, /device:TPU:1, one launch (start us, length us, event | category | flops | bytes accessed | tf_op | source)
XLA Modules:
  0.0 87.3 jit_solution(462153279570323848)
XLA Ops:
  0.0 0.0 copy-start.1
  0.0 2.0 %tail.1 = (f32[12,128,128]{2,1,0:T(8,128)S(1)}, f32[2,8,128]{2,1,0:T(8,128)S(1)}) custom-call(s32[1]{0:T(128)} %bitcast.place_ref, f32[2048,256]{1,0:T(8,128)} %key_hbm.3, f32[2048,256]{1,0:T(8,128)} %value_hbm.3, f32[3,3,2048]{2,1,0:T(4,128)} %bitcast.16, f32[8,2048]{1,0:T(8,128)} %bitcast.11), custom_call_target="tpu_custom_call" | custom-call | flops 4194304 | bytes 3145728 | tf_op jit(solution)/shard_map/tail/pallas_call | solution.py:769
  2.1 4.4 %collective-permute-start.2 = (f32[12,128,128]{2,1,0:T(8,128)S(1)}, f32[12,128,128]{2,1,0:T(8,128)S(1)}, u32[]{:S(2)}, u32[]{:S(2)}) collective-permute-start(f32[12,128,128]{2,1,0:T(8,128)S(1)} %get-tuple-element.47), channel_id=1, source_target_pairs={{0,2},{2,4},{4,6},{6,8},{8,10},{10,12},{12,14},{14,16},{16,18},{18... | collective-permute-start | bytes 2359304 | tf_op jit(solution)/shard_map/ppermute | solution.py:697
  6.5 0.0 copy-done.1
  6.5 0.0 copy-start
  6.5 0.0 copy-start.10
  6.5 0.0 copy-start.2
  6.5 0.0 copy-start.5
  6.5 0.0 copy-start.7
  6.6 0.0 copy-start.8
  6.6 0.0 copy-start.9
  6.6 5.5 %prep.1 = (f32[16,256,128]{2,1,0:T(8,128)S(1)}, f32[16,256,128]{2,1,0:T(8,128)S(1)}, f32[16,256,128]{2,1,0:T(8,128)S(1)}, f32[16,256,128]{2,1,0:T(8,128)S(1)}, f...) custom-call(f32[2048,256]{1,0:T(8,128)} %key_hbm.3, ...), custom_call_target="tpu_custom_call" | custom-call | flops 10485760 | bytes 20971520 | tf_op jit(solution)/shard_map/prep/pallas_call | solution.py:784
  12.1 3.5 %collective-permute-start.1 = (f32[16,16,128]{2,1,0:T(8,128)S(1)}, f32[16,16,128]{2,1,0:T(8,128)S(1)}, u32[]{:S(2)}, u32[]{:S(2)}) collective-permute-start(f32[16,16,128]{2,1,0:T(8,128)S(1)} %get-tuple-element.32), channel_id=1, source_target_pairs={{0,2},{2,4},{4,6},{6,8},{8,10},{10,12},{12,14},{14,16},{16,18},{18... | collective-permute-start | bytes 393224 | tf_op jit(solution)/shard_map/ppermute | solution.py:697
  15.6 3.6 %collective-permute-start = (f32[4,128,128]{2,1,0:T(8,128)S(1)}, f32[4,128,128]{2,1,0:T(8,128)S(1)}, u32[]{:S(2)}, u32[]{:S(2)}) collective-permute-start(f32[4,128,128]{2,1,0:T(8,128)S(1)} %get-tuple-element.31), channel_id=1, source_target_pairs={{0,2},{2,4},{4,6},{6,8},{8,10},{10,12},{12,14},{14,16},{16,18},{18... | collective-permute-start | bytes 786440 | tf_op jit(solution)/shard_map/ppermute | solution.py:697
  19.2 0.0 copy-done
  19.2 0.0 copy-done.10
  19.3 0.0 copy-done.2
  19.3 0.0 copy-done.5
  19.3 0.0 copy-done.7
  19.3 0.0 copy-done.8
  19.3 0.0 copy-done.9
  19.3 0.0 copy-start.3
  19.3 0.0 copy-start.4
  19.3 10.2 %local.1 = (f32[16,136,128]{2,1,0:T(8,128)S(1)}, f32[16,384,128]{2,1,0:T(8,128)S(1)}, f32[16,136,128]{2,1,0:T(8,128)S(1)}, f32[16,136,128]{2,1,0:T(8,128)S(1)}, ...) custom-call(f32[16,256,128]{2,1,0:T(8,128)S(1)} %get-tuple-element.3, ...), custom_call_target="tpu_custom_call" | custom-call | flops 4194304000 | bytes 31457280 | tf_op jit(solution)/shard_map/local/pallas_call | solution.py:810
  29.5 0.0 collective-permute-done.1.rims_ref
  29.5 0.0 collective-permute-done.2.halo_ref
  29.5 0.0 copy-done.3
  29.5 0.0 copy-done.4
  29.6 3.9 %join.2 = (f32[12,8,128]{2,1,0:T(8,128)S(1)}, f32[12,264,128]{2,1,0:T(8,128)}) custom-call(f32[12,128,128]{2,1,0:T(8,128)S(1)} %collective-permute-done.2.halo_ref, f32[16,16,128]{2,1,0:T(8,128)S(1)} %collective-permute-done.1.rims_ref, f32[16,384,128]{2,1,0:T(8,128)S(1)} %get-tuple-element.39.spectrum_ref, ...), custom_call_target="tpu_custom_call" | custom-call | flops 196608000 | bytes 7864320 | tf_op jit(solution)/shard_map/join/pallas_call | solution.py:848
  33.4 0.0 collective-permute-done.halo_ref
  33.4 0.0 copy-start.6
  33.4 1.9 %join.3 = (f32[16,8,128]{2,1,0:T(8,128)S(1)}, f32[4,264,128]{2,1,0:T(8,128)}) custom-call(f32[4,128,128]{2,1,0:T(8,128)S(1)} %collective-permute-done.halo_ref, f32[16,16,128]{2,1,0:T(8,128)S(1)} %collective-permute-done.1.rims_ref, f32[16,384,128]{2,1,0:T(8,128)S(1)} %get-tuple-element.39.spectrum_ref, f32[16,136,128]{2,1,0:T(8,128)S(1)} %get-tuple-element.40.medium_ref, ...), custom_call_target="tpu_custom_call" | custom-call | flops 65536000 | bytes 2621440 | tf_op jit(solution)/shard_map/join/pallas_call | solution.py:848
  35.4 14.8 %all_to_all.15.states_hbm = f32[8,2,8,128]{3,2,1,0:T(8,128)} all-to-all(f32[8,2,8,128]{3,2,1,0:T(8,128)S(1)} %bitcast.26), channel_id=1, replica_groups={{0,2,4,6,8,10,12,14},{16,18,20,22,24,26,28,30},{32,34,36,38,40,42,44,46..., dimensions={0} | all-to-all | bytes 131072 | tf_op jit(solution)/shard_map/all_to_all | solution.py:718
  50.2 0.9 ring.1
  51.1 13.4 %all_to_all.16.rings_ref = f32[16,2,8,128]{3,2,1,0:T(8,128)S(1)} all-to-all(f32[16,2,8,128]{3,2,1,0:T(8,128)S(1)} %ring.1), channel_id=1, replica_groups={{0,16,32,48,64,80,96,112,128,144,160,176,192,208,224,240},{2,18,34,50,6..., dimensions={0} | all-to-all | bytes 262144 | tf_op jit(solution)/shard_map/all_to_all | solution.py:718
  64.5 0.9 scan.1
  65.3 9.6 %all_to_all.17 = f32[8,2,8,128]{3,2,1,0:T(8,128)S(1)} all-to-all(f32[8,2,8,128]{3,2,1,0:T(8,128)S(1)} %scan.1), channel_id=1, replica_groups={{0,2,4,6,8,10,12,14},{16,18,20,22,24,26,28,30},{32,34,36,38,40,42,44,46..., dimensions={0} | all-to-all | bytes 131072 | tf_op jit(solution)/shard_map/all_to_all | solution.py:718
  74.9 0.0 copy-done.6
  74.9 3.2 %finish.1 = (f32[16,256,128]{2,1,0:T(8,128)S(1)}, f32[1,256]{1,0:T(1,128)S(1)}) custom-call(f32[16,8,128]{2,1,0:T(8,128)S(1)} %bitcast.25, f32[16,376,128]{2,1,0:T(8,128)} %get-tuple-element.50.early_hbm, f32[12,264,128]{2,1,0:T(8,128)} %get-tuple-element.51.late_hbm, f32[4,264,128]{2,1,0:T(8,128)} %get-tuple-element.52.later_hbm, ...), custom_call_target="tpu_custom_call" | custom-call | flops 20971520 | bytes 8388608 | tf_op jit(solution)/shard_map/finish/pallas_call | solution.py:910
  78.2 7.6 %psum.7.squares_ref = f32[1,256]{1,0:T(1,128)S(1)} all-reduce(f32[1,256]{1,0:T(1,128)S(1)} %get-tuple-element.54), channel_id=1, replica_groups=mesh['seq'=128,'chan'=2] {'chan'}, use_global_device_ids=true, to_apply=%region_0.0 | all-reduce | flops 256 | bytes 2048 | tf_op jit(solution)/shard_map/psum | solution.py:926
  85.7 1.5 %scale.1 = f32[2048,256]{1,0:T(8,128)} custom-call(f32[16,256,128]{2,1,0:T(8,128)S(1)} %get-tuple-element.53.mixed_ref, f32[1,256]{1,0:T(1,128)S(1)} %psum.7.squares_ref), custom_call_target="tpu_custom_call" | custom-call | flops 524288 | bytes 4194304 | tf_op jit(solution)/shard_map/scale/pallas_call | solution.py:927
  (1 shorter events, 0.0 us)
Async XLA Ops:
  0.0 6.5 %copy-start.1 = (f32[3,2048,3]{1,2,0:T(4,128)S(1)}, f32[3,2048,3]{1,2,0:T(4,128)}, u32[]{:S(2)}) copy-start(f32[3,2048,3]{1,2,0:T(4,128)} %param.22) | copy-start | bytes 221188
  2.1 27.5 %collective-permute-start.2 = (f32[12,128,128]{2,1,0:T(8,128)S(1)}, f32[12,128,128]{2,1,0:T(8,128)S(1)}, u32[]{:S(2)}, u32[]{:S(2)}) collective-permute-start(f32[12,128,128]{2,1,0:T(8,128)S(1)} %get-tuple-element.47), channel_id=1, source_target_pairs={{0,2},{2,4},{4,6},{6,8},{8,10},{10,12},{12,14},{14,16},{16,18},{18... | collective-permute-start | bytes 2359304 | tf_op jit(solution)/shard_map/ppermute | solution.py:697
  6.5 12.7 %copy-start = (f32[2048,8]{0,1:T(8,128)S(1)}, f32[2048,8]{0,1:T(8,128)}, u32[]{:S(2)}) copy-start(f32[2048,8]{0,1:T(8,128)} %param.25) | copy-start | bytes 196612
  6.5 12.7 %copy-start.10 = (f32[2048,8]{0,1:T(8,128)S(1)}, f32[2048,8]{0,1:T(8,128)}, u32[]{:S(2)}) copy-start(f32[2048,8]{0,1:T(8,128)} %param.26) | copy-start | bytes 196612
  6.5 12.7 %copy-start.2 = (f32[3,2048,3]{1,2,0:T(4,128)S(1)}, f32[3,2048,3]{1,2,0:T(4,128)}, u32[]{:S(2)}) copy-start(f32[3,2048,3]{1,2,0:T(4,128)} %param.23) | copy-start | bytes 221188
  6.5 12.7 %copy-start.5 = (f32[2048]{0:T(1024)S(1)}, f32[2048]{0:T(1024)}, u32[]{:S(2)}) copy-start(f32[2048]{0:T(1024)} %param.27) | copy-start | bytes 24580
  6.5 12.7 %copy-start.7 = (bf16[256,1536]{1,0:T(8,128)(2,1)S(1)}, bf16[256,1536]{1,0:T(8,128)(2,1)}, u32[]{:S(2)}) copy-start(bf16[256,1536]{1,0:T(8,128)(2,1)} %constant.20.clone.inverse_ref) | copy-start | bytes 2359300
  6.6 12.7 %copy-start.8 = (bf16[512,768]{1,0:T(8,128)(2,1)S(1)}, bf16[512,768]{1,0:T(8,128)(2,1)}, u32[]{:S(2)}) copy-start(bf16[512,768]{1,0:T(8,128)(2,1)} %constant.18.clone.forward_ref) | copy-start | bytes 2359300
  6.6 12.7 %copy-start.9 = (bf16[384,384]{1,0:T(8,128)(2,1)S(1)}, bf16[384,384]{1,0:T(8,128)(2,1)}, u32[]{:S(2)}) copy-start(bf16[384,384]{1,0:T(8,128)(2,1)} %constant.19.clone.spectrum_ref) | copy-start | bytes 884740
  12.1 17.4 %collective-permute-start.1 = (f32[16,16,128]{2,1,0:T(8,128)S(1)}, f32[16,16,128]{2,1,0:T(8,128)S(1)}, u32[]{:S(2)}, u32[]{:S(2)}) collective-permute-start(f32[16,16,128]{2,1,0:T(8,128)S(1)} %get-tuple-element.32), channel_id=1, source_target_pairs={{0,2},{2,4},{4,6},{6,8},{8,10},{10,12},{12,14},{14,16},{16,18},{18... | collective-permute-start | bytes 393224 | tf_op jit(solution)/shard_map/ppermute | solution.py:697
  15.6 17.8 %collective-permute-start = (f32[4,128,128]{2,1,0:T(8,128)S(1)}, f32[4,128,128]{2,1,0:T(8,128)S(1)}, u32[]{:S(2)}, u32[]{:S(2)}) collective-permute-start(f32[4,128,128]{2,1,0:T(8,128)S(1)} %get-tuple-element.31), channel_id=1, source_target_pairs={{0,2},{2,4},{4,6},{6,8},{8,10},{10,12},{12,14},{14,16},{16,18},{18... | collective-permute-start | bytes 786440 | tf_op jit(solution)/shard_map/ppermute | solution.py:697
  19.3 10.2 %copy-start.3 = (bf16[144,768]{1,0:T(8,128)(2,1)S(1)}, bf16[144,768]{1,0:T(8,128)(2,1)}, u32[]{:S(2)}) copy-start(bf16[144,768]{1,0:T(8,128)(2,1)} %constant.22.clone.inverse_ref) | copy-start | bytes 663556
  19.3 10.2 %copy-start.4 = (bf16[256,384]{1,0:T(8,128)(2,1)S(1)}, bf16[256,384]{1,0:T(8,128)(2,1)}, u32[]{:S(2)}) copy-start(bf16[256,384]{1,0:T(8,128)(2,1)} %constant.21.clone.forward_ref) | copy-start | bytes 589828
  33.4 41.5 %copy-start.6 = (f32[2048]{0:T(1024)S(1)}, f32[2048]{0:T(1024)}, u32[]{:S(2)}) copy-start(f32[2048]{0:T(1024)} %param.28) | copy-start | bytes 24580

commit v6 on v5

--- a/solution.py
+++ b/solution.py
@@ -20,6 +20,7 @@
 MAIN = 15
 HEAD_ROWS = HEAD * SEG
 MAIN_ROWS = MAIN * SEG
+EARLY_ROWS = 144
 RIMS = 16
 RING = 8
 LIMIT = 24 * 1024 * 1024
@@ -60,27 +61,23 @@
 
 def tables():
     times = row_times()
-    first = packed_forward(times + 128) * (times < 128)[None, :]
+    early = times[:EARLY_ROWS]
+    first = packed_forward(early + 128) * (early < 128)[None, :]
     second = packed_forward(times)
-    forward = np.concatenate([first, second], 0)
     taps = packed_forward(np.arange(TAPS))
     real, imag = taps[:128], taps[128:].copy()
     cross = real.copy()
     cross[0] = imag[0]
     imag[0] = 0.0
     spectrum = np.concatenate([real, imag, cross], 0)
-    inverse = np.concatenate(
-        [
-            packed_inverse(times + 128) * (times < 128)[:, None],
-            packed_inverse(times) * (times >= 128)[:, None],
-        ],
-        1,
-    )
+    first_back = packed_inverse(early + 128) * (early < 128)[:, None]
+    second_back = packed_inverse(times) * (times >= 128)[:, None]
     halo = packed_forward(np.arange(128))
     halo[:, :2] = 0.0
     head_times = np.concatenate([times[:HEAD_ROWS], [-2, -1], np.full(6, 255)])
     halo_back = packed_inverse(head_times + 128) * (head_times < 128)[:, None]
-    return [three_pass(m) for m in (forward, spectrum, inverse, halo, halo_back)]
+    matrices = (first, second, spectrum, first_back, second_back, halo, halo_back)
+    return [three_pass(m) for m in matrices]
 
 
 def halves(x):
@@ -89,10 +86,13 @@
     return high, low
 
 
-def matmul3(matrix, x):
-    high, low = halves(x)
+def matmul_halves(matrix, high, low):
     stacked = jnp.concatenate([high, high, low], 0)
     return jnp.dot(matrix, stacked, preferred_element_type=F32)
+
+
+def matmul3(matrix, x):
+    return matmul_halves(matrix, *halves(x))
 
 
 def spectral_product(x, taps):
@@ -151,17 +151,14 @@
     return outs, states
 
 
-def segment_powers(rates, step):
-    return [jnp.exp(-(step * distance) * rates) for distance in (1, 2, 4)]
-
-
-def prefix(state, powers, mode):
-    place = sublane(state.shape)
-    total = state
-    for power, distance in zip(powers, (1, 2, 4)):
-        moved = jnp.where(place >= distance, down(total, distance), 0.0)
-        total = total + spread(power[mode : mode + 1]) * moved
-    return jnp.where(place >= 1, down(total), 0.0), total[SEG - 1 :]
+def prefix(ends, rates, step, by_segment):
+    for r in range(MODES):
+        by_segment[pl.ds(r, SEG, stride=MODES), :] = ends[r]
+    power = jnp.exp(-step * rates)
+    enters = [jnp.zeros_like(rates)]
+    for i in range(SEG):
+        enters.append(power * enters[i] + by_segment[pl.ds(MODES * i, MODES), :])
+    return enters[:SEG], enters[SEG]
 
 
 def turned(block):
@@ -320,22 +317,23 @@
     rate_ref,
     amplitude_ref,
     skip_ref,
-    forward_ref,
+    first_ref,
+    second_window_ref,
     spectrum_ref,
-    inverse_ref,
+    first_back_ref,
+    second_back_ref,
     taps_out,
     spectrum_out,
     medium_out,
     query_out,
     key2_out,
-    enter_out,
     leave_out,
-    reach_main_out,
     late_hbm,
     gated_t,
     medium_t,
     query_all,
     key2_all,
+    by_segment,
     late,
     late_sem,
 ):
@@ -343,7 +341,6 @@
     tiles = key_t.shape[0]
     group = gated_t.shape[1] // LANES
     top = sublane((SEG, LANES)) == 0
-    segment = sublane((SEG, LANES)).astype(F32)
 
     def slabs_of(ref, tile):
         head = [ref[tile, pl.ds(k, SEG, stride=HEAD), :] for k in range(HEAD)]
@@ -382,10 +379,12 @@
 
         filters = [taps_t[step * group + part, 0:TAPS, :] for part in range(group)]
         spectrum = matmul3(spectrum_ref[...], jnp.concatenate(filters, 1))
-        both = matmul3(forward_ref[...], gated_t[...])
-        first = spectral_product(both[:T], spectrum)
-        second = spectral_product(both[T:], spectrum)
-        medium_t[...] = matmul3(inverse_ref[...], jnp.concatenate([first, second], 0))
+        high, low = halves(gated_t[...])
+        first = matmul_halves(first_ref[...], high[:EARLY_ROWS], low[:EARLY_ROWS])
+        second = matmul_halves(second_window_ref[...], high, low)
+        medium_t[...] = matmul3(second_back_ref[...], spectral_product(second, spectrum))
+        head = matmul3(first_back_ref[...], spectral_product(first, spectrum))
+        medium_t[0:HEAD_ROWS, :] = medium_t[0:HEAD_ROWS, :] + head[0:HEAD_ROWS]
 
         for part in range(group):
             tile = step * group + part
@@ -415,14 +414,10 @@
             )
             for k in range(MAIN):
                 late[tile, pl.ds(T + SEG * k, SEG), :] = outs[k]
+            enters, leave_out[tile] = prefix(ends, rates, float(MAIN), by_segment.at[part])
+            for i in range(SEG):
+                late[tile, pl.ds(T + MAIN_ROWS + MODES * i, MODES), :] = enters[i]
             pltpu.make_async_copy(late.at[tile], late_hbm.at[tile], late_sem.at[tile]).start()
-            powers = segment_powers(rates, float(MAIN))
-            for r in range(MODES):
-                enter, leave = prefix(ends[r], powers, r)
-                enter_out[tile, r] = enter
-                leave_out[tile, r : r + 1, :] = leave
-                rate = spread(rates[r : r + 1])
-                reach_main_out[tile, r] = jnp.exp(-(rate * (segment * float(MAIN))))
         return _
 
     lax.fori_loop(0, tiles // group, body, 0)
@@ -441,9 +436,7 @@
     key2_ref,
     key_t,
     value_t,
-    enter_main_ref,
     leave_main_ref,
-    reach_main_ref,
     short_ref,
     second_ref,
     rate_ref,
@@ -453,29 +446,32 @@
     inverse_ref,
     *rest,
 ):
-    *before, state_out, late_hbm, medium_t, late, late_sem = rest
     tiles = halo_ref.shape[0]
-    group = medium_t.shape[1] // LANES
+    copies = []
+    if base:
+        state_ref, late_ref, state_out, late_hbm, medium_t, by_segment, late, late_sem = rest
+        state_out[0:base] = state_ref[...]
+        copies.append(
+            pltpu.make_async_copy(late_ref, late_hbm.at[pl.ds(0, base)], late_sem.at[tiles])
+        )
+        copies[0].start()
+    else:
+        state_out, late, medium_t, by_segment = rest
+    group = medium_t.shape[2] // LANES
     top = sublane((SEG, LANES)) == 0
-    for ref in before:
-        state_out[0:base] = ref[...]
-
-    def body(step, _):
+
+    def body(step):
         tile_list = [base + step * group + part for part in range(group)]
         halo = matmul3(
             forward_ref[...], jnp.concatenate([halo_ref[tile - base] for tile in tile_list], 1)
         )
         filters = jnp.concatenate([spectrum_ref[tile] for tile in tile_list], 1)
-        medium_t[...] = matmul3(inverse_ref[...], spectral_product(halo, filters))
+        medium_t[step] = matmul3(inverse_ref[...], spectral_product(halo, filters))
         for part, tile in enumerate(tile_list):
-            one(tile, pl.ds(part * LANES, LANES))
-        return _
-
-    def copy_of(tile):
-        return pltpu.make_async_copy(late.at[tile], late_hbm.at[tile], late_sem.at[tile])
-
-    def one(tile, local):
-        lanes = pl.ds(pl.multiple_of(tile * LANES, LANES), LANES)
+            one(tile, medium_t.at[step], pl.ds(part * LANES, LANES), tile - base)
+
+    def one(tile, medium_t, local, slot):
+        lanes = pl.ds(tile * LANES, LANES)
 
         def rim(k):
             return rims_ref[tile, k : k + 1, :]
@@ -538,22 +534,22 @@
         )
         for k in range(HEAD):
             late[tile - base, pl.ds(SEG * k, SEG), :] = outs[k]
-        powers = segment_powers(rates, float(HEAD))
-        whole = jnp.exp(-float(MAIN_ROWS) * rates)
-        for r in range(MODES):
-            enter, leave = prefix(ends[r], powers, r)
-            late[tile - base, pl.ds(HEAD_ROWS + SEG * r, SEG), :] = enter
-            late[tile - base, pl.ds(HEAD_ROWS + SEG * (MODES + r), SEG), :] = enter_main_ref[
-                tile, r
-            ] + reach_main_ref[tile, r] * spread(leave)
-            state_out[tile, r : r + 1, :] = (
-                leave_main_ref[tile, r : r + 1, :] + leave * whole[r : r + 1]
+        enters, leave = prefix(ends, rates, float(HEAD), by_segment.at[slot])
+        for i in range(SEG):
+            late[tile - base, pl.ds(HEAD_ROWS + MODES * i, MODES), :] = enters[i]
+        late[tile - base, pl.ds(HEAD_ROWS + MODES * SEG, MODES), :] = leave
+        state_out[tile] = leave_main_ref[tile] + leave * jnp.exp(-float(MAIN_ROWS) * rates)
+        if base:
+            copy = pltpu.make_async_copy(
+                late.at[tile - base], late_hbm.at[tile], late_sem.at[tile - base]
             )
-        copy_of(tile - base).start()
-
-    lax.fori_loop(0, tiles // group, body, 0, unroll=True)
-    for tile in range(tiles):
-        copy_of(tile).wait()
+            copy.start()
+            copies.append(copy)
+
+    for step in range(tiles // group):
+        body(step)
+    for copy in copies:
+        copy.wait()
 
 
 def ring_kernel(states_hbm, rate_ref, out_ref, states, sem):
@@ -588,7 +584,6 @@
     state_ref,
     early_hbm,
     late_hbm,
-    later_hbm,
     rims_ref,
     second_ref,
     rate_ref,
@@ -597,7 +592,7 @@
     squares_out,
     early,
     late,
-    reach,
+    by_segment,
     squares_t,
     sems,
 ):
@@ -607,32 +602,17 @@
     copies = []
     for chunk in range(chunks):
         here = pl.ds(chunk * count, count)
-        first = chunk * count
-        if first < late_hbm.shape[0]:
-            joined = late_hbm.at[here]
-        else:
-            joined = later_hbm.at[pl.ds(first - late_hbm.shape[0], count)]
-        for place, (source, target) in enumerate(((early_hbm.at[here], early), (joined, late))):
-            copy = pltpu.make_async_copy(source, target.at[here], sems.at[place, chunk])
+        for place, (source, target) in enumerate(((early_hbm, early), (late_hbm, late))):
+            copy = pltpu.make_async_copy(source.at[here], target.at[here], sems.at[place, chunk])
             copy.start()
             copies.append(copy)
     squares_t[...] = jnp.zeros_like(squares_t)
     top = sublane((SEG, LANES)) == 0
-    segment = sublane((SEG, LANES)).astype(F32)
-
-    def reaches(tile, _):
-        lanes = pl.ds(pl.multiple_of(tile * LANES, LANES), LANES)
-        for r in range(MODES):
-            rate = spread(rate_ref[r : r + 1, lanes])
-            reach[tile, r] = jnp.exp(-(rate * (segment * float(HEAD))))
-            reach[tile, MODES + r] = jnp.exp(-(rate * (segment * float(MAIN) + float(HEAD_ROWS))))
-        return _
-
-    lax.fori_loop(0, tiles, reaches, 0)
-
-    def body(tile, _):
-        lanes = pl.ds(pl.multiple_of(tile * LANES, LANES), LANES)
-        decays = jnp.exp(-rate_ref[:, lanes])
+
+    def body(tile):
+        lanes = pl.ds(tile * LANES, LANES)
+        rates = rate_ref[:, lanes]
+        decays = jnp.exp(-rates)
         taps = [second_ref[0, j : j + 1, lanes] for j in range(3)]
         older, last = rims_ref[tile, 6:7, :], rims_ref[tile, 7:8, :]
         mends = [spread(taps[1] * last + taps[2] * older), spread(taps[2] * last)]
@@ -640,13 +620,15 @@
         states = state_ref[tile]
         decay = [spread(decays[r : r + 1]) for r in range(MODES)]
 
-        def half(length, half_index, own_ref, own_row, first_row):
-            enter_row = HEAD_ROWS + half_index * MODES * SEG
-            carry = [
-                late[tile, pl.ds(enter_row + SEG * r, SEG), :]
-                + reach[tile, half_index * MODES + r] * spread(states[r : r + 1])
-                for r in range(MODES)
-            ]
+        def half(length, entering, enter_ref, enter_row, own_ref, own_row, first_row):
+            step = jnp.exp(-float(length) * rates)
+            slot = 0 if first_row == 0 else 1
+            for i in range(SEG):
+                rows = pl.ds(MODES * i, MODES)
+                enter = enter_ref[tile, pl.ds(enter_row + MODES * i, MODES), :]
+                by_segment[slot, rows, :] = enter + entering
+                entering = step * entering
+            carry = [by_segment[slot, pl.ds(r, SEG, stride=MODES), :] for r in range(MODES)]
             for k in range(length):
                 carry = [decay[r] * carry[r] for r in range(MODES)]
                 total = own_ref[tile, pl.ds(own_row + SEG * k, SEG), :]
@@ -660,14 +642,16 @@
                 squares_t[rows, :] = squares_t[rows, :] + mixed * mixed
                 mixed_out[tile, pl.ds(first_row + k, SEG, stride=length), :] = mixed * gain
 
-        half(HEAD, 0, late, 0, 0)
-        half(MAIN, 1, early, T, HEAD_ROWS)
-        return _
+        leave = late[tile, pl.ds(HEAD_ROWS + MODES * SEG, MODES), :]
+        later = leave + states * jnp.exp(-float(HEAD_ROWS) * rates)
+        half(HEAD, states, late, HEAD_ROWS, late, 0, 0)
+        half(MAIN, later, early, T + MAIN_ROWS, early, T, HEAD_ROWS)
 
     for chunk in range(chunks):
         copies[2 * chunk].wait()
         copies[2 * chunk + 1].wait()
-        lax.fori_loop(chunk * count, (chunk + 1) * count, body, 0)
+        for tile in range(chunk * count, (chunk + 1) * count):
+            body(tile)
     sums = jnp.sum(squares_t[...], axis=1, keepdims=True)
     squares_t[...] = jnp.broadcast_to(sums, squares_t.shape)
     head = [squares_t[pl.ds(i, HEAD, stride=SEG), :] for i in range(SEG)]
@@ -737,8 +721,7 @@
     channels = query_proj.shape[0]
     count = lax.axis_size("seq")
     tiles = channels // LANES
-    group = min(4, tiles)
-    join_group = min(2, tiles)
+    group = min(8, tiles)
     chunks = min(4, tiles)
     parts = (tiles - tiles // chunks, tiles // chunks)
     short_t = jnp.transpose(short_filter, (0, 2, 1))
@@ -747,7 +730,7 @@
     amplitude = residue.T * jnp.sqrt(-jnp.expm1(-2.0 * rate_t))
     skip = skip_gain[None, :]
     gain = norm_gain[None, :]
-    forward, spectrum, inverse, halo_forward, halo_inverse = tables()
+    *windows, halo_forward, halo_inverse = tables()
     held = pl.BlockSpec(memory_space=pltpu.VMEM)
     outside = pl.BlockSpec(memory_space=pl.ANY)
     words = channels * T
@@ -773,7 +756,7 @@
         [struct(parts[0], TAPS, LANES), struct(share, MODES, LANES)],
         [pltpu.VMEM((parts[0] * LANES, LANES), F32)] * 2
         + [pltpu.VMEM((3, 3, channels), F32), pltpu.VMEM((share, MODES, LANES), F32)]
-        + [pltpu.SemaphoreType.DMA((parts[0] // (tiles // chunks),))] * 2
+        + [pltpu.SemaphoreType.DMA((2,))] * 2
         + [pltpu.SemaphoreType.DMA, pltpu.SemaphoreType.DMA((share,))],
         words * 8,
         words * 6,
@@ -797,34 +780,32 @@
     border = from_behind(rims)
     halo_two = from_behind(tail_two)
 
+    early_rows = T + MAIN_ROWS + MODES * SEG
     (
         taps,
         tap_spectrum,
         medium,
         query,
         key2,
-        enter_main,
         leave_main,
-        reach_main,
         early,
     ) = call(
         local_kernel,
-        [held] * 14,
-        [held] * 8 + [outside],
+        [held] * (11 + len(windows)),
+        [held] * 6 + [outside],
         [
             struct(tiles, HEAD_ROWS, LANES),
             struct(tiles, 384, LANES),
             struct(tiles, HEAD_ROWS, LANES),
             struct(tiles, HEAD_ROWS, LANES),
             struct(tiles, HEAD_ROWS, LANES),
-            struct(tiles, MODES, SEG, LANES),
             struct(tiles, MODES, LANES),
-            struct(tiles, MODES, SEG, LANES),
-            hbm(tiles, T + MAIN_ROWS, LANES),
+            hbm(tiles, early_rows, LANES),
         ],
         [pltpu.VMEM((T, group * LANES), F32)] * 2
         + [pltpu.VMEM((group, T, LANES), F32)] * 2
-        + [pltpu.VMEM((tiles, T + MAIN_ROWS, LANES), F32), pltpu.SemaphoreType.DMA((tiles,))],
+        + [pltpu.VMEM((group, MODES * SEG, LANES), F32)]
+        + [pltpu.VMEM((tiles, early_rows, LANES), F32), pltpu.SemaphoreType.DMA((tiles,))],
         words * 8000,
         words * 60,
         "local",
@@ -836,27 +817,30 @@
         rate_t,
         amplitude,
         skip,
-        forward,
-        spectrum,
-        inverse,
+        *windows,
     )
 
-    late_rows = HEAD_ROWS + 2 * MODES * SEG
-    state, late = (), []
+    late_rows = HEAD_ROWS + MODES * SEG + MODES
+    joined = ()
     for base, part in zip((0, parts[0]), (halo, halo_two)):
-        count_here = part.shape[0]
-        *state, joined = call(
+        here = part.shape[0]
+        join_group = 2 if base else 4
+        late_shape = (base + here, late_rows, LANES)
+        scratch = [
+            pltpu.VMEM((here // join_group, HEAD_ROWS + 8, join_group * LANES), F32),
+            pltpu.VMEM((here, MODES * SEG, LANES), F32),
+        ]
+        if base:
+            scratch.append(pltpu.VMEM((here, late_rows, LANES), F32))
+            scratch.append(pltpu.SemaphoreType.DMA((here + 1,)))
+        joined = call(
             functools.partial(join_kernel, base),
-            [held] * (19 + len(state)),
-            [held, outside],
-            [struct(base + count_here, MODES, LANES), hbm(count_here, late_rows, LANES)],
-            [
-                pltpu.VMEM((HEAD_ROWS + 8, join_group * LANES), F32),
-                pltpu.VMEM((count_here, late_rows, LANES), F32),
-                pltpu.SemaphoreType.DMA((count_here,)),
-            ],
-            count_here * 500 * T * LANES,
-            count_here * 20 * T * LANES,
+            [held] * (17 + len(joined)),
+            [held, outside if base else held],
+            [struct(base + here, MODES, LANES), (hbm if base else struct)(*late_shape)],
+            scratch,
+            here * 500 * T * LANES,
+            here * 20 * T * LANES,
             "join",
         )(
             part,
@@ -868,9 +852,7 @@
             key2,
             turned_fields[0],
             turned_fields[1],
-            enter_main,
             leave_main,
-            reach_main,
             short_t,
             second_t,
             rate_t,
@@ -878,10 +860,9 @@
             skip,
             halo_forward,
             halo_inverse,
-            *state,
+            *joined,
         )
-        late.append(in_hbm(joined))
-    (state,) = state
+    state, late = joined
 
     share_shape = (RING, share, MODES, LANES)
     ring_states = in_hbm(exchange(state.reshape(share_shape), ring_groups))
@@ -909,20 +890,20 @@
 
     mixed, squares = call(
         finish_kernel,
-        [held] + [outside] * 3 + [held] * 4,
+        [held] + [outside] * 2 + [held] * 4,
         [held] * 2,
         [struct(tiles, T, LANES), struct(1, T)],
         [
-            pltpu.VMEM((tiles, T + MAIN_ROWS, LANES), F32),
+            pltpu.VMEM((tiles, early_rows, LANES), F32),
             pltpu.VMEM((tiles, late_rows, LANES), F32),
-            pltpu.VMEM((tiles, 2 * MODES, SEG, LANES), F32),
+            pltpu.VMEM((2, MODES * SEG, LANES), F32),
             pltpu.VMEM((T, LANES), F32),
-            pltpu.SemaphoreType.DMA((2, chunks)),
+            pltpu.SemaphoreType.DMA((2, 2 * chunks)),
         ],
         words * 40,
         words * 16,
         "finish",
-    )(incoming, in_hbm(early), *late, border, second_t, rate_t, gain)
+    )(incoming, in_hbm(early), in_hbm(late), border, second_t, rate_t, gain)
     total = lax.psum(squares, "chan")
     return call(
         functools.partial(scale_kernel, float(channels * lax.axis_size("chan"))),

time: 87.7 us -> 87.7 us (level)
  Pallas kernels: 30 us -> 26.6 us
  blocking collectives: 45.4 us -> 47.8 us
  waiting for transfers between devices: 0.01 us -> 0.89 us
    pallas_call x4, Pallas kernels: 19.2 us -> 15.9 us  [the longest x1 7.98 us: local(): call(local_kernel, [held] * (11 + len(windows)), [held] * 6 + [outside],...]
    all_to_all x3, blocking collectives: 37.8 us -> 40.2 us  [exchange(): lax.all_to_all(rows, 'seq', split_axis=0, concat_axis=0, axis_index_group...]
    ppermute x3, waiting for transfers between devices: 0.01 us -> 0.89 us  [from_behind(): return lax.ppermute(block, 'seq', [(i, i + 1) for i in range(count - 1)])]
  transfers between devices with their start and end apart: 3 -> 3, of which waited for: 0 -> 1; matrix products, arithmetic and copies ran while one was open for 0% -> 0% of each run, Pallas kernels for 22% -> 19%
where the time goes in v6:
time: 87.7 us; the launch traced here: 87.3 us
  blocking collectives  47.8 us (55%)
  Pallas kernels  26.6 us (30%)
  starting transfers between devices  11.5 us (13%)
  waiting for transfers between devices  0.89 us (1%)
    all_to_all x3, blocking collectives, exchange(): lax.all_to_all(rows, 'seq', split_axis=0, concat_axis=0, axis_index_group...  40.2 us
    ppermute x3, starting transfers between devices, from_behind(): return lax.ppermute(block, 'seq', [(i, i + 1) for i in range(count - 1)])  11.5 us
    pallas_call x1, Pallas kernels, local(): call(local_kernel, [held] * (11 + len(windows)), [held] * 6 + [outside],...  7.98 us
    psum x1, blocking collectives, local(): total = lax.psum(squares, 'chan')  7.57 us
    pallas_call x1, Pallas kernels, local(): call(prep_kernel, [outside] * 6 + [held] * 2, [held] * 8, [struct(tiles,...  5.5 us
    pallas_call x2, Pallas kernels, local(): call(functools.partial(join_kernel, base), [held] * (17 + len(joined)), [...  4.72 us
    pallas_call x1, Pallas kernels, local(): call(finish_kernel, [held] + [outside] * 2 + [held] * 4, [held] * 2, [str...  3.2 us
    pallas_call x1, Pallas kernels, local(): call(tail_kernel, [pl.BlockSpec(memory_space=pltpu.SMEM)] + [outside] * 4...  1.88 us
  transfers between devices with their start and end apart: 3, of which 1 were waited for; matrix products, arithmetic and copies ran while one was open for 0% of the time, Pallas kernels for 19%

profile of v6, /device:TPU:1, one launch (start us, length us, event | category | flops | bytes accessed | tf_op | source)
XLA Modules:
  0.0 87.3 jit_solution(2706345688153266066)
XLA Ops:
  0.0 0.0 copy-start.1
  0.0 1.9 %tail.1 = (f32[12,128,128]{2,1,0:T(8,128)S(1)}, f32[2,8,128]{2,1,0:T(8,128)S(1)}) custom-call(s32[1]{0:T(128)} %bitcast.place_ref, f32[2048,256]{1,0:T(8,128)} %key_hbm.3, f32[2048,256]{1,0:T(8,128)} %value_hbm.3, f32[3,3,2048]{2,1,0:T(4,128)} %bitcast.16, f32[8,2048]{1,0:T(8,128)} %bitcast.11), custom_call_target="tpu_custom_call" | custom-call | flops 4194304 | bytes 3145728 | tf_op jit(solution)/shard_map/tail/pallas_call | solution.py:752
  1.9 4.4 %collective-permute-start.2 = (f32[12,128,128]{2,1,0:T(8,128)S(1)}, f32[12,128,128]{2,1,0:T(8,128)S(1)}, u32[]{:S(2)}, u32[]{:S(2)}) collective-permute-start(f32[12,128,128]{2,1,0:T(8,128)S(1)} %get-tuple-element.43), channel_id=1, source_target_pairs={{0,2},{2,4},{4,6},{6,8},{8,10},{10,12},{12,14},{14,16},{16,18},{18... | collective-permute-start | bytes 2359304 | tf_op jit(solution)/shard_map/ppermute | solution.py:681
  6.3 0.0 copy-done.1
  6.3 0.0 copy-start
  6.3 0.0 copy-start.12
  6.3 0.0 copy-start.3
  6.4 0.0 copy-start.5
  6.4 0.0 copy-start.7
  6.4 0.0 copy-start.8
  6.4 0.0 copy-start.9
  6.4 0.0 copy-start.10
  6.4 0.0 copy-start.11
  6.4 5.5 %prep.1 = (f32[16,256,128]{2,1,0:T(8,128)S(1)}, f32[16,256,128]{2,1,0:T(8,128)S(1)}, f32[16,256,128]{2,1,0:T(8,128)S(1)}, f32[16,256,128]{2,1,0:T(8,128)S(1)}, f...) custom-call(f32[2048,256]{1,0:T(8,128)} %key_hbm.3, ...), custom_call_target="tpu_custom_call" | custom-call | flops 10485760 | bytes 20971520 | tf_op jit(solution)/shard_map/prep/pallas_call | solution.py:767
  11.9 3.5 %collective-permute-start.1 = (f32[16,16,128]{2,1,0:T(8,128)S(1)}, f32[16,16,128]{2,1,0:T(8,128)S(1)}, u32[]{:S(2)}, u32[]{:S(2)}) collective-permute-start(f32[16,16,128]{2,1,0:T(8,128)S(1)} %get-tuple-element.30), channel_id=1, source_target_pairs={{0,2},{2,4},{4,6},{6,8},{8,10},{10,12},{12,14},{14,16},{16,18},{18... | collective-permute-start | bytes 393224 | tf_op jit(solution)/shard_map/ppermute | solution.py:681
  15.5 3.6 %collective-permute-start = (f32[4,128,128]{2,1,0:T(8,128)S(1)}, f32[4,128,128]{2,1,0:T(8,128)S(1)}, u32[]{:S(2)}, u32[]{:S(2)}) collective-permute-start(f32[4,128,128]{2,1,0:T(8,128)S(1)} %get-tuple-element.29), channel_id=1, source_target_pairs={{0,2},{2,4},{4,6},{6,8},{8,10},{10,12},{12,14},{14,16},{16,18},{18... | collective-permute-start | bytes 786440 | tf_op jit(solution)/shard_map/ppermute | solution.py:681
  19.0 0.0 copy-done
  19.0 0.0 copy-done.12
  19.1 0.0 copy-done.3
  19.1 0.0 copy-done.5
  19.1 0.0 copy-done.7
  19.1 0.0 copy-done.8
  19.1 0.0 copy-done.9
  19.1 0.0 copy-done.10
  19.2 0.0 copy-done.11
  19.2 0.0 copy-start.2
  19.2 0.0 copy-start.4
  19.2 8.0 %local.1 = (f32[16,136,128]{2,1,0:T(8,128)S(1)}, f32[16,384,128]{2,1,0:T(8,128)S(1)}, f32[16,136,128]{2,1,0:T(8,128)S(1)}, f32[16,136,128]{2,1,0:T(8,128)S(1)}, ...) custom-call(f32[16,256,128]{2,1,0:T(8,128)S(1)} %get-tuple-element.31.key_t, ...), custom_call_target="tpu_custom_call" | custom-call | flops 4194304000 | bytes 31457280 | tf_op jit(solution)/shard_map/local/pallas_call | solution.py:792
  27.2 0.0 collective-permute-done.1.rims_ref
  27.2 0.0 collective-permute-done.2.halo_ref
  27.2 0.0 copy-done.2
  27.2 0.0 copy-done.4
  27.2 2.8 %join.2 = (f32[12,8,128]{2,1,0:T(8,128)S(1)}, f32[12,208,128]{2,1,0:T(8,128)S(1)}) custom-call(f32[12,128,128]{2,1,0:T(8,128)S(1)} %collective-permute-done.2.halo_ref, f32[16,16,128]{2,1,0:T(8,128)S(1)} %collective-permute-done.1.rims_ref, f32[16,384,128]{2,1,0:T(8,128)S(1)} %get-tuple-element.37.spectrum_ref, ...), custom_call_target="tpu_custom_call" | custom-call | flops 196608000 | bytes 7864320 | tf_op jit(solution)/shard_map/join/pallas_call | solution.py:836
  30.0 0.9 %collective-permute-done.halo_ref = f32[4,128,128]{2,1,0:T(8,128)S(1)} collective-permute-done((f32[4,128,128]{2,1,0:T(8,128)S(1)}, f32[4,128,128]{2,1,0:T(8,128)S(1)}, u32[]{:S(2)}, u32[]{:S(2)}) %collective-permute-start) | collective-permute-done | bytes 262176 | tf_op jit(solution)/shard_map/ppermute | solution.py:681
  30.9 0.0 copy-start.6
  30.9 1.9 %join.3 = (f32[16,8,128]{2,1,0:T(8,128)S(1)}, f32[16,208,128]{2,1,0:T(8,128)}) custom-call(f32[4,128,128]{2,1,0:T(8,128)S(1)} %collective-permute-done.halo_ref, f32[16,16,128]{2,1,0:T(8,128)S(1)} %collective-permute-done.1.rims_ref, f32[16,384,128]{2,1,0:T(8,128)S(1)} %get-tuple-element.37.spectrum_ref, f32[16,136,128]{2,1,0:T(8,128)S(1)} %get-tuple-element.38.medium_ref, ...), custom_call_target="tpu_custom_call" | custom-call | flops 65536000 | bytes 2621440 | tf_op jit(solution)/shard_map/join/pallas_call | solution.py:836
  32.8 17.2 %all_to_all.15.states_hbm = f32[8,2,8,128]{3,2,1,0:T(8,128)} all-to-all(f32[8,2,8,128]{3,2,1,0:T(8,128)S(1)} %bitcast.26), channel_id=1, replica_groups={{0,2,4,6,8,10,12,14},{16,18,20,22,24,26,28,30},{32,34,36,38,40,42,44,46..., dimensions={0} | all-to-all | bytes 131072 | tf_op jit(solution)/shard_map/all_to_all | solution.py:702
  50.0 0.9 ring.1
  50.9 13.4 %all_to_all.16.rings_ref = f32[16,2,8,128]{3,2,1,0:T(8,128)S(1)} all-to-all(f32[16,2,8,128]{3,2,1,0:T(8,128)S(1)} %ring.1), channel_id=1, replica_groups={{0,16,32,48,64,80,96,112,128,144,160,176,192,208,224,240},{2,18,34,50,6..., dimensions={0} | all-to-all | bytes 262144 | tf_op jit(solution)/shard_map/all_to_all | solution.py:702
  64.3 0.9 scan.1
  65.2 9.6 %all_to_all.17 = f32[8,2,8,128]{3,2,1,0:T(8,128)S(1)} all-to-all(f32[8,2,8,128]{3,2,1,0:T(8,128)S(1)} %scan.1), channel_id=1, replica_groups={{0,2,4,6,8,10,12,14},{16,18,20,22,24,26,28,30},{32,34,36,38,40,42,44,46..., dimensions={0} | all-to-all | bytes 131072 | tf_op jit(solution)/shard_map/all_to_all | solution.py:702
  74.8 0.0 copy-done.6
  74.8 3.2 %finish.1 = (f32[16,256,128]{2,1,0:T(8,128)S(1)}, f32[1,256]{1,0:T(1,128)S(1)}) custom-call(f32[16,8,128]{2,1,0:T(8,128)S(1)} %bitcast.25, f32[16,440,128]{2,1,0:T(8,128)} %get-tuple-element.47.early_hbm, f32[16,208,128]{2,1,0:T(8,128)} %get-tuple-element.48.late_hbm, f32[16,16,128]{2,1,0:T(8,128)S(1)} %collective-permute-done.1.rims_ref, ...), custom_call_target="tpu_custom_call" | custom-call | flops 20971520 | bytes 8388608 | tf_op jit(solution)/shard_map/finish/pallas_call | solution.py:891
  78.0 7.6 %psum.7.squares_ref = f32[1,256]{1,0:T(1,128)S(1)} all-reduce(f32[1,256]{1,0:T(1,128)S(1)} %get-tuple-element.50), channel_id=1, replica_groups=mesh['seq'=128,'chan'=2] {'chan'}, use_global_device_ids=true, to_apply=%region_0.0 | all-reduce | flops 256 | bytes 2048 | tf_op jit(solution)/shard_map/psum | solution.py:907
  85.6 1.5 %scale.1 = f32[2048,256]{1,0:T(8,128)} custom-call(f32[16,256,128]{2,1,0:T(8,128)S(1)} %get-tuple-element.49.mixed_ref, f32[1,256]{1,0:T(1,128)S(1)} %psum.7.squares_ref), custom_call_target="tpu_custom_call" | custom-call | flops 524288 | bytes 4194304 | tf_op jit(solution)/shard_map/scale/pallas_call | solution.py:908
  (1 shorter events, 0.0 us)
Async XLA Ops:
  0.0 6.3 %copy-start.1 = (f32[3,2048,3]{1,2,0:T(4,128)S(1)}, f32[3,2048,3]{1,2,0:T(4,128)}, u32[]{:S(2)}) copy-start(f32[3,2048,3]{1,2,0:T(4,128)} %param.24) | copy-start | bytes 221188
  1.9 25.3 %collective-permute-start.2 = (f32[12,128,128]{2,1,0:T(8,128)S(1)}, f32[12,128,128]{2,1,0:T(8,128)S(1)}, u32[]{:S(2)}, u32[]{:S(2)}) collective-permute-start(f32[12,128,128]{2,1,0:T(8,128)S(1)} %get-tuple-element.43), channel_id=1, source_target_pairs={{0,2},{2,4},{4,6},{6,8},{8,10},{10,12},{12,14},{14,16},{16,18},{18... | collective-permute-start | bytes 2359304 | tf_op jit(solution)/shard_map/ppermute | solution.py:681
  6.3 12.7 %copy-start = (f32[2048,8]{0,1:T(8,128)S(1)}, f32[2048,8]{0,1:T(8,128)}, u32[]{:S(2)}) copy-start(f32[2048,8]{0,1:T(8,128)} %param.27) | copy-start | bytes 196612
  6.3 12.7 %copy-start.12 = (f32[2048,8]{0,1:T(8,128)S(1)}, f32[2048,8]{0,1:T(8,128)}, u32[]{:S(2)}) copy-start(f32[2048,8]{0,1:T(8,128)} %param.28) | copy-start | bytes 196612
  6.3 12.7 %copy-start.3 = (f32[3,2048,3]{1,2,0:T(4,128)S(1)}, f32[3,2048,3]{1,2,0:T(4,128)}, u32[]{:S(2)}) copy-start(f32[3,2048,3]{1,2,0:T(4,128)} %param.25) | copy-start | bytes 221188
  6.4 12.7 %copy-start.5 = (f32[2048]{0:T(1024)S(1)}, f32[2048]{0:T(1024)}, u32[]{:S(2)}) copy-start(f32[2048]{0:T(1024)} %param.29) | copy-start | bytes 24580
  6.4 12.7 %copy-start.7 = (bf16[256,768]{1,0:T(8,128)(2,1)S(1)}, bf16[256,768]{1,0:T(8,128)(2,1)}, u32[]{:S(2)}) copy-start(bf16[256,768]{1,0:T(8,128)(2,1)} %constant.26.clone.second_back_ref) | copy-start | bytes 1179652
  6.4 12.7 %copy-start.8 = (bf16[256,768]{1,0:T(8,128)(2,1)S(1)}, bf16[256,768]{1,0:T(8,128)(2,1)}, u32[]{:S(2)}) copy-start(bf16[256,768]{1,0:T(8,128)(2,1)} %constant.23.clone.second_window_ref) | copy-start | bytes 1179652
  6.4 12.7 %copy-start.9 = (bf16[384,384]{1,0:T(8,128)(2,1)S(1)}, bf16[384,384]{1,0:T(8,128)(2,1)}, u32[]{:S(2)}) copy-start(bf16[384,384]{1,0:T(8,128)(2,1)} %constant.24.clone.spectrum_ref) | copy-start | bytes 884740
  6.4 12.7 %copy-start.10 = (bf16[256,432]{1,0:T(8,128)(2,1)S(1)}, bf16[256,432]{1,0:T(8,128)(2,1)}, u32[]{:S(2)}) copy-start(bf16[256,432]{1,0:T(8,128)(2,1)} %constant.22.clone.first_ref) | copy-start | bytes 663556
  6.4 12.7 %copy-start.11 = (bf16[144,768]{1,0:T(8,128)(2,1)S(1)}, bf16[144,768]{1,0:T(8,128)(2,1)}, u32[]{:S(2)}) copy-start(bf16[144,768]{1,0:T(8,128)(2,1)} %constant.25.clone.first_back_ref) | copy-start | bytes 663556
  11.9 15.2 %collective-permute-start.1 = (f32[16,16,128]{2,1,0:T(8,128)S(1)}, f32[16,16,128]{2,1,0:T(8,128)S(1)}, u32[]{:S(2)}, u32[]{:S(2)}) collective-permute-start(f32[16,16,128]{2,1,0:T(8,128)S(1)} %get-tuple-element.30), channel_id=1, source_target_pairs={{0,2},{2,4},{4,6},{6,8},{8,10},{10,12},{12,14},{14,16},{16,18},{18... | collective-permute-start | bytes 393224 | tf_op jit(solution)/shard_map/ppermute | solution.py:681
  15.5 15.4 %collective-permute-start = (f32[4,128,128]{2,1,0:T(8,128)S(1)}, f32[4,128,128]{2,1,0:T(8,128)S(1)}, u32[]{:S(2)}, u32[]{:S(2)}) collective-permute-start(f32[4,128,128]{2,1,0:T(8,128)S(1)} %get-tuple-element.29), channel_id=1, source_target_pairs={{0,2},{2,4},{4,6},{6,8},{8,10},{10,12},{12,14},{14,16},{16,18},{18... | collective-permute-start | bytes 786440 | tf_op jit(solution)/shard_map/ppermute | solution.py:681
  19.2 8.0 %copy-start.2 = (bf16[144,768]{1,0:T(8,128)(2,1)S(1)}, bf16[144,768]{1,0:T(8,128)(2,1)}, u32[]{:S(2)}) copy-start(bf16[144,768]{1,0:T(8,128)(2,1)} %constant.28.clone.inverse_ref) | copy-start | bytes 663556
  19.2 8.0 %copy-start.4 = (bf16[256,384]{1,0:T(8,128)(2,1)S(1)}, bf16[256,384]{1,0:T(8,128)(2,1)}, u32[]{:S(2)}) copy-start(bf16[256,384]{1,0:T(8,128)(2,1)} %constant.27.clone.forward_ref) | copy-start | bytes 589828
  30.9 43.9 %copy-start.6 = (f32[2048]{0:T(1024)S(1)}, f32[2048]{0:T(1024)}, u32[]{:S(2)}) copy-start(f32[2048]{0:T(1024)} %param.30) | copy-start | bytes 24580

commit v7 on v6

--- a/solution.py
+++ b/solution.py
@@ -183,7 +183,8 @@
     rate_sem,
 ):
     chunks = key_sem.shape[0]
-    rows = key_in.shape[0] // chunks
+    tiles = tail_ref.shape[0]
+    bounds = [chunk * tiles // chunks for chunk in range(chunks + 1)]
     copies = []
     filters = pltpu.make_async_copy(short_hbm, short_ref, short_sem)
     filters.start()
@@ -197,7 +198,7 @@
         copy.start()
         rates.append(copy)
     for chunk in range(chunks):
-        here = pl.ds(chunk * rows, rows)
+        here = pl.ds(bounds[chunk] * LANES, (bounds[chunk + 1] - bounds[chunk]) * LANES)
         for source, target, sem in (
             (key_hbm, key_in, key_sem),
             (value_hbm, value_in, value_sem),
@@ -211,7 +212,7 @@
     for chunk in range(chunks):
         copies[2 * chunk].wait()
         copies[2 * chunk + 1].wait()
-        for tile in range(chunk * rows // LANES, (chunk + 1) * rows // LANES):
+        for tile in range(bounds[chunk], bounds[chunk + 1]):
             lanes = pl.ds(tile * LANES, LANES)
 
             def feature(ref, index):
@@ -406,17 +407,20 @@
             ]
             rates, gains = rate_ref[:, lanes], amplitude_ref[:, lanes]
             decays = jnp.exp(-rates)
+            decay = [spread(decays[r : r + 1]) for r in range(MODES)]
             outs, ends = recurrence(
                 inputs,
-                [spread(decays[r : r + 1]) for r in range(MODES)],
+                decay,
                 [spread(gains[r : r + 1]) for r in range(MODES)],
                 spread(skip_ref[:, lanes]),
             )
-            for k in range(MAIN):
-                late[tile, pl.ds(T + SEG * k, SEG), :] = outs[k]
             enters, leave_out[tile] = prefix(ends, rates, float(MAIN), by_segment.at[part])
             for i in range(SEG):
-                late[tile, pl.ds(T + MAIN_ROWS + MODES * i, MODES), :] = enters[i]
+                by_segment[part, pl.ds(MODES * i, MODES), :] = enters[i]
+            carry = [by_segment[part, pl.ds(r, SEG, stride=MODES), :] for r in range(MODES)]
+            for k in range(MAIN):
+                carry = [decay[r] * carry[r] for r in range(MODES)]
+                late[tile, pl.ds(T + SEG * k, SEG), :] = sum(carry, outs[k])
             pltpu.make_async_copy(late.at[tile], late_hbm.at[tile], late_sem.at[tile]).start()
         return _
 
@@ -457,16 +461,17 @@
         copies[0].start()
     else:
         state_out, late, medium_t, by_segment = rest
-    group = medium_t.shape[2] // LANES
+    steps = medium_t.shape[0]
     top = sublane((SEG, LANES)) == 0
 
     def body(step):
-        tile_list = [base + step * group + part for part in range(group)]
+        tile_list = list(range(base + step * tiles // steps, base + (step + 1) * tiles // steps))
+        width = len(tile_list) * LANES
         halo = matmul3(
             forward_ref[...], jnp.concatenate([halo_ref[tile - base] for tile in tile_list], 1)
         )
         filters = jnp.concatenate([spectrum_ref[tile] for tile in tile_list], 1)
-        medium_t[step] = matmul3(inverse_ref[...], spectral_product(halo, filters))
+        medium_t[step, :, 0:width] = matmul3(inverse_ref[...], spectral_product(halo, filters))
         for part, tile in enumerate(tile_list):
             one(tile, medium_t.at[step], pl.ds(part * LANES, LANES), tile - base)
 
@@ -546,17 +551,14 @@
             copy.start()
             copies.append(copy)
 
-    for step in range(tiles // group):
+    for step in range(steps):
         body(step)
     for copy in copies:
         copy.wait()
 
 
-def ring_kernel(states_hbm, rate_ref, out_ref, states, sem):
-    copy = pltpu.make_async_copy(states_hbm, states, sem)
-    copy.start()
+def ring_kernel(states, rate_ref, out_ref):
     decay = jnp.exp(-float(T) * rate_ref[...])
-    copy.wait()
     total = states[0]
     for k in range(1, states.shape[0]):
         total = decay * total + states[k]
@@ -620,13 +622,12 @@
         states = state_ref[tile]
         decay = [spread(decays[r : r + 1]) for r in range(MODES)]
 
-        def half(length, entering, enter_ref, enter_row, own_ref, own_row, first_row):
+        def half(length, entering, enters, own_ref, own_row, first_row):
             step = jnp.exp(-float(length) * rates)
             slot = 0 if first_row == 0 else 1
             for i in range(SEG):
                 rows = pl.ds(MODES * i, MODES)
-                enter = enter_ref[tile, pl.ds(enter_row + MODES * i, MODES), :]
-                by_segment[slot, rows, :] = enter + entering
+                by_segment[slot, rows, :] = enters[i] + entering if enters else entering
                 entering = step * entering
             carry = [by_segment[slot, pl.ds(r, SEG, stride=MODES), :] for r in range(MODES)]
             for k in range(length):
@@ -644,8 +645,9 @@
 
         leave = late[tile, pl.ds(HEAD_ROWS + MODES * SEG, MODES), :]
         later = leave + states * jnp.exp(-float(HEAD_ROWS) * rates)
-        half(HEAD, states, late, HEAD_ROWS, late, 0, 0)
-        half(MAIN, later, early, T + MAIN_ROWS, early, T, HEAD_ROWS)
+        enters = [late[tile, pl.ds(HEAD_ROWS + MODES * i, MODES), :] for i in range(SEG)]
+        half(HEAD, states, enters, late, 0, 0)
+        half(MAIN, later, None, early, T, HEAD_ROWS)
 
     for chunk in range(chunks):
         copies[2 * chunk].wait()
@@ -723,7 +725,8 @@
     tiles = channels // LANES
     group = min(8, tiles)
     chunks = min(4, tiles)
-    parts = (tiles - tiles // chunks, tiles // chunks)
+    second = max(1, tiles * 3 // 16)
+    parts = (tiles - second, second)
     short_t = jnp.transpose(short_filter, (0, 2, 1))
     second_t = jnp.transpose(second_short, (0, 2, 1))
     rate_t = decay_rate.T
@@ -780,7 +783,7 @@
     border = from_behind(rims)
     halo_two = from_behind(tail_two)
 
-    early_rows = T + MAIN_ROWS + MODES * SEG
+    early_rows = T + MAIN_ROWS
     (
         taps,
         tap_spectrum,
@@ -824,10 +827,10 @@
     joined = ()
     for base, part in zip((0, parts[0]), (halo, halo_two)):
         here = part.shape[0]
-        join_group = 2 if base else 4
+        join_steps = min(here, 1 if base else 2)
         late_shape = (base + here, late_rows, LANES)
         scratch = [
-            pltpu.VMEM((here // join_group, HEAD_ROWS + 8, join_group * LANES), F32),
+            pltpu.VMEM((join_steps, HEAD_ROWS + 8, -(-here // join_steps) * LANES), F32),
             pltpu.VMEM((here, MODES * SEG, LANES), F32),
         ]
         if base:
@@ -865,13 +868,13 @@
     state, late = joined
 
     share_shape = (RING, share, MODES, LANES)
-    ring_states = in_hbm(exchange(state.reshape(share_shape), ring_groups))
+    ring_states = exchange(state.reshape(share_shape), ring_groups)
     totals = call(
         ring_kernel,
-        [outside, held],
+        [held, held],
         held,
         struct(rings, share, MODES, LANES),
-        [pltpu.VMEM(share_shape, F32), pltpu.SemaphoreType.DMA],
+        [],
         count * LANES * 30,
         count * LANES * 8,
         "ring",
@@ -885,7 +888,7 @@
         count * LANES * 30,
         count * LANES * 8,
         "scan",
-    )(place, ring_states, exchange(totals, across_groups), own_rate)
+    )(place, in_hbm(ring_states), exchange(totals, across_groups), own_rate)
     incoming = exchange(scanned, ring_groups).reshape(tiles, MODES, LANES)
 
     mixed, squares = call(

time: 87.7 us -> 86.3 us (0.984)
  transfers between devices with their start and end apart: 3 -> 3, of which waited for: 1 -> 1; matrix products, arithmetic and copies ran while one was open for 0% -> 0% of each run, Pallas kernels for 19% -> 20%
where the time goes in v7:
time: 86.3 us; the launch traced here: 86 us
  blocking collectives  47.7 us (55%)
  Pallas kernels  25.9 us (30%)
  starting transfers between devices  11.5 us (13%)
    all_to_all x3, blocking collectives, exchange(): lax.all_to_all(rows, 'seq', split_axis=0, concat_axis=0, axis_index_group...  40.1 us
    ppermute x3, starting transfers between devices, from_behind(): return lax.ppermute(block, 'seq', [(i, i + 1) for i in range(count - 1)])  11.5 us
    pallas_call x1, Pallas kernels, local(): call(local_kernel, [held] * (11 + len(windows)), [held] * 6 + [outside],...  8.48 us
    psum x1, blocking collectives, local(): total = lax.psum(squares, 'chan')  7.58 us
    pallas_call x1, Pallas kernels, local(): call(prep_kernel, [outside] * 6 + [held] * 2, [held] * 8, [struct(tiles,...  5.51 us
    pallas_call x2, Pallas kernels, local(): call(functools.partial(join_kernel, base), [held] * (17 + len(joined)), [...  4.39 us
    pallas_call x1, Pallas kernels, local(): call(finish_kernel, [held] + [outside] * 2 + [held] * 4, [held] * 2, [str...  3.18 us
    pallas_call x1, Pallas kernels, local(): call(tail_kernel, [pl.BlockSpec(memory_space=pltpu.SMEM)] + [outside] * 4...  1.92 us
  transfers between devices with their start and end apart: 3, of which 1 were waited for; matrix products, arithmetic and copies ran while one was open for 0% of the time, Pallas kernels for 20%

profile of v7, /device:TPU:1, one launch (start us, length us, event | category | flops | bytes accessed | tf_op | source)
XLA Modules:
  0.0 86.0 jit_solution(6036523867603960505)
XLA Ops:
  0.0 0.0 copy-start.1
  0.0 1.9 %tail.1 = (f32[13,128,128]{2,1,0:T(8,128)S(1)}, f32[2,8,128]{2,1,0:T(8,128)S(1)}) custom-call(s32[1]{0:T(128)} %bitcast.place_ref, f32[2048,256]{1,0:T(8,128)} %key_hbm.3, f32[2048,256]{1,0:T(8,128)} %value_hbm.3, f32[3,3,2048]{2,1,0:T(4,128)} %bitcast.16, f32[8,2048]{1,0:T(8,128)} %bitcast.11), custom_call_target="tpu_custom_call" | custom-call | flops 4194304 | bytes 3145728 | tf_op jit(solution)/shard_map/tail/pallas_call | solution.py:755
  1.9 4.4 %collective-permute-start.2 = (f32[13,128,128]{2,1,0:T(8,128)S(1)}, f32[13,128,128]{2,1,0:T(8,128)S(1)}, u32[]{:S(2)}, u32[]{:S(2)}) collective-permute-start(f32[13,128,128]{2,1,0:T(8,128)S(1)} %get-tuple-element.43), channel_id=1, source_target_pairs={{0,2},{2,4},{4,6},{6,8},{8,10},{10,12},{12,14},{14,16},{16,18},{18... | collective-permute-start | bytes 2555912 | tf_op jit(solution)/shard_map/ppermute | solution.py:683
  6.4 0.0 copy-done.1
  6.4 0.0 copy-start
  6.4 0.0 copy-start.13
  6.4 0.0 copy-start.3
  6.4 0.0 copy-start.6
  6.4 0.0 copy-start.8
  6.4 0.0 copy-start.9
  6.4 0.0 copy-start.10
  6.5 0.0 copy-start.11
  6.5 0.0 copy-start.12
  6.5 5.5 %prep.1 = (f32[16,256,128]{2,1,0:T(8,128)S(1)}, f32[16,256,128]{2,1,0:T(8,128)S(1)}, f32[16,256,128]{2,1,0:T(8,128)S(1)}, f32[16,256,128]{2,1,0:T(8,128)S(1)}, f...) custom-call(f32[2048,256]{1,0:T(8,128)} %key_hbm.3, ...), custom_call_target="tpu_custom_call" | custom-call | flops 10485760 | bytes 20971520 | tf_op jit(solution)/shard_map/prep/pallas_call | solution.py:770
  12.0 3.5 %collective-permute-start.1 = (f32[16,16,128]{2,1,0:T(8,128)S(1)}, f32[16,16,128]{2,1,0:T(8,128)S(1)}, u32[]{:S(2)}, u32[]{:S(2)}) collective-permute-start(f32[16,16,128]{2,1,0:T(8,128)S(1)} %get-tuple-element.30), channel_id=1, source_target_pairs={{0,2},{2,4},{4,6},{6,8},{8,10},{10,12},{12,14},{14,16},{16,18},{18... | collective-permute-start | bytes 393224 | tf_op jit(solution)/shard_map/ppermute | solution.py:683
  15.5 3.5 %collective-permute-start = (f32[3,128,128]{2,1,0:T(8,128)S(1)}, f32[3,128,128]{2,1,0:T(8,128)S(1)}, u32[]{:S(2)}, u32[]{:S(2)}) collective-permute-start(f32[3,128,128]{2,1,0:T(8,128)S(1)} %get-tuple-element.29), channel_id=1, source_target_pairs={{0,2},{2,4},{4,6},{6,8},{8,10},{10,12},{12,14},{14,16},{16,18},{18... | collective-permute-start | bytes 589832 | tf_op jit(solution)/shard_map/ppermute | solution.py:683
  19.1 0.0 copy-done
  19.1 0.0 copy-done.13
  19.1 0.0 copy-done.3
  19.1 0.0 copy-done.6
  19.2 0.0 copy-done.8
  19.2 0.0 copy-done.9
  19.2 0.0 copy-done.10
  19.2 0.0 copy-done.11
  19.2 0.0 copy-done.12
  19.2 0.0 copy-start.2
  19.2 0.0 copy-start.4
  19.2 8.5 %local.1 = (f32[16,136,128]{2,1,0:T(8,128)S(1)}, f32[16,384,128]{2,1,0:T(8,128)S(1)}, f32[16,136,128]{2,1,0:T(8,128)S(1)}, f32[16,136,128]{2,1,0:T(8,128)S(1)}, ...) custom-call(f32[16,256,128]{2,1,0:T(8,128)S(1)} %get-tuple-element.31.key_t, ...), custom_call_target="tpu_custom_call" | custom-call | flops 4194304000 | bytes 31457280 | tf_op jit(solution)/shard_map/local/pallas_call | solution.py:795
  27.7 0.0 collective-permute-done.1.rims_ref
  27.7 0.0 collective-permute-done.2.halo_ref
  27.7 0.0 copy-done.2
  27.8 0.0 copy-done.4
  27.8 2.8 %join.2 = (f32[13,8,128]{2,1,0:T(8,128)S(1)}, f32[13,208,128]{2,1,0:T(8,128)S(1)}) custom-call(f32[13,128,128]{2,1,0:T(8,128)S(1)} %collective-permute-done.2.halo_ref, f32[16,16,128]{2,1,0:T(8,128)S(1)} %collective-permute-done.1.rims_ref, f32[16,384,128]{2,1,0:T(8,128)S(1)} %get-tuple-element.37.spectrum_ref, ...), custom_call_target="tpu_custom_call" | custom-call | flops 212992000 | bytes 8519680 | tf_op jit(solution)/shard_map/join/pallas_call | solution.py:839
  30.6 0.4 collective-permute-done.halo_ref
  30.9 0.0 copy-start.7
  30.9 1.6 %join.3 = (f32[16,8,128]{2,1,0:T(8,128)S(1)}, f32[16,208,128]{2,1,0:T(8,128)}) custom-call(f32[3,128,128]{2,1,0:T(8,128)S(1)} %collective-permute-done.halo_ref, f32[16,16,128]{2,1,0:T(8,128)S(1)} %collective-permute-done.1.rims_ref, f32[16,384,128]{2,1,0:T(8,128)S(1)} %get-tuple-element.37.spectrum_ref, f32[16,136,128]{2,1,0:T(8,128)S(1)} %get-tuple-element.38.medium_ref, ...), custom_call_target="tpu_custom_call" | custom-call | flops 49152000 | bytes 1966080 | tf_op jit(solution)/shard_map/join/pallas_call | solution.py:839
  32.5 17.1 %all_to_all.15.states.states_hbm = f32[8,2,8,128]{3,2,1,0:T(8,128)S(1)} all-to-all(f32[8,2,8,128]{3,2,1,0:T(8,128)S(1)} %bitcast.26), channel_id=1, replica_groups={{0,2,4,6,8,10,12,14},{16,18,20,22,24,26,28,30},{32,34,36,38,40,42,44,46..., dimensions={0} | all-to-all | bytes 131072 | tf_op jit(solution)/shard_map/all_to_all | solution.py:704
  49.6 0.0 copy-start.5
  49.6 13.4 %all_to_all.16.rings_ref = f32[16,2,8,128]{3,2,1,0:T(8,128)S(1)} all-to-all(f32[16,2,8,128]{3,2,1,0:T(8,128)S(1)} %ring.1), channel_id=1, replica_groups={{0,16,32,48,64,80,96,112,128,144,160,176,192,208,224,240},{2,18,34,50,6..., dimensions={0} | all-to-all | bytes 262144 | tf_op jit(solution)/shard_map/all_to_all | solution.py:704
  63.0 0.0 copy-done.5
  63.0 0.9 %scan.1 = f32[8,2,8,128]{3,2,1,0:T(8,128)S(1)} custom-call(s32[1]{0:T(128)} %bitcast.place_ref, f32[8,2,8,128]{3,2,1,0:T(8,128)} %copy-done.5, f32[16,2,8,128]{3,2,1,0:T(8,128)S(1)} %all_to_all.16.rings_ref, f32[2,8,128]{2,1,0:T(8,128)S(1)} %get-tuple-element.28._.rate_ref), custom_call_target="tpu_custom_call" | custom-call | flops 491520 | bytes 131072 | tf_op jit(solution)/shard_map/scan/pallas_call | solution.py:882
  63.9 9.6 %all_to_all.17 = f32[8,2,8,128]{3,2,1,0:T(8,128)S(1)} all-to-all(f32[8,2,8,128]{3,2,1,0:T(8,128)S(1)} %scan.1), channel_id=1, replica_groups={{0,2,4,6,8,10,12,14},{16,18,20,22,24,26,28,30},{32,34,36,38,40,42,44,46..., dimensions={0} | all-to-all | bytes 131072 | tf_op jit(solution)/shard_map/all_to_all | solution.py:704
  73.5 0.0 copy-done.7
  73.5 3.2 %finish.1 = (f32[16,256,128]{2,1,0:T(8,128)S(1)}, f32[1,256]{1,0:T(1,128)S(1)}) custom-call(f32[16,8,128]{2,1,0:T(8,128)S(1)} %bitcast.25, f32[16,376,128]{2,1,0:T(8,128)} %get-tuple-element.47.early_hbm, f32[16,208,128]{2,1,0:T(8,128)} %get-tuple-element.48.late_hbm, f32[16,16,128]{2,1,0:T(8,128)S(1)} %collective-permute-done.1.rims_ref, ...), custom_call_target="tpu_custom_call" | custom-call | flops 20971520 | bytes 8388608 | tf_op jit(solution)/shard_map/finish/pallas_call | solution.py:894
  76.7 7.6 %psum.7.squares_ref = f32[1,256]{1,0:T(1,128)S(1)} all-reduce(f32[1,256]{1,0:T(1,128)S(1)} %get-tuple-element.50), channel_id=1, replica_groups=mesh['seq'=128,'chan'=2] {'chan'}, use_global_device_ids=true, to_apply=%region_0.0 | all-reduce | flops 256 | bytes 2048 | tf_op jit(solution)/shard_map/psum | solution.py:910
  84.3 1.5 %scale.1 = f32[2048,256]{1,0:T(8,128)} custom-call(f32[16,256,128]{2,1,0:T(8,128)S(1)} %get-tuple-element.49.mixed_ref, f32[1,256]{1,0:T(1,128)S(1)} %psum.7.squares_ref), custom_call_target="tpu_custom_call" | custom-call | flops 524288 | bytes 4194304 | tf_op jit(solution)/shard_map/scale/pallas_call | solution.py:911
  (2 shorter events, 0.1 us)
Async XLA Ops:
  0.0 6.4 %copy-start.1 = (f32[3,2048,3]{1,2,0:T(4,128)S(1)}, f32[3,2048,3]{1,2,0:T(4,128)}, u32[]{:S(2)}) copy-start(f32[3,2048,3]{1,2,0:T(4,128)} %param.24) | copy-start | bytes 221188
  1.9 25.8 %collective-permute-start.2 = (f32[13,128,128]{2,1,0:T(8,128)S(1)}, f32[13,128,128]{2,1,0:T(8,128)S(1)}, u32[]{:S(2)}, u32[]{:S(2)}) collective-permute-start(f32[13,128,128]{2,1,0:T(8,128)S(1)} %get-tuple-element.43), channel_id=1, source_target_pairs={{0,2},{2,4},{4,6},{6,8},{8,10},{10,12},{12,14},{14,16},{16,18},{18... | collective-permute-start | bytes 2555912 | tf_op jit(solution)/shard_map/ppermute | solution.py:683
  6.4 12.7 %copy-start = (f32[2048,8]{0,1:T(8,128)S(1)}, f32[2048,8]{0,1:T(8,128)}, u32[]{:S(2)}) copy-start(f32[2048,8]{0,1:T(8,128)} %param.27) | copy-start | bytes 196612
  6.4 12.7 %copy-start.13 = (f32[2048,8]{0,1:T(8,128)S(1)}, f32[2048,8]{0,1:T(8,128)}, u32[]{:S(2)}) copy-start(f32[2048,8]{0,1:T(8,128)} %param.28) | copy-start | bytes 196612
  6.4 12.7 %copy-start.3 = (f32[3,2048,3]{1,2,0:T(4,128)S(1)}, f32[3,2048,3]{1,2,0:T(4,128)}, u32[]{:S(2)}) copy-start(f32[3,2048,3]{1,2,0:T(4,128)} %param.25) | copy-start | bytes 221188
  6.4 12.7 %copy-start.6 = (f32[2048]{0:T(1024)S(1)}, f32[2048]{0:T(1024)}, u32[]{:S(2)}) copy-start(f32[2048]{0:T(1024)} %param.29) | copy-start | bytes 24580
  6.4 12.7 %copy-start.8 = (bf16[256,768]{1,0:T(8,128)(2,1)S(1)}, bf16[256,768]{1,0:T(8,128)(2,1)}, u32[]{:S(2)}) copy-start(bf16[256,768]{1,0:T(8,128)(2,1)} %constant.26.clone.second_back_ref) | copy-start | bytes 1179652
  6.4 12.7 %copy-start.9 = (bf16[256,768]{1,0:T(8,128)(2,1)S(1)}, bf16[256,768]{1,0:T(8,128)(2,1)}, u32[]{:S(2)}) copy-start(bf16[256,768]{1,0:T(8,128)(2,1)} %constant.23.clone.second_window_ref) | copy-start | bytes 1179652
  6.4 12.7 %copy-start.10 = (bf16[384,384]{1,0:T(8,128)(2,1)S(1)}, bf16[384,384]{1,0:T(8,128)(2,1)}, u32[]{:S(2)}) copy-start(bf16[384,384]{1,0:T(8,128)(2,1)} %constant.24.clone.spectrum_ref) | copy-start | bytes 884740
  6.5 12.7 %copy-start.11 = (bf16[256,432]{1,0:T(8,128)(2,1)S(1)}, bf16[256,432]{1,0:T(8,128)(2,1)}, u32[]{:S(2)}) copy-start(bf16[256,432]{1,0:T(8,128)(2,1)} %constant.22.clone.first_ref) | copy-start | bytes 663556
  6.5 12.7 %copy-start.12 = (bf16[144,768]{1,0:T(8,128)(2,1)S(1)}, bf16[144,768]{1,0:T(8,128)(2,1)}, u32[]{:S(2)}) copy-start(bf16[144,768]{1,0:T(8,128)(2,1)} %constant.25.clone.first_back_ref) | copy-start | bytes 663556
  12.0 15.7 %collective-permute-start.1 = (f32[16,16,128]{2,1,0:T(8,128)S(1)}, f32[16,16,128]{2,1,0:T(8,128)S(1)}, u32[]{:S(2)}, u32[]{:S(2)}) collective-permute-start(f32[16,16,128]{2,1,0:T(8,128)S(1)} %get-tuple-element.30), channel_id=1, source_target_pairs={{0,2},{2,4},{4,6},{6,8},{8,10},{10,12},{12,14},{14,16},{16,18},{18... | collective-permute-start | bytes 393224 | tf_op jit(solution)/shard_map/ppermute | solution.py:683
  15.5 15.4 %collective-permute-start = (f32[3,128,128]{2,1,0:T(8,128)S(1)}, f32[3,128,128]{2,1,0:T(8,128)S(1)}, u32[]{:S(2)}, u32[]{:S(2)}) collective-permute-start(f32[3,128,128]{2,1,0:T(8,128)S(1)} %get-tuple-element.29), channel_id=1, source_target_pairs={{0,2},{2,4},{4,6},{6,8},{8,10},{10,12},{12,14},{14,16},{16,18},{18... | collective-permute-start | bytes 589832 | tf_op jit(solution)/shard_map/ppermute | solution.py:683
  19.2 8.5 %copy-start.2 = (bf16[144,768]{1,0:T(8,128)(2,1)S(1)}, bf16[144,768]{1,0:T(8,128)(2,1)}, u32[]{:S(2)}) copy-start(bf16[144,768]{1,0:T(8,128)(2,1)} %constant.28.clone.inverse_ref) | copy-start | bytes 663556
  19.2 8.5 %copy-start.4 = (bf16[256,384]{1,0:T(8,128)(2,1)S(1)}, bf16[256,384]{1,0:T(8,128)(2,1)}, u32[]{:S(2)}) copy-start(bf16[256,384]{1,0:T(8,128)(2,1)} %constant.27.clone.forward_ref) | copy-start | bytes 589828
  30.9 42.6 %copy-start.7 = (f32[2048]{0:T(1024)S(1)}, f32[2048]{0:T(1024)}, u32[]{:S(2)}) copy-start(f32[2048]{0:T(1024)} %param.30) | copy-start | bytes 24580
  49.6 13.4 %copy-start.5 = (f32[8,2,8,128]{3,2,1,0:T(8,128)}, f32[8,2,8,128]{3,2,1,0:T(8,128)S(1)}, u32[]{:S(2)}) copy-start(f32[8,2,8,128]{3,2,1,0:T(8,128)S(1)} %all_to_all.15.states.states_hbm) | copy-start | bytes 196612

commit v8 on v7

--- a/solution.py
+++ b/solution.py
@@ -21,7 +21,7 @@
 HEAD_ROWS = HEAD * SEG
 MAIN_ROWS = MAIN * SEG
 EARLY_ROWS = 144
-RIMS = 16
+RIMS = 13
 RING = 8
 LIMIT = 24 * 1024 * 1024
 
@@ -221,6 +221,7 @@
                 return taps[0] * here + taps[1] * down(here) + taps[2] * down(here, 2)
 
             tail_ref[tile] = feature(key_in, 1) * feature(value_in, 2)
+            tail_ref[tile, 0:2, :] = turned(key_in[lanes, :])[LANES - 2 :]
     for copy in rates:
         copy.wait()
     own_rate_out[...] = rates_in[...]
@@ -275,11 +276,13 @@
             copies[chunk * len(fields) + place].wait()
         for tile in range(chunk * rows // LANES, (chunk + 1) * rows // LANES):
             lanes = pl.ds(tile * LANES, LANES)
-            rims_out[tile] = jnp.zeros((RIMS, LANES), F32)
             for place, (_, source, target) in enumerate(fields):
                 if place < 5:
                     target[tile] = turned(source[lanes, :])
-                    rims_out[tile, 2 * place : 2 * place + 2, :] = target[tile, T - 2 : T, :]
+                    for k in range(2 if place else 0):
+                        rims_out[2 * place - 2 + k, tile : tile + 1, :] = target[
+                            tile, T - 2 + k : T - 1 + k, :
+                        ]
                 else:
                     target[tile, 0:TAPS, :] = turned(source[lanes, :])
                     target[tile, TAPS:HEAD_ROWS, :] = jnp.zeros((HEAD_ROWS - TAPS, LANES), F32)
@@ -298,10 +301,11 @@
                     taps = [short_ref[index, j : j + 1, lanes] for j in range(3)]
                     gated = gated * (taps[0] * here + taps[1] * down(here) + taps[2] * down(here, 2))
                 tail_out[late] = gated
+                tail_out[late, 0:2, :] = key_t[tile, T - 2 : T, :]
             for k in range(2):
-                rims_out[tile, 10 + k : 11 + k, :] = feature(query_t, 0, T - 2 + k)
+                rims_out[8 + k, tile : tile + 1, :] = feature(query_t, 0, T - 2 + k)
             for k in range(3):
-                rims_out[tile, 12 + k : 13 + k, :] = feature(key_t, 1, T // 2 - 1 + k) * feature(
+                rims_out[10 + k, tile : tile + 1, :] = feature(key_t, 1, T // 2 - 1 + k) * feature(
                     value_t, 2, T // 2 - 1 + k
                 )
 
@@ -479,7 +483,9 @@
         lanes = pl.ds(tile * LANES, LANES)
 
         def rim(k):
-            return rims_ref[tile, k : k + 1, :]
+            if k < 2:
+                return halo_ref[tile - base, k : k + 1, :]
+            return rims_ref[k - 2, tile : tile + 1, :]
 
         def taps_of(ref, index):
             return [ref[index, j : j + 1, lanes] for j in range(3)]
@@ -616,7 +622,7 @@
         rates = rate_ref[:, lanes]
         decays = jnp.exp(-rates)
         taps = [second_ref[0, j : j + 1, lanes] for j in range(3)]
-        older, last = rims_ref[tile, 6:7, :], rims_ref[tile, 7:8, :]
+        older, last = rims_ref[4, tile : tile + 1, :], rims_ref[5, tile : tile + 1, :]
         mends = [spread(taps[1] * last + taps[2] * older), spread(taps[2] * last)]
         gain = spread(gain_ref[:, lanes])
         states = state_ref[tile]
@@ -772,7 +778,7 @@
         [outside] * 6 + [held] * 2,
         [held] * 8,
         [struct(tiles, T, LANES)] * 5
-        + [struct(tiles, HEAD_ROWS, LANES), struct(tiles, RIMS, LANES)]
+        + [struct(tiles, HEAD_ROWS, LANES), struct(RIMS, tiles, LANES)]
         + [struct(parts[1], TAPS, LANES)],
         [pltpu.VMEM((channels, T), F32)] * 5
         + [pltpu.VMEM((channels, TAPS), F32), pltpu.SemaphoreType.DMA((6, chunks))],

time: 86.3 us -> 86 us (level)
  transfers between devices with their start and end apart: 3 -> 3, of which waited for: 1 -> 0; matrix products, arithmetic and copies ran while one was open for 0% -> 0% of each run, Pallas kernels for 20% -> 20%
where the time goes in v8:
time: 86 us; the launch traced here: 85.6 us
  blocking collectives  47.4 us (55%)
  Pallas kernels  26.1 us (30%)
  starting transfers between devices  11.5 us (13%)
    all_to_all x3, blocking collectives, exchange(): lax.all_to_all(rows, 'seq', split_axis=0, concat_axis=0, axis_index_group...  39.9 us
    ppermute x3, starting transfers between devices, from_behind(): return lax.ppermute(block, 'seq', [(i, i + 1) for i in range(count - 1)])  11.5 us
    pallas_call x1, Pallas kernels, local(): call(local_kernel, [held] * (11 + len(windows)), [held] * 6 + [outside],...  8.49 us
    psum x1, blocking collectives, local(): total = lax.psum(squares, 'chan')  7.58 us
    pallas_call x1, Pallas kernels, local(): call(prep_kernel, [outside] * 6 + [held] * 2, [held] * 8, [struct(tiles,...  5.5 us
    pallas_call x2, Pallas kernels, local(): call(functools.partial(join_kernel, base), [held] * (17 + len(joined)), [...  4.4 us
    pallas_call x1, Pallas kernels, local(): call(finish_kernel, [held] + [outside] * 2 + [held] * 4, [held] * 2, [str...  3.18 us
    pallas_call x1, Pallas kernels, local(): call(tail_kernel, [pl.BlockSpec(memory_space=pltpu.SMEM)] + [outside] * 4...  2.07 us
  transfers between devices with their start and end apart: 3, of which 0 were waited for; matrix products, arithmetic and copies ran while one was open for 0% of the time, Pallas kernels for 20%

profile of v8, /device:TPU:1, one launch (start us, length us, event | category | flops | bytes accessed | tf_op | source)
XLA Modules:
  0.0 85.6 jit_solution(13418434806557814390)
XLA Ops:
  0.0 0.0 copy-start.1
  0.0 2.1 %tail.1 = (f32[13,128,128]{2,1,0:T(8,128)S(1)}, f32[2,8,128]{2,1,0:T(8,128)S(1)}) custom-call(s32[1]{0:T(128)} %bitcast.place_ref, f32[2048,256]{1,0:T(8,128)} %key_hbm.3, f32[2048,256]{1,0:T(8,128)} %value_hbm.3, f32[3,3,2048]{2,1,0:T(4,128)} %bitcast.16, f32[8,2048]{1,0:T(8,128)} %bitcast.11), custom_call_target="tpu_custom_call" | custom-call | flops 4194304 | bytes 3145728 | tf_op jit(solution)/shard_map/tail/pallas_call | solution.py:761
  2.1 4.4 %collective-permute-start.2 = (f32[13,128,128]{2,1,0:T(8,128)S(1)}, f32[13,128,128]{2,1,0:T(8,128)S(1)}, u32[]{:S(2)}, u32[]{:S(2)}) collective-permute-start(f32[13,128,128]{2,1,0:T(8,128)S(1)} %get-tuple-element.43), channel_id=1, source_target_pairs={{0,2},{2,4},{4,6},{6,8},{8,10},{10,12},{12,14},{14,16},{16,18},{18... | collective-permute-start | bytes 2555912 | tf_op jit(solution)/shard_map/ppermute | solution.py:689
  6.5 0.0 copy-done.1
  6.5 0.0 copy-start
  6.5 0.0 copy-start.13
  6.5 0.0 copy-start.2
  6.6 0.0 copy-start.6
  6.6 0.0 copy-start.8
  6.6 0.0 copy-start.9
  6.6 0.0 copy-start.10
  6.6 0.0 copy-start.11
  6.6 0.0 copy-start.12
  6.6 5.5 %prep.1 = (f32[16,256,128]{2,1,0:T(8,128)S(1)}, f32[16,256,128]{2,1,0:T(8,128)S(1)}, f32[16,256,128]{2,1,0:T(8,128)S(1)}, f32[16,256,128]{2,1,0:T(8,128)S(1)}, f...) custom-call(f32[2048,256]{1,0:T(8,128)} %key_hbm.3, ...), custom_call_target="tpu_custom_call" | custom-call | flops 10485760 | bytes 20971520 | tf_op jit(solution)/shard_map/prep/pallas_call | solution.py:776
  12.1 3.5 %collective-permute-start.1 = (f32[13,16,128]{2,1,0:T(8,128)S(1)}, f32[13,16,128]{2,1,0:T(8,128)S(1)}, u32[]{:S(2)}, u32[]{:S(2)}) collective-permute-start(f32[13,16,128]{2,1,0:T(8,128)S(1)} %get-tuple-element.30), channel_id=1, source_target_pairs={{0,2},{2,4},{4,6},{6,8},{8,10},{10,12},{12,14},{14,16},{16,18},{18... | collective-permute-start | bytes 319496 | tf_op jit(solution)/shard_map/ppermute | solution.py:689
  15.6 3.6 %collective-permute-start = (f32[3,128,128]{2,1,0:T(8,128)S(1)}, f32[3,128,128]{2,1,0:T(8,128)S(1)}, u32[]{:S(2)}, u32[]{:S(2)}) collective-permute-start(f32[3,128,128]{2,1,0:T(8,128)S(1)} %get-tuple-element.29), channel_id=1, source_target_pairs={{0,2},{2,4},{4,6},{6,8},{8,10},{10,12},{12,14},{14,16},{16,18},{18... | collective-permute-start | bytes 589832 | tf_op jit(solution)/shard_map/ppermute | solution.py:689
  19.2 0.0 copy-done
  19.2 0.0 copy-done.13
  19.3 0.0 copy-done.2
  19.3 0.0 copy-done.6
  19.3 0.0 copy-done.8
  19.3 0.0 copy-done.9
  19.3 0.0 copy-done.10
  19.3 0.0 copy-done.11
  19.3 0.0 copy-done.12
  19.4 0.0 copy-start.3
  19.4 0.0 copy-start.4
  19.4 8.5 %local.1 = (f32[16,136,128]{2,1,0:T(8,128)S(1)}, f32[16,384,128]{2,1,0:T(8,128)S(1)}, f32[16,136,128]{2,1,0:T(8,128)S(1)}, f32[16,136,128]{2,1,0:T(8,128)S(1)}, ...) custom-call(f32[16,256,128]{2,1,0:T(8,128)S(1)} %get-tuple-element.31.key_t, ...), custom_call_target="tpu_custom_call" | custom-call | flops 4194304000 | bytes 31457280 | tf_op jit(solution)/shard_map/local/pallas_call | solution.py:801
  27.9 0.0 collective-permute-done.1.rims_ref
  27.9 0.0 collective-permute-done.2.halo_ref
  27.9 0.0 copy-done.3
  27.9 0.0 copy-done.4
  27.9 2.8 %join.2 = (f32[13,8,128]{2,1,0:T(8,128)S(1)}, f32[13,208,128]{2,1,0:T(8,128)S(1)}) custom-call(f32[13,128,128]{2,1,0:T(8,128)S(1)} %collective-permute-done.2.halo_ref, f32[13,16,128]{2,1,0:T(8,128)S(1)} %collective-permute-done.1.rims_ref, f32[16,384,128]{2,1,0:T(8,128)S(1)} %get-tuple-element.37.spectrum_ref, ...), custom_call_target="tpu_custom_call" | custom-call | flops 212992000 | bytes 8519680 | tf_op jit(solution)/shard_map/join/pallas_call | solution.py:845
  30.7 0.0 collective-permute-done.halo_ref
  30.7 0.0 copy-start.7
  30.8 1.6 %join.3 = (f32[16,8,128]{2,1,0:T(8,128)S(1)}, f32[16,208,128]{2,1,0:T(8,128)}) custom-call(f32[3,128,128]{2,1,0:T(8,128)S(1)} %collective-permute-done.halo_ref, f32[13,16,128]{2,1,0:T(8,128)S(1)} %collective-permute-done.1.rims_ref, f32[16,384,128]{2,1,0:T(8,128)S(1)} %get-tuple-element.37.spectrum_ref, f32[16,136,128]{2,1,0:T(8,128)S(1)} %get-tuple-element.38.medium_ref, ...), custom_call_target="tpu_custom_call" | custom-call | flops 49152000 | bytes 1966080 | tf_op jit(solution)/shard_map/join/pallas_call | solution.py:845
  32.4 16.9 %all_to_all.15.states.states_hbm = f32[8,2,8,128]{3,2,1,0:T(8,128)S(1)} all-to-all(f32[8,2,8,128]{3,2,1,0:T(8,128)S(1)} %bitcast.26), channel_id=1, replica_groups={{0,2,4,6,8,10,12,14},{16,18,20,22,24,26,28,30},{32,34,36,38,40,42,44,46..., dimensions={0} | all-to-all | bytes 131072 | tf_op jit(solution)/shard_map/all_to_all | solution.py:710
  49.2 0.0 copy-start.5
  49.3 13.4 %all_to_all.16.rings_ref = f32[16,2,8,128]{3,2,1,0:T(8,128)S(1)} all-to-all(f32[16,2,8,128]{3,2,1,0:T(8,128)S(1)} %ring.1), channel_id=1, replica_groups={{0,16,32,48,64,80,96,112,128,144,160,176,192,208,224,240},{2,18,34,50,6..., dimensions={0} | all-to-all | bytes 262144 | tf_op jit(solution)/shard_map/all_to_all | solution.py:710
  62.7 0.0 copy-done.5
  62.7 0.9 %scan.1 = f32[8,2,8,128]{3,2,1,0:T(8,128)S(1)} custom-call(s32[1]{0:T(128)} %bitcast.place_ref, f32[8,2,8,128]{3,2,1,0:T(8,128)} %copy-done.5, f32[16,2,8,128]{3,2,1,0:T(8,128)S(1)} %all_to_all.16.rings_ref, f32[2,8,128]{2,1,0:T(8,128)S(1)} %get-tuple-element.28._.rate_ref), custom_call_target="tpu_custom_call" | custom-call | flops 491520 | bytes 131072 | tf_op jit(solution)/shard_map/scan/pallas_call | solution.py:888
  63.5 9.6 %all_to_all.17 = f32[8,2,8,128]{3,2,1,0:T(8,128)S(1)} all-to-all(f32[8,2,8,128]{3,2,1,0:T(8,128)S(1)} %scan.1), channel_id=1, replica_groups={{0,2,4,6,8,10,12,14},{16,18,20,22,24,26,28,30},{32,34,36,38,40,42,44,46..., dimensions={0} | all-to-all | bytes 131072 | tf_op jit(solution)/shard_map/all_to_all | solution.py:710
  73.1 0.0 copy-done.7
  73.1 3.2 %finish.1 = (f32[16,256,128]{2,1,0:T(8,128)S(1)}, f32[1,256]{1,0:T(1,128)S(1)}) custom-call(f32[16,8,128]{2,1,0:T(8,128)S(1)} %bitcast.25, f32[16,376,128]{2,1,0:T(8,128)} %get-tuple-element.47.early_hbm, f32[16,208,128]{2,1,0:T(8,128)} %get-tuple-element.48.late_hbm, f32[13,16,128]{2,1,0:T(8,128)S(1)} %collective-permute-done.1.rims_ref, ...), custom_call_target="tpu_custom_call" | custom-call | flops 20971520 | bytes 8388608 | tf_op jit(solution)/shard_map/finish/pallas_call | solution.py:900
  76.3 7.6 %psum.7.squares_ref = f32[1,256]{1,0:T(1,128)S(1)} all-reduce(f32[1,256]{1,0:T(1,128)S(1)} %get-tuple-element.50), channel_id=1, replica_groups=mesh['seq'=128,'chan'=2] {'chan'}, use_global_device_ids=true, to_apply=%region_0.0 | all-reduce | flops 256 | bytes 2048 | tf_op jit(solution)/shard_map/psum | solution.py:916
  83.9 1.5 %scale.1 = f32[2048,256]{1,0:T(8,128)} custom-call(f32[16,256,128]{2,1,0:T(8,128)S(1)} %get-tuple-element.49.mixed_ref, f32[1,256]{1,0:T(1,128)S(1)} %psum.7.squares_ref), custom_call_target="tpu_custom_call" | custom-call | flops 524288 | bytes 4194304 | tf_op jit(solution)/shard_map/scale/pallas_call | solution.py:917
  (2 shorter events, 0.1 us)
Async XLA Ops:
  0.0 6.5 %copy-start.1 = (f32[3,2048,3]{1,2,0:T(4,128)S(1)}, f32[3,2048,3]{1,2,0:T(4,128)}, u32[]{:S(2)}) copy-start(f32[3,2048,3]{1,2,0:T(4,128)} %param.24) | copy-start | bytes 221188
  2.1 25.8 %collective-permute-start.2 = (f32[13,128,128]{2,1,0:T(8,128)S(1)}, f32[13,128,128]{2,1,0:T(8,128)S(1)}, u32[]{:S(2)}, u32[]{:S(2)}) collective-permute-start(f32[13,128,128]{2,1,0:T(8,128)S(1)} %get-tuple-element.43), channel_id=1, source_target_pairs={{0,2},{2,4},{4,6},{6,8},{8,10},{10,12},{12,14},{14,16},{16,18},{18... | collective-permute-start | bytes 2555912 | tf_op jit(solution)/shard_map/ppermute | solution.py:689
  6.5 12.7 %copy-start = (f32[2048,8]{0,1:T(8,128)S(1)}, f32[2048,8]{0,1:T(8,128)}, u32[]{:S(2)}) copy-start(f32[2048,8]{0,1:T(8,128)} %param.27) | copy-start | bytes 196612
  6.5 12.7 %copy-start.13 = (f32[2048,8]{0,1:T(8,128)S(1)}, f32[2048,8]{0,1:T(8,128)}, u32[]{:S(2)}) copy-start(f32[2048,8]{0,1:T(8,128)} %param.28) | copy-start | bytes 196612
  6.5 12.7 %copy-start.2 = (f32[3,2048,3]{1,2,0:T(4,128)S(1)}, f32[3,2048,3]{1,2,0:T(4,128)}, u32[]{:S(2)}) copy-start(f32[3,2048,3]{1,2,0:T(4,128)} %param.25) | copy-start | bytes 221188
  6.6 12.7 %copy-start.6 = (f32[2048]{0:T(1024)S(1)}, f32[2048]{0:T(1024)}, u32[]{:S(2)}) copy-start(f32[2048]{0:T(1024)} %param.29) | copy-start | bytes 24580
  6.6 12.7 %copy-start.8 = (bf16[256,768]{1,0:T(8,128)(2,1)S(1)}, bf16[256,768]{1,0:T(8,128)(2,1)}, u32[]{:S(2)}) copy-start(bf16[256,768]{1,0:T(8,128)(2,1)} %constant.26.clone.second_back_ref) | copy-start | bytes 1179652
  6.6 12.7 %copy-start.9 = (bf16[256,768]{1,0:T(8,128)(2,1)S(1)}, bf16[256,768]{1,0:T(8,128)(2,1)}, u32[]{:S(2)}) copy-start(bf16[256,768]{1,0:T(8,128)(2,1)} %constant.23.clone.second_window_ref) | copy-start | bytes 1179652
  6.6 12.7 %copy-start.10 = (bf16[384,384]{1,0:T(8,128)(2,1)S(1)}, bf16[384,384]{1,0:T(8,128)(2,1)}, u32[]{:S(2)}) copy-start(bf16[384,384]{1,0:T(8,128)(2,1)} %constant.24.clone.spectrum_ref) | copy-start | bytes 884740
  6.6 12.7 %copy-start.11 = (bf16[256,432]{1,0:T(8,128)(2,1)S(1)}, bf16[256,432]{1,0:T(8,128)(2,1)}, u32[]{:S(2)}) copy-start(bf16[256,432]{1,0:T(8,128)(2,1)} %constant.22.clone.first_ref) | copy-start | bytes 663556
  6.6 12.7 %copy-start.12 = (bf16[144,768]{1,0:T(8,128)(2,1)S(1)}, bf16[144,768]{1,0:T(8,128)(2,1)}, u32[]{:S(2)}) copy-start(bf16[144,768]{1,0:T(8,128)(2,1)} %constant.25.clone.first_back_ref) | copy-start | bytes 663556
  12.1 15.7 %collective-permute-start.1 = (f32[13,16,128]{2,1,0:T(8,128)S(1)}, f32[13,16,128]{2,1,0:T(8,128)S(1)}, u32[]{:S(2)}, u32[]{:S(2)}) collective-permute-start(f32[13,16,128]{2,1,0:T(8,128)S(1)} %get-tuple-element.30), channel_id=1, source_target_pairs={{0,2},{2,4},{4,6},{6,8},{8,10},{10,12},{12,14},{14,16},{16,18},{18... | collective-permute-start | bytes 319496 | tf_op jit(solution)/shard_map/ppermute | solution.py:689
  15.6 15.1 %collective-permute-start = (f32[3,128,128]{2,1,0:T(8,128)S(1)}, f32[3,128,128]{2,1,0:T(8,128)S(1)}, u32[]{:S(2)}, u32[]{:S(2)}) collective-permute-start(f32[3,128,128]{2,1,0:T(8,128)S(1)} %get-tuple-element.29), channel_id=1, source_target_pairs={{0,2},{2,4},{4,6},{6,8},{8,10},{10,12},{12,14},{14,16},{16,18},{18... | collective-permute-start | bytes 589832 | tf_op jit(solution)/shard_map/ppermute | solution.py:689
  19.4 8.5 %copy-start.3 = (bf16[144,768]{1,0:T(8,128)(2,1)S(1)}, bf16[144,768]{1,0:T(8,128)(2,1)}, u32[]{:S(2)}) copy-start(bf16[144,768]{1,0:T(8,128)(2,1)} %constant.28.clone.inverse_ref) | copy-start | bytes 663556
  19.4 8.5 %copy-start.4 = (bf16[256,384]{1,0:T(8,128)(2,1)S(1)}, bf16[256,384]{1,0:T(8,128)(2,1)}, u32[]{:S(2)}) copy-start(bf16[256,384]{1,0:T(8,128)(2,1)} %constant.27.clone.forward_ref) | copy-start | bytes 589828
  30.7 42.4 %copy-start.7 = (f32[2048]{0:T(1024)S(1)}, f32[2048]{0:T(1024)}, u32[]{:S(2)}) copy-start(f32[2048]{0:T(1024)} %param.30) | copy-start | bytes 24580
  49.2 13.4 %copy-start.5 = (f32[8,2,8,128]{3,2,1,0:T(8,128)}, f32[8,2,8,128]{3,2,1,0:T(8,128)S(1)}, u32[]{:S(2)}) copy-start(f32[8,2,8,128]{3,2,1,0:T(8,128)S(1)} %all_to_all.15.states.states_hbm) | copy-start | bytes 196612
